TPU v7x, 32 devices: a whole 2x2x4 slice. The times are simulated.
32 devices in a mesh: seq: 16 (over z, x, core), head: 2 (over y).
Axes of the slice: x: 2, y: 2, z: 4, core: 2. Of those that a mesh axis runs over, the one named last changes fastest.
Arguments:
- queries: bfloat16 [4096, 1792], P('seq', 'head'), may hold values from -120 to 120
- key_rows: bfloat16 [4096, 256], P('seq', 'head'), may hold values from -9 to 9
- value_rows: bfloat16 [4096, 256], P('seq', 'head'), may hold values from -6 to 6
- out_weight: bfloat16 [1792, 3584], P('head', 'seq'), may hold values from -0.125 to 0.125
Outputs:
- projected: bfloat16 [4096, 3584], P('seq', 'head')
All inputs are finite; a program needn't handle non-finite values.
Results may differ from a plain program's by a relative error of at most 0.009.
Values may be sent and summed in bfloat16 or wider, within the bound.
No kernel may reach another device: no remote copies, remote signals or barrier semaphores. Data moves between devices by JAX's collectives and lax.ppermute only.
A program may use at most 64 MiB of HBM per device.

v0:
```python
import functools
import math

import jax
import jax.numpy as jnp
from jax import lax
from jax.sharding import PartitionSpec as P

QPK = 7
HD = 128
BLK = 256


masked_score = -1e30


def padded_2(shard, sides, width):
    for axis, dim in sides:
        devices, length = (lax.axis_size(axis), shard.shape[dim])
        up = [(i, (i + 1) % devices) for i in range(devices - 1)]
        down = [(j, i) for i, j in up]
        last = lax.slice_in_dim(shard, length - width, length, axis=dim)
        first = lax.slice_in_dim(shard, 0, width, axis=dim)
        before = lax.ppermute(last, axis, up)
        after = lax.ppermute(first, axis, down)
        shard = jnp.concatenate([before, shard, after], axis=dim)
    return shard


def partner_2(value, axis, apart):
    mask = 2**apart
    pairs = [(source, source ^ mask) for source in range(lax.axis_size(axis))]
    return lax.ppermute(value, axis, pairs)


def head_partial(key_block, value_block, usable, query_head):
    scores = lax.dot_general(
        query_head, key_block, (((1,), (1,)), ((), ())), preferred_element_type=jnp.float32
    )
    scores = scores * (1.0 / math.sqrt(HD))
    scores = jnp.where(usable[None, :], scores, masked_score)
    peak = jnp.max(scores, axis=1)
    weights = jnp.exp(scores - peak[:, None])
    weight_sum = jnp.sum(weights, axis=1)
    numerator = jnp.dot(
        weights.astype(jnp.bfloat16), value_block, preferred_element_type=jnp.float32
    )
    return (peak, weight_sum, numerator)


def attend(query_block, key_value, usable):
    return lax.map(functools.partial(head_partial, key_value[0], key_value[1], usable), query_block)


def finish(partial_value):
    blended = partial_value[2] / partial_value[1][..., None]
    return jnp.transpose(blended, (1, 0, 2)).reshape(blended.shape[1], -1).astype(jnp.bfloat16)


def block_slice(array, block_slot):
    return array[:, block_slot * BLK : (block_slot + 1) * BLK]


def local(queries, key_rows, value_rows, out_weight):
    token_count = key_rows.shape[0]
    per_dev = token_count // BLK
    seq_count = lax.axis_size("seq")
    device_rank = lax.axis_index("seq")
    remote_bits = seq_count.bit_length() - 1
    query_heads = jnp.transpose(queries.reshape(token_count, QPK, HD), (1, 0, 2))
    key_value = jnp.stack([key_rows, value_rows])
    padded = padded_2(key_value, (("seq", 1),), BLK)
    all_true = jnp.ones((BLK,), dtype=bool)
    lower_usable = jnp.broadcast_to(device_rank > 0, (BLK,))
    upper_usable = jnp.broadcast_to(device_rank < seq_count - 1, (BLK,))
    ordering = [bit_number for bit_number in range(remote_bits) if per_dev << bit_number >= 2]
    partners = [partner_2(key_value, "seq", bit_number) for bit_number in ordering]
    pieces = [block_slice(padded, 0), block_slice(padded, 1), block_slice(padded, 2)]
    validity = [lower_usable, all_true, upper_usable]
    pieces, validity = (pieces, validity)
    pieces = pieces + [block_slice(partner, 0) for partner in partners]
    validity = validity + [all_true for partner in partners]
    partial_value = attend(
        block_slice(query_heads, 0), jnp.concatenate(pieces, 1), jnp.concatenate(validity)
    )
    results = finish(partial_value)
    column_terms = jnp.dot(
        results,
        lax.all_gather(out_weight, "seq", axis=1, tiled=True),
        preferred_element_type=jnp.float32,
    )
    return lax.psum_scatter(
        column_terms.astype(jnp.bfloat16), "head", scatter_dimension=1, tiled=True
    )


def solution(mesh):
    in_specs = (P("seq", "head"), P("seq", "head"), P("seq", "head"), P("head", "seq"))
    out_specs = P("seq", "head")
    return jax.shard_map(local, mesh=mesh, in_specs=in_specs, out_specs=out_specs, check_vma=False)
```

profile of v0, /device:TPU:0, one launch (start us, length us, event | category | flops | bytes accessed | tf_op | source)
XLA Modules:
  0.0 118.7 jit_solution(7272156074299152580)
XLA Ops:
  6.5 0.7 all-gather.2.cloned.1.call-update
  7.3 0.9 pad_maximum_fusion
  8.2 2.4 %collective-permute-start = (bf16[2,256,128]{2,1,0:T(8,128)(2,1)S(1)}, bf16[2,256,128]{2,1,0:T(8,128)(2,1)S(1)}, u32[]{:S(2)}, u32[]{:S(2)}) collective-permute-start(bf16[2,256,128]{2,1,0:T(8,128)(2,1)S(1)} %pad_maximum_fusion), channel_id=1, source_target_pairs={{0,2},{2,4},{4,6},{6,8},{8,10},{10,12},{12,14},{14,16},{16,18},{18... | collective-permute-start | bytes 393224 | tf_op jit(solution)/shard_map/ppermute | solution.py:24
  10.6 1.3 %collective-permute-start.1 = (bf16[2,256,128]{2,1,0:T(8,128)(2,1)S(1)}, bf16[2,256,128]{2,1,0:T(8,128)(2,1)S(1)}, u32[]{:S(2)}, u32[]{:S(2)}) collective-permute-start(bf16[2,256,128]{2,1,0:T(8,128)(2,1)S(1)} %pad_maximum_fusion), channel_id=1, source_target_pairs={{2,0},{4,2},{6,4},{8,6},{10,8},{12,10},{14,12},{16,14},{18,16},{20... | collective-permute-start | bytes 393224 | tf_op jit(solution)/shard_map/ppermute | solution.py:25
  11.9 4.9 %collective-permute-start.2 = (bf16[2,256,128]{2,1,0:T(8,128)(2,1)S(1)}, bf16[2,256,128]{2,1,0:T(8,128)(2,1)S(1)}, u32[]{:S(2)}, u32[]{:S(2)}) collective-permute-start(bf16[2,256,128]{2,1,0:T(8,128)(2,1)S(1)} %pad_maximum_fusion), channel_id=1, source_target_pairs={{0,4},{2,6},{4,0},{6,2},{8,12},{10,14},{12,8},{14,10},{16,20},{18,... | collective-permute-start | bytes 393224 | tf_op jit(solution)/shard_map/ppermute | solution.py:33
  16.8 1.6 %collective-permute-start.3 = (bf16[2,256,128]{2,1,0:T(8,128)(2,1)S(1)}, bf16[2,256,128]{2,1,0:T(8,128)(2,1)S(1)}, u32[]{:S(2)}, u32[]{:S(2)}) collective-permute-start(bf16[2,256,128]{2,1,0:T(8,128)(2,1)S(1)} %pad_maximum_fusion), channel_id=1, source_target_pairs={{0,8},{2,10},{4,12},{6,14},{8,0},{10,2},{12,4},{14,6},{16,24},{18,... | collective-permute-start | bytes 393224 | tf_op jit(solution)/shard_map/ppermute | solution.py:33
  18.4 2.6 %collective-permute-start.4 = (bf16[2,256,128]{2,1,0:T(8,128)(2,1)S(1)}, bf16[2,256,128]{2,1,0:T(8,128)(2,1)S(1)}, u32[]{:S(2)}, u32[]{:S(2)}) collective-permute-start(bf16[2,256,128]{2,1,0:T(8,128)(2,1)S(1)} %pad_maximum_fusion), channel_id=1, source_target_pairs={{0,16},{2,18},{4,20},{6,22},{8,24},{10,26},{12,28},{14,30},{16,0},... | collective-permute-start | bytes 393224 | tf_op jit(solution)/shard_map/ppermute | solution.py:33
  20.9 1.2 %copy.5 = bf16[256,896]{0,1:T(8,128)(2,1)S(1)} copy(bf16[256,896]{1,0:T(8,128)(2,1)} %param.6) | data formatting | bytes 917504 | tf_op args[0]
  22.4 9.1 %collective-permute-done.3 = bf16[2,256,128]{2,1,0:T(8,128)(2,1)S(1)} collective-permute-done((bf16[2,256,128]{2,1,0:T(8,128)(2,1)S(1)}, bf16[2,256,128]{2,1,0:T(8,128)(2,1)S(1)}, u32[]{:S(2)}, u32[]{:S(2)}) %collective-permute-start.3) | collective-permute-done | bytes 131104 | tf_op jit(solution)/shard_map/ppermute | solution.py:33
  31.6 9.9 %while.12 = (s32[]{:T(128)}, f32[7,256]{1,0:T(8,128)S(1)}, f32[7,256,128]{1,2,0:T(8,128)S(1)}, pred[1536]{0:T(1024)(128)(4,1)S(1)}, bf16[7,256,128]{1,2,0:T(8,12...) while((s32[]{:T(128)}, f32[7,256]{1,0:T(8,128)S(1)}, ...), condition=%wide.region_3.4_spmd, body=%wide.region_0.3_spmd.sunk | while | flops 204078592 | bytes 5709929 | solution.py:52
  31.6 0.5 fusion.23
  32.1 0.5 fusion.25
  32.6 0.4 fusion.24
  33.0 0.5 fusion.23
  33.5 0.5 fusion.25
  34.0 0.4 fusion.24
  34.4 0.5 fusion.23
  34.9 0.5 fusion.25
  35.4 0.4 fusion.24
  35.8 0.5 fusion.23
  36.3 0.5 fusion.25
  37.2 0.5 fusion.23
  37.7 0.5 fusion.25
  38.7 0.5 fusion.23
  39.2 0.5 fusion.25
  39.7 0.4 fusion.24
  40.1 0.5 fusion.23
  40.6 0.5 fusion.25
  41.1 0.4 fusion.24
  41.6 36.3 %all-gather.2.cloned.1.call-done = bf16[896,3584]{0,1:T(8,128)(2,1)} async-done(((bf16[896,224]{0,1:T(8,128)(2,1)}), bf16[896,3584]{0,1:T(8,128)(2,1)}) %all-gather.2.cloned.1.call-update) | async-done | bytes 6422544 | tf_op jit(solution)/shard_map/all_gather | solution.py:89
  77.9 6.3 %convolution_convert_fusion = bf16[256,3584]{1,0:T(8,128)(2,1)} fusion(bf16[256,896]{0,1:T(8,128)(2,1)S(1)} %bitcast.39, bf16[896,3584]{0,1:T(8,128)(2,1)} %all-gather.2.cloned.1.call-done), kind=kOutput, calls=%fused_computation.11 | convolution fusion | flops 1645084672 | bytes 8716288 | tf_op jit(solution)/shard_map/dot_general | solution.py:87
  84.1 27.7 %reduce-scatter.2.cloned.1.call-done = bf16[256,1792]{1,0:T(8,128)(2,1)} async-done(((bf16[256,3584]{1,0:T(8,128)(2,1)}), bf16[256,1792]{1,0:T(8,128)(2,1)}) %reduce-scatter.2.cloned.1.call-update) | async-done | bytes 917520 | tf_op jit(solution)/shard_map/reduce_scatter | solution.py:92
  (35 shorter events, 1.4 us)
Async XLA Ops:
  6.5 15.7 %copy-start.1 = (bf16[256,128]{1,0:T(8,128)(2,1)S(1)}, bf16[256,128]{1,0:T(8,128)(2,1)}, u32[]{:S(2)}) copy-start(bf16[256,128]{1,0:T(8,128)(2,1)} %param.7) | copy-start | bytes 196612
  6.5 15.8 %copy-start = (bf16[256,128]{1,0:T(8,128)(2,1)S(1)}, bf16[256,128]{1,0:T(8,128)(2,1)}, u32[]{:S(2)}) copy-start(bf16[256,128]{1,0:T(8,128)(2,1)} %param.8) | copy-start | bytes 196612
  6.5 71.3 %all-gather.2.cloned.1.call-start = ((), (), s32[]{:S(2)}) async-start(), calls=%async_computation.1 | async-start | bytes 6823936 | tf_op jit(solution)/shard_map/all_gather | solution.py:89
  7.3 104.6 %reduce-scatter.2.cloned.1.call-start = ((), (), s32[]{:S(2)}) async-start(), calls=%async_computation.2 | async-start | bytes 2752512 | tf_op jit(solution)/shard_map/reduce_scatter | solution.py:92
  8.2 14.1 %collective-permute-start = (bf16[2,256,128]{2,1,0:T(8,128)(2,1)S(1)}, bf16[2,256,128]{2,1,0:T(8,128)(2,1)S(1)}, u32[]{:S(2)}, u32[]{:S(2)}) collective-permute-start(bf16[2,256,128]{2,1,0:T(8,128)(2,1)S(1)} %pad_maximum_fusion), channel_id=1, source_target_pairs={{0,2},{2,4},{4,6},{6,8},{8,10},{10,12},{12,14},{14,16},{16,18},{18... | collective-permute-start | bytes 393224 | tf_op jit(solution)/shard_map/ppermute | solution.py:24
  10.6 11.8 %collective-permute-start.1 = (bf16[2,256,128]{2,1,0:T(8,128)(2,1)S(1)}, bf16[2,256,128]{2,1,0:T(8,128)(2,1)S(1)}, u32[]{:S(2)}, u32[]{:S(2)}) collective-permute-start(bf16[2,256,128]{2,1,0:T(8,128)(2,1)S(1)} %pad_maximum_fusion), channel_id=1, source_target_pairs={{2,0},{4,2},{6,4},{8,6},{10,8},{12,10},{14,12},{16,14},{18,16},{20... | collective-permute-start | bytes 393224 | tf_op jit(solution)/shard_map/ppermute | solution.py:25
  11.9 10.5 %collective-permute-start.2 = (bf16[2,256,128]{2,1,0:T(8,128)(2,1)S(1)}, bf16[2,256,128]{2,1,0:T(8,128)(2,1)S(1)}, u32[]{:S(2)}, u32[]{:S(2)}) collective-permute-start(bf16[2,256,128]{2,1,0:T(8,128)(2,1)S(1)} %pad_maximum_fusion), channel_id=1, source_target_pairs={{0,4},{2,6},{4,0},{6,2},{8,12},{10,14},{12,8},{14,10},{16,20},{18,... | collective-permute-start | bytes 393224 | tf_op jit(solution)/shard_map/ppermute | solution.py:33
  16.8 14.7 %collective-permute-start.3 = (bf16[2,256,128]{2,1,0:T(8,128)(2,1)S(1)}, bf16[2,256,128]{2,1,0:T(8,128)(2,1)S(1)}, u32[]{:S(2)}, u32[]{:S(2)}) collective-permute-start(bf16[2,256,128]{2,1,0:T(8,128)(2,1)S(1)} %pad_maximum_fusion), channel_id=1, source_target_pairs={{0,8},{2,10},{4,12},{6,14},{8,0},{10,2},{12,4},{14,6},{16,24},{18,... | collective-permute-start | bytes 393224 | tf_op jit(solution)/shard_map/ppermute | solution.py:33
  18.4 13.1 %collective-permute-start.4 = (bf16[2,256,128]{2,1,0:T(8,128)(2,1)S(1)}, bf16[2,256,128]{2,1,0:T(8,128)(2,1)S(1)}, u32[]{:S(2)}, u32[]{:S(2)}) collective-permute-start(bf16[2,256,128]{2,1,0:T(8,128)(2,1)S(1)} %pad_maximum_fusion), channel_id=1, source_target_pairs={{0,16},{2,18},{4,20},{6,22},{8,24},{10,26},{12,28},{14,30},{16,0},... | collective-permute-start | bytes 393224 | tf_op jit(solution)/shard_map/ppermute | solution.py:33
Sparse Core Ops, SparseCore 0:
  9.6 68.1 all-gather.1
  84.3 27.5 reduce-scatter.1
where the time goes:
time: 119 us
  waiting for transfers between devices  73.8 us (62%)
  between operations  13.6 us (11%)
  matrix products  13.2 us (11%)
  starting transfers between devices  12.8 us (11%)
  other arithmetic  3.53 us (3%)
  local copies, waits for them, and re-layouts  1.7 us (1%)
    all_gather x1, waiting for transfers between devices, local(): lax.all_gather(out_weight, 'seq', axis=1, tiled=True)  36.3 us
    reduce_scatter x1, waiting for transfers between devices, local(): lax.psum_scatter(column_terms.astype(jnp.bfloat16), 'head', scatter_dimen...  27.7 us
    ppermute x3, starting transfers between devices, partner_2(): return lax.ppermute(value, axis, pairs)  9.08 us
    ppermute x3, waiting for transfers between devices, partner_2(): return lax.ppermute(value, axis, pairs)  9.06 us
    dot_general x1, matrix products, local(): jnp.dot(results, lax.all_gather(out_weight, 'seq', axis=1, tiled=True), p...  6.25 us
    dot_general x7, matrix products, head_partial(): jnp.dot(weights.astype(jnp.bfloat16), value_block, preferred_element_type...  3.48 us
    dot_general x7, matrix products, head_partial(): lax.dot_general(query_head, key_block, (((1,), (1,)), ((), ())), preferre...  3.42 us
    reduce_sum x7, other arithmetic, head_partial(): weight_sum = jnp.sum(weights, axis=1)  2.53 us
  transfers between devices with their start and end apart: 7, of which 3 were waited for; matrix products, arithmetic and copies ran while one was open for 10% of the time, Pallas kernels for 0%

commit v1 on v0

v1 whole, which is shorter than its diff:
```python
import functools
import math

import jax
import jax.numpy as jnp
from jax import lax
from jax.experimental import pallas as pl
from jax.experimental.pallas import tpu as pltpu
from jax.sharding import PartitionSpec as P

HD = 128
BLK = 256

masked_score = -1e30
vmem_limit = 20 * 2**20
in_vmem = pl.BlockSpec(memory_space=pltpu.VMEM)


def call_kernel(body, out_shape, operands, scratch=(), flops=0, moved=0, transcendentals=0):
    many = isinstance(out_shape, (list, tuple))
    return pl.pallas_call(
        body,
        out_shape=out_shape,
        in_specs=[in_vmem] * len(operands),
        out_specs=[in_vmem] * len(out_shape) if many else in_vmem,
        scratch_shapes=list(scratch),
        compiler_params=pltpu.CompilerParams(vmem_limit_bytes=vmem_limit),
        cost_estimate=pl.CostEstimate(
            flops=flops, bytes_accessed=moved, transcendentals=transcendentals
        ),
    )(*operands)


def flip(value, mask):
    pairs = [(source, source ^ mask) for source in range(lax.axis_size("seq"))]
    return lax.ppermute(value, "seq", pairs)


def attention_body(blocks, heads, *refs):
    query_ref, block_refs, out_ref = refs[0], refs[1 : 1 + blocks], refs[1 + blocks]
    rank = lax.axis_index("seq")
    inside = jnp.logical_and(rank > 0, rank < lax.axis_size("seq") - 1)
    bias = jnp.where(inside, 0.0, masked_score).astype(jnp.float32)
    scale = math.log2(math.e) / math.sqrt(HD)

    def scores_of(head):
        query = query_ref[:, head * HD : (head + 1) * HD]
        scores = [
            lax.dot_general(
                query, ref[0], (((1,), (1,)), ((), ())), preferred_element_type=jnp.float32
            )
            for ref in block_refs
        ]
        scores[-1] = scores[-1] + bias
        return scores

    scores = scores_of(0)
    for head in range(heads):
        later = scores_of(head + 1) if head + 1 < heads else None
        peak = jnp.max(functools.reduce(jnp.maximum, scores), axis=1, keepdims=True) * scale
        weights = [jnp.exp2(part * scale - peak) for part in scores]
        weight_sum = jnp.sum(functools.reduce(jnp.add, weights), axis=1, keepdims=True)
        numerator = functools.reduce(
            jnp.add,
            [
                jnp.dot(part.astype(jnp.bfloat16), ref[1], preferred_element_type=jnp.float32)
                for part, ref in zip(weights, block_refs)
            ],
        )
        out_ref[:, head * HD : (head + 1) * HD] = (numerator / weight_sum).astype(jnp.bfloat16)
        scores = later


def attend(queries, pieces):
    blocks, (rows, width) = len(pieces), queries.shape
    pairs = rows * blocks * BLK * (width // HD)
    return call_kernel(
        functools.partial(attention_body, blocks, width // HD),
        jax.ShapeDtypeStruct(queries.shape, jnp.bfloat16),
        [queries, *pieces],
        flops=4 * pairs * HD,
        moved=4 * queries.size + 2 * blocks * pieces[0].size,
        transcendentals=pairs,
    )


def exchange_blocks(rows):
    count = lax.axis_size("seq")
    bits = count.bit_length() - 1
    outer = [(i, i + 1) for i in range(1, count - 1, 2)]
    outer = outer + [(j, i) for i, j in outer]
    far = [flip(rows, 1 << bit) for bit in range(bits - 1, 1, -1)]
    beside = lax.ppermute(rows, "seq", outer)
    return [rows, flip(rows, 1), flip(rows, 2)] + far + [beside]


def after(value, earlier):
    return lax.optimization_barrier((value, earlier))[0]


class Ring:
    def __init__(self):
        self.count = lax.axis_size("seq")
        self.layers = self.count // 4
        self.chips = self.count // 2

    def place(self, index):
        layer = jnp.where(index < self.layers, index, self.chips - 1 - index)
        return layer, (index >= self.layers).astype(jnp.int32)

    def index(self):
        rank = lax.axis_index("seq")
        layer = rank // 4
        return jnp.where(rank // 2 % 2 == 0, layer, self.chips - 1 - layer)

    def shift(self, value, step):
        def rank_of(index):
            index = index % self.chips
            return 4 * index if index < self.layers else 4 * (self.chips - 1 - index) + 2

        pairs = [
            (rank_of(index) + core, rank_of(index + step) + core)
            for index in range(self.chips)
            for core in (0, 1)
        ]
        return lax.ppermute(value, "seq", pairs)

    def offsets(self):
        steps = [0]
        for step in range(1, self.chips // 2):
            steps += [step, -step]
        return steps + [self.chips // 2]

    def side_and_slot(self, offset):
        layer, across = self.place(lax.rem(self.index() + offset + self.chips, self.chips))
        per_side = self.layers // 2
        return layer // per_side, 2 * lax.rem(layer, per_side) + across

    def ranks(self, side, offsets):
        before, answer = jnp.int32(0), []
        for offset in offsets:
            belongs = self.side_and_slot(offset)[0] == side
            answer.append((belongs, before))
            before = before + belongs.astype(jnp.int32)
        return answer


def hold(held, slot, same_ref, other_ref):
    step = same_ref.shape[0]
    core = lax.axis_index("seq") % 2
    for where, ref in ((core, same_ref), (1 - core, other_ref)):
        held[pl.ds(pl.multiple_of((2 * slot + where) * step, 16), step), :] = ref[...]


def times(rows_ref, weight):
    return lax.dot_general(
        rows_ref[...], weight, (((1,), (1,)), ((), ())), preferred_element_type=jnp.float32
    )


def sent_body(first, width, offsets, *refs):
    rows_ref, same_refs = refs[0], refs[1 : 1 + len(offsets)]
    other_refs, (out_ref, held) = refs[1 + len(offsets) : 1 + 2 * len(offsets)], refs[-2:]
    ring = Ring()
    ranks = ring.ranks(1 - lax.axis_index("head"), offsets)
    for (belongs, rank), same_ref, other_ref in zip(ranks, same_refs, other_refs):
        for slot in range(width):

            @pl.when(jnp.logical_and(belongs, rank == first + slot))
            def _():
                hold(held, slot, same_ref, other_ref)

    out_ref[...] = times(rows_ref, held[...]).astype(jnp.bfloat16)


def sent(attended, first, width, offsets, same, other):
    step, depth = same[0].shape
    columns = 2 * width * step
    return call_kernel(
        functools.partial(sent_body, first, width, offsets),
        jax.ShapeDtypeStruct((attended.shape[0], columns), jnp.bfloat16),
        [attended, *same[: len(offsets)], *other[: len(offsets)]],
        scratch=[pltpu.VMEM((columns, depth), jnp.bfloat16)],
        flops=2 * attended.size * columns,
        moved=2 * columns * (attended.shape[0] + depth),
    )


def kept_body(offsets, *refs):
    rows_ref, same_refs = refs[0], refs[1 : 1 + len(offsets)]
    other_refs, (out_ref, held) = refs[1 + len(offsets) : 1 + 2 * len(offsets)], refs[-2:]
    ring, head = Ring(), lax.axis_index("head")
    for offset, same_ref, other_ref in zip(offsets, same_refs, other_refs):
        side, slot = ring.side_and_slot(offset)

        @pl.when(side == head)
        def _():
            hold(held, slot, same_ref, other_ref)

    slots, _, columns = out_ref.shape
    for slot in range(slots):
        out_ref[slot] = times(rows_ref, held[slot * columns : (slot + 1) * columns, :])


def kept(attended, offsets, same, other):
    (step, depth), slots = same[0].shape, len(offsets) // 2
    return call_kernel(
        functools.partial(kept_body, offsets),
        jax.ShapeDtypeStruct((slots, attended.shape[0], 2 * step), jnp.float32),
        [attended, *same, *other],
        scratch=[pltpu.VMEM((2 * slots * step, depth), jnp.bfloat16)],
        flops=4 * attended.size * slots * step,
        moved=4 * slots * step * (2 * attended.shape[0] + depth),
    )


def total_body(offsets, widths, *refs):
    kept_ref, received, out_ref = refs[0], refs[1:-1], refs[-1]
    ring = Ring()
    slots, _, columns = kept_ref.shape
    ranks = ring.ranks(lax.axis_index("head"), offsets)
    placed = [(ref, at) for ref, width in zip(received, widths) for at in range(width)]
    slot_of = [jnp.int32(0)] * len(placed)
    for offset, (belongs, rank) in zip(offsets, ranks):
        slot = ring.side_and_slot(offset)[1]
        for entry in range(len(placed)):
            here = jnp.logical_and(belongs, rank == entry)
            slot_of[entry] = jnp.where(here, slot, slot_of[entry])
    for slot in range(slots):
        for entry, (ref, at) in enumerate(placed):

            @pl.when(slot_of[entry] == slot)
            def _():
                there = ref[:, at * columns : (at + 1) * columns].astype(jnp.float32)
                out_ref[:, slot * columns : (slot + 1) * columns] = (kept_ref[slot] + there).astype(
                    jnp.bfloat16
                )


def total(kept_terms, received, widths, offsets):
    slots, rows, columns = kept_terms.shape
    return call_kernel(
        functools.partial(total_body, offsets, widths),
        jax.ShapeDtypeStruct((rows, slots * columns), jnp.bfloat16),
        [kept_terms, *received],
        moved=8 * kept_terms.size,
    )


def project_on_ring(queries, kv, out_weight):
    ring = Ring()
    shard = out_weight.T
    half = shard.shape[0] // 2

    def swap(value):
        return lax.ppermute(value, "head", [(0, 1), (1, 0)])

    def both_ways(onward, back):
        return ring.shift(onward, -1), ring.shift(back, 1)

    offsets = ring.offsets()
    same = [shard]
    pieces = exchange_blocks(kv)
    tied = (1, 2, 3, 4, 5)
    tied_pieces = [pieces[i] for i in tied]
    shard, tied_pieces = lax.optimization_barrier((shard, tied_pieces))
    for i, piece in zip(tied, tied_pieces):
        pieces[i] = piece
    first_pair = both_ways(shard, shard)
    attended = attend(queries, pieces)
    first_pair, attended = lax.optimization_barrier((first_pair, attended))
    second_pair = both_ways(*first_pair)
    third_pair = both_ways(*second_pair)
    same = [shard, *first_pair, *second_pair, *third_pair]
    other = [flip(value, 1) for value in same]
    first = swap(sent(attended, 0, 1, offsets[:5], same, other))
    third_pair, first = lax.optimization_barrier((third_pair, first))
    opposite = both_ways(third_pair[0][:half], third_pair[1][half:])
    same.append(jnp.concatenate(opposite, axis=0))
    other.append(flip(same[-1], 1))
    widths = (1, 2, 1)
    second = swap(sent(attended, 1, 2, offsets[:7], same, other))
    third = swap(sent(attended, 3, 1, offsets, same, other))
    terms = kept(attended, offsets, same, other)
    return total(terms, [first, second, third], widths, offsets)


def project_gathered(attended, out_weight):
    terms = jnp.dot(
        attended,
        lax.all_gather(out_weight, "seq", axis=1, tiled=True),
        preferred_element_type=jnp.float32,
    )
    return lax.psum_scatter(terms.astype(jnp.bfloat16), "head", scatter_dimension=1, tiled=True)


def local(queries, key_rows, value_rows, out_weight):
    kv = jnp.stack([key_rows, value_rows])
    chips = lax.axis_size("seq") // 2
    if chips == 8 and lax.axis_size("head") == 2 and out_weight.shape[1] % 32 == 0:
        return project_on_ring(queries, kv, out_weight)
    attended = attend(queries, exchange_blocks(kv))
    return project_gathered(attended, out_weight)


def solution(mesh):
    in_specs = (P("seq", "head"), P("seq", "head"), P("seq", "head"), P("head", "seq"))
    out_specs = P("seq", "head")
    return jax.shard_map(local, mesh=mesh, in_specs=in_specs, out_specs=out_specs, check_vma=False)
```

time: 119 us -> 80.1 us (0.67)
  waiting for transfers between devices: 73.8 us -> 45.5 us
  between operations: 13.6 us -> 0.11 us
  matrix products: 13.2 us -> 0 us
  starting transfers between devices: 12.8 us -> 22.9 us
  Pallas kernels: 0 us -> 9.38 us
  other arithmetic: 3.53 us -> 0.88 us
    ppermute x5 -> x24, waiting for transfers between devices: 9.06 us -> 45.5 us  [the longest x8 26.3 us: shift(): return lax.ppermute(value, 'seq', pairs)]
    all_gather x1 -> x0, waiting for transfers between devices: 36.3 us -> none  [local(): lax.all_gather(out_weight, 'seq', axis=1, tiled=True)]
    reduce_scatter x1 -> x0, waiting for transfers between devices: 27.7 us -> none  [local(): lax.psum_scatter(column_terms.astype(jnp.bfloat16), 'head', scatter_dimen...]
    dot_general x15 -> x0, matrix products: 13.2 us -> none  [the longest x1 6.25 us: local(): jnp.dot(results, lax.all_gather(out_weight, 'seq', axis=1, tiled=True), p...]
    ppermute x5 -> x24, starting transfers between devices: 12.7 us -> 22.9 us  [the longest x12 9.52 us: flip(): return lax.ppermute(value, 'seq', pairs)]
    pallas_call x0 -> x6, Pallas kernels: none -> 9.38 us  [call_kernel(): pl.pallas_call(body, out_shape=out_shape, in_specs=[in_vmem] * len(operan...]
    reduce_sum x7 -> x0, other arithmetic: 2.53 us -> none  [head_partial(): weight_sum = jnp.sum(weights, axis=1)]
  transfers between devices with their start and end apart: 7 -> 24, of which waited for: 3 -> 11; matrix products, arithmetic and copies ran while one was open for 10% -> 0% of each run, Pallas kernels for 0% -> 10%
where the time goes in v1:
time: 80.1 us; the launch traced here: 79.9 us
  waiting for transfers between devices  45.5 us (57%)
  starting transfers between devices  22.9 us (29%)
  Pallas kernels  9.38 us (12%)
  local copies, waits for them, and re-layouts  1.1 us (1%)
  other arithmetic  0.88 us (1%)
    ppermute x8, waiting for transfers between devices, shift(): return lax.ppermute(value, 'seq', pairs)  26.3 us
    ppermute x3, waiting for transfers between devices, swap(): return lax.ppermute(value, 'head', [(0, 1), (1, 0)])  14 us
    ppermute x12, starting transfers between devices, flip(): return lax.ppermute(value, 'seq', pairs)  9.52 us
    pallas_call x6, Pallas kernels, call_kernel(): pl.pallas_call(body, out_shape=out_shape, in_specs=[in_vmem] * len(operan...  9.38 us
    ppermute x8, starting transfers between devices, shift(): return lax.ppermute(value, 'seq', pairs)  8.81 us
    ppermute x12, waiting for transfers between devices, flip(): return lax.ppermute(value, 'seq', pairs)  5.22 us
    ppermute x3, starting transfers between devices, swap(): return lax.ppermute(value, 'head', [(0, 1), (1, 0)])  3.86 us
  transfers between devices with their start and end apart: 24, of which 11 were waited for; matrix products, arithmetic and copies ran while one was open for 0% of the time, Pallas kernels for 10%

profile of v1, /device:TPU:0, one launch (start us, length us, event | category | flops | bytes accessed | tf_op | source)
XLA Modules:
  0.0 79.9 jit_solution(6580301168962058830)
XLA Ops:
  0.0 0.9 %pad_maximum_fusion.refs_1_ = bf16[2,256,128]{2,1,0:T(8,128)(2,1)S(1)} fusion(bf16[1,256,128]{2,1,0:T(8,128)(2,1)} %bitcast.10, bf16[1,256,128]{2,1,0:T(8,128)(2,1)} %bitcast.11), kind=kLoop, calls=%fused_computation | loop fusion | flops 65536 | bytes 262144 | tf_op jit(solution)/shard_map/stack | solution.py:298
  0.9 0.7 collective-permute-start.4
  1.6 5.1 %collective-permute-start.3 = (bf16[2,256,128]{2,1,0:T(8,128)(2,1)S(1)}, bf16[2,256,128]{2,1,0:T(8,128)(2,1)S(1)}, u32[]{:S(2)}, u32[]{:S(2)}) collective-permute-start(bf16[2,256,128]{2,1,0:T(8,128)(2,1)S(1)} %pad_maximum_fusion.refs_1_), channel_id=1, source_target_pairs={{0,8},{2,10},{4,12},{6,14},{8,0},{10,2},{12,4},{14,6},{16,24},{18,... | collective-permute-start | bytes 393224 | tf_op jit(solution)/shard_map/ppermute | solution.py:36
  6.7 2.6 %collective-permute-start.2 = (bf16[2,256,128]{2,1,0:T(8,128)(2,1)S(1)}, bf16[2,256,128]{2,1,0:T(8,128)(2,1)S(1)}, u32[]{:S(2)}, u32[]{:S(2)}) collective-permute-start(bf16[2,256,128]{2,1,0:T(8,128)(2,1)S(1)} %pad_maximum_fusion.refs_1_), channel_id=1, source_target_pairs={{0,16},{2,18},{4,20},{6,22},{8,24},{10,26},{12,28},{14,30},{16,0},... | collective-permute-start | bytes 393224 | tf_op jit(solution)/shard_map/ppermute | solution.py:36
  9.3 0.7 collective-permute-start.1
  10.0 5.2 %collective-permute-done.3.refs_5_ = bf16[2,256,128]{2,1,0:T(8,128)(2,1)S(1)} collective-permute-done((bf16[2,256,128]{2,1,0:T(8,128)(2,1)S(1)}, bf16[2,256,128]{2,1,0:T(8,128)(2,1)S(1)}, u32[]{:S(2)}, u32[]{:S(2)}) %collective-permute-start.3) | collective-permute-done | bytes 131104 | tf_op jit(solution)/shard_map/ppermute | solution.py:36
  15.2 2.6 %collective-permute-start.6 = (bf16[224,896]{1,0:T(8,128)(2,1)}, bf16[224,896]{1,0:T(8,128)(2,1)S(1)}, u32[]{:S(2)}, u32[]{:S(2)}) collective-permute-start(bf16[224,896]{1,0:T(8,128)(2,1)} %bitcast.3), channel_id=1, source_target_pairs={{0,8},{2,10},{8,16},{10,18},{16,24},{18,26},{24,28},{26,30},{28,20... | collective-permute-start | bytes 1204232 | tf_op jit(solution)/shard_map/ppermute | solution.py:126
  17.8 1.0 %copy-done.1 = bf16[256,896]{1,0:T(8,128)(2,1)S(1)} copy-done((bf16[256,896]{1,0:T(8,128)(2,1)S(1)}, bf16[256,896]{1,0:T(8,128)(2,1)}, u32[]{:S(2)}) %copy-start.1) | copy-done | bytes 458776
  18.9 4.2 %shard_map.46.refs_0_ = bf16[256,896]{1,0:T(8,128)(2,1)S(1)} custom-call(bf16[256,896]{1,0:T(8,128)(2,1)S(1)} %copy-done.1, bf16[2,256,128]{2,1,0:T(8,128)(2,1)S(1)} %pad_maximum_fusion.refs_1_, bf16[2,256,128]{2,1,0:T(8,128)(2,1)S(1)} %collective-permute-done.refs_2_, bf16[2,256,128]{2,1,0:T(8,128)(2,1)S(1)} %collective-permute-done.1.refs_3_, ...), custom_call_target="tpu_custom_call" | custom-call | flops 1409286144 | bytes 1703936 | tf_op jit(solution)/shard_map/pallas_call | solution.py:21
  23.0 4.1 %collective-permute-done.6.refs_3_ = bf16[224,896]{1,0:T(8,128)(2,1)S(1)} collective-permute-done((bf16[224,896]{1,0:T(8,128)(2,1)}, bf16[224,896]{1,0:T(8,128)(2,1)S(1)}, u32[]{:S(2)}, u32[]{:S(2)}) %collective-permute-start.6) | collective-permute-done | bytes 401440 | tf_op jit(solution)/shard_map/ppermute | solution.py:126
  27.1 0.8 %collective-permute-done.5.refs_2_ = bf16[224,896]{1,0:T(8,128)(2,1)S(1)} collective-permute-done((bf16[224,896]{1,0:T(8,128)(2,1)}, bf16[224,896]{1,0:T(8,128)(2,1)S(1)}, u32[]{:S(2)}, u32[]{:S(2)}) %collective-permute-start.5) | collective-permute-done | bytes 401440 | tf_op jit(solution)/shard_map/ppermute | solution.py:126
  27.9 0.9 %collective-permute-start.7 = (bf16[224,896]{1,0:T(8,128)(2,1)S(1)}, bf16[224,896]{1,0:T(8,128)(2,1)S(1)}, u32[]{:S(2)}, u32[]{:S(2)}) collective-permute-start(bf16[224,896]{1,0:T(8,128)(2,1)S(1)} %collective-permute-done.5.refs_2_), channel_id=1, source_target_pairs={{0,4},{2,6},{8,0},{10,2},{16,8},{18,10},{24,16},{26,18},{28,24},{3... | collective-permute-start | bytes 1204232 | tf_op jit(solution)/shard_map/ppermute | solution.py:126
  28.9 1.1 %collective-permute-start.8 = (bf16[224,896]{1,0:T(8,128)(2,1)S(1)}, bf16[224,896]{1,0:T(8,128)(2,1)S(1)}, u32[]{:S(2)}, u32[]{:S(2)}) collective-permute-start(bf16[224,896]{1,0:T(8,128)(2,1)S(1)} %collective-permute-done.6.refs_3_), channel_id=1, source_target_pairs={{0,8},{2,10},{8,16},{10,18},{16,24},{18,26},{24,28},{26,30},{28,20... | collective-permute-start | bytes 1204232 | tf_op jit(solution)/shard_map/ppermute | solution.py:126
  30.5 7.4 %collective-permute-done.7.refs_4_ = bf16[224,896]{1,0:T(8,128)(2,1)S(1)} collective-permute-done((bf16[224,896]{1,0:T(8,128)(2,1)S(1)}, bf16[224,896]{1,0:T(8,128)(2,1)S(1)}, u32[]{:S(2)}, u32[]{:S(2)}) %collective-permute-start.7) | collective-permute-done | bytes 401440 | tf_op jit(solution)/shard_map/ppermute | solution.py:126
  37.9 1.1 %collective-permute-done.8.refs_5_ = bf16[224,896]{1,0:T(8,128)(2,1)S(1)} collective-permute-done((bf16[224,896]{1,0:T(8,128)(2,1)S(1)}, bf16[224,896]{1,0:T(8,128)(2,1)S(1)}, u32[]{:S(2)}, u32[]{:S(2)}) %collective-permute-start.8) | collective-permute-done | bytes 401440 | tf_op jit(solution)/shard_map/ppermute | solution.py:126
  39.0 1.4 %collective-permute-start.9 = (bf16[224,896]{1,0:T(8,128)(2,1)S(1)}, bf16[224,896]{1,0:T(8,128)(2,1)S(1)}, u32[]{:S(2)}, u32[]{:S(2)}) collective-permute-start(bf16[224,896]{1,0:T(8,128)(2,1)S(1)} %collective-permute-done.7.refs_4_), channel_id=1, source_target_pairs={{0,4},{2,6},{8,0},{10,2},{16,8},{18,10},{24,16},{26,18},{28,24},{3... | collective-permute-start | bytes 1204232 | tf_op jit(solution)/shard_map/ppermute | solution.py:126
  40.5 0.6 collective-permute-start.10
  41.1 0.6 shard_map.47
  41.7 1.6 %collective-permute-start.16 = (bf16[256,448]{1,0:T(8,128)(2,1)S(1)}, bf16[256,448]{1,0:T(8,128)(2,1)S(1)}, u32[]{:S(2)}, u32[]{:S(2)}) collective-permute-start(bf16[256,448]{1,0:T(8,128)(2,1)S(1)} %shard_map.47), channel_id=1, source_target_pairs={{0,1},{1,0},{2,3},{3,2},{4,5},{5,4},{6,7},{7,6},{8,9},{9,8},{10,11... | collective-permute-start | bytes 688136 | tf_op jit(solution)/shard_map/ppermute | solution.py:256
  43.3 7.5 %collective-permute-done.9.refs_6_ = bf16[224,896]{1,0:T(8,128)(2,1)S(1)} collective-permute-done((bf16[224,896]{1,0:T(8,128)(2,1)S(1)}, bf16[224,896]{1,0:T(8,128)(2,1)S(1)}, u32[]{:S(2)}, u32[]{:S(2)}) %collective-permute-start.9) | collective-permute-done | bytes 401440 | tf_op jit(solution)/shard_map/ppermute | solution.py:126
  50.8 1.1 %collective-permute-done.10.refs_7_ = bf16[224,896]{1,0:T(8,128)(2,1)S(1)} collective-permute-done((bf16[224,896]{1,0:T(8,128)(2,1)S(1)}, bf16[224,896]{1,0:T(8,128)(2,1)S(1)}, u32[]{:S(2)}, u32[]{:S(2)}) %collective-permute-start.10) | collective-permute-done | bytes 401440 | tf_op jit(solution)/shard_map/ppermute | solution.py:126
  51.9 0.8 %collective-permute-start.17 = (bf16[112,896]{1,0:T(8,128)(2,1)S(1)}, bf16[112,896]{1,0:T(8,128)(2,1)S(1)}, u32[]{:S(2)}, u32[]{:S(2)}) collective-permute-start(bf16[112,896]{1,0:T(8,128)(2,1)S(1)} %slice.6), channel_id=1, source_target_pairs={{0,4},{2,6},{8,0},{10,2},{16,8},{18,10},{24,16},{26,18},{28,24},{3... | collective-permute-start | bytes 602120 | tf_op jit(solution)/shard_map/ppermute | solution.py:126
  52.8 1.3 %collective-permute-start.18 = (bf16[112,896]{1,0:T(8,128)(2,1)S(1)}, bf16[112,896]{1,0:T(8,128)(2,1)S(1)}, u32[]{:S(2)}, u32[]{:S(2)}) collective-permute-start(bf16[112,896]{1,0:T(8,128)(2,1)S(1)} %slice.7), channel_id=1, source_target_pairs={{0,8},{2,10},{8,16},{10,18},{16,24},{18,26},{24,28},{26,30},{28,20... | collective-permute-start | bytes 602120 | tf_op jit(solution)/shard_map/ppermute | solution.py:126
  54.6 3.7 %collective-permute-done.17 = bf16[112,896]{1,0:T(8,128)(2,1)S(1)} collective-permute-done((bf16[112,896]{1,0:T(8,128)(2,1)S(1)}, bf16[112,896]{1,0:T(8,128)(2,1)S(1)}, u32[]{:S(2)}, u32[]{:S(2)}) %collective-permute-start.17) | collective-permute-done | bytes 200736 | tf_op jit(solution)/shard_map/ppermute | solution.py:126
  58.3 0.5 collective-permute-done.18
  59.0 1.0 %shard_map.49 = bf16[256,896]{1,0:T(8,128)(2,1)S(1)} custom-call(bf16[256,896]{1,0:T(8,128)(2,1)S(1)} %shard_map.46.refs_0_, bf16[224,896]{1,0:T(8,128)(2,1)S(1)} %bitcast.7, bf16[224,896]{1,0:T(8,128)(2,1)S(1)} %collective-permute-done.5.refs_2_, bf16[224,896]{1,0:T(8,128)(2,1)S(1)} %collective-permute-done.6.refs_3_, ...), custom_call_target="tpu_custom_call" | custom-call | flops 411041792 | bytes 2064384 | tf_op jit(solution)/shard_map/pallas_call | solution.py:21
  60.0 1.6 %collective-permute-start.22 = (bf16[256,896]{1,0:T(8,128)(2,1)S(1)}, bf16[256,896]{1,0:T(8,128)(2,1)S(1)}, u32[]{:S(2)}, u32[]{:S(2)}) collective-permute-start(bf16[256,896]{1,0:T(8,128)(2,1)S(1)} %shard_map.49), channel_id=1, source_target_pairs={{0,1},{1,0},{2,3},{3,2},{4,5},{5,4},{6,7},{7,6},{8,9},{9,8},{10,11... | collective-permute-start | bytes 1376264 | tf_op jit(solution)/shard_map/ppermute | solution.py:256
  62.1 0.7 collective-permute-start.23
  62.8 1.6 %shard_map.48.refs_0_ = f32[4,256,448]{2,1,0:T(8,128)S(1)} custom-call(bf16[256,896]{1,0:T(8,128)(2,1)S(1)} %shard_map.46.refs_0_, bf16[224,896]{1,0:T(8,128)(2,1)S(1)} %bitcast.9, bf16[224,896]{1,0:T(8,128)(2,1)S(1)} %collective-permute-done.5.refs_2_, bf16[224,896]{1,0:T(8,128)(2,1)S(1)} %collective-permute-done.6.refs_3_, ...), custom_call_target="tpu_custom_call" | custom-call | flops 822083584 | bytes 5046272 | tf_op jit(solution)/shard_map/pallas_call | solution.py:21
  64.4 9.0 %collective-permute-done.22.refs_2_ = bf16[256,896]{1,0:T(8,128)(2,1)S(1)} collective-permute-done((bf16[256,896]{1,0:T(8,128)(2,1)S(1)}, bf16[256,896]{1,0:T(8,128)(2,1)S(1)}, u32[]{:S(2)}, u32[]{:S(2)}) %collective-permute-start.22) | collective-permute-done | bytes 458784 | tf_op jit(solution)/shard_map/ppermute | solution.py:256
  73.4 5.1 %collective-permute-done.23.refs_3_ = bf16[256,448]{1,0:T(8,128)(2,1)S(1)} collective-permute-done((bf16[256,448]{1,0:T(8,128)(2,1)S(1)}, bf16[256,448]{1,0:T(8,128)(2,1)S(1)}, u32[]{:S(2)}, u32[]{:S(2)}) %collective-permute-start.23) | collective-permute-done | bytes 229408 | tf_op jit(solution)/shard_map/ppermute | solution.py:256
  78.4 1.4 %shard_map.51 = bf16[256,1792]{1,0:T(8,128)(2,1)} custom-call(f32[4,256,448]{2,1,0:T(8,128)S(1)} %shard_map.48.refs_0_, bf16[256,448]{1,0:T(8,128)(2,1)S(1)} %collective-permute-done.16.refs_1_, bf16[256,896]{1,0:T(8,128)(2,1)S(1)} %collective-permute-done.22.refs_2_, bf16[256,448]{1,0:T(8,128)(2,1)S(1)} %collective-permute-done.23.refs_3_), custom_call_target="tpu_custom_call" | custom-call | bytes 3670016 | tf_op jit(solution)/shard_map/pallas_call | solution.py:21
  (31 shorter events, 1.7 us)
Async XLA Ops:
  0.9 9.1 %collective-permute-start.4 = (bf16[2,256,128]{2,1,0:T(8,128)(2,1)S(1)}, bf16[2,256,128]{2,1,0:T(8,128)(2,1)S(1)}, u32[]{:S(2)}, u32[]{:S(2)}) collective-permute-start(bf16[2,256,128]{2,1,0:T(8,128)(2,1)S(1)} %pad_maximum_fusion.refs_1_), channel_id=1, source_target_pairs={{2,4},{6,8},{10,12},{14,16},{18,20},{22,24},{26,28},{4,2},{8,6},{1... | collective-permute-start | bytes 393224 | tf_op jit(solution)/shard_map/ppermute | solution.py:93
  1.6 13.6 %collective-permute-start.3 = (bf16[2,256,128]{2,1,0:T(8,128)(2,1)S(1)}, bf16[2,256,128]{2,1,0:T(8,128)(2,1)S(1)}, u32[]{:S(2)}, u32[]{:S(2)}) collective-permute-start(bf16[2,256,128]{2,1,0:T(8,128)(2,1)S(1)} %pad_maximum_fusion.refs_1_), channel_id=1, source_target_pairs={{0,8},{2,10},{4,12},{6,14},{8,0},{10,2},{12,4},{14,6},{16,24},{18,... | collective-permute-start | bytes 393224 | tf_op jit(solution)/shard_map/ppermute | solution.py:36
  6.7 8.5 %collective-permute-start.2 = (bf16[2,256,128]{2,1,0:T(8,128)(2,1)S(1)}, bf16[2,256,128]{2,1,0:T(8,128)(2,1)S(1)}, u32[]{:S(2)}, u32[]{:S(2)}) collective-permute-start(bf16[2,256,128]{2,1,0:T(8,128)(2,1)S(1)} %pad_maximum_fusion.refs_1_), channel_id=1, source_target_pairs={{0,16},{2,18},{4,20},{6,22},{8,24},{10,26},{12,28},{14,30},{16,0},... | collective-permute-start | bytes 393224 | tf_op jit(solution)/shard_map/ppermute | solution.py:36
  9.3 5.9 %collective-permute-start.1 = (bf16[2,256,128]{2,1,0:T(8,128)(2,1)S(1)}, bf16[2,256,128]{2,1,0:T(8,128)(2,1)S(1)}, u32[]{:S(2)}, u32[]{:S(2)}) collective-permute-start(bf16[2,256,128]{2,1,0:T(8,128)(2,1)S(1)} %pad_maximum_fusion.refs_1_), channel_id=1, source_target_pairs={{0,4},{2,6},{4,0},{6,2},{8,12},{10,14},{12,8},{14,10},{16,20},{18,... | collective-permute-start | bytes 393224 | tf_op jit(solution)/shard_map/ppermute | solution.py:36
  10.0 5.2 %collective-permute-start = (bf16[2,256,128]{2,1,0:T(8,128)(2,1)S(1)}, bf16[2,256,128]{2,1,0:T(8,128)(2,1)S(1)}, u32[]{:S(2)}, u32[]{:S(2)}) collective-permute-start(bf16[2,256,128]{2,1,0:T(8,128)(2,1)S(1)} %pad_maximum_fusion.refs_1_), channel_id=1, source_target_pairs={{0,2},{2,0},{4,6},{6,4},{8,10},{10,8},{12,14},{14,12},{16,18},{18,... | collective-permute-start | bytes 393224 | tf_op jit(solution)/shard_map/ppermute | solution.py:36
  15.2 14.8 %copy-start = (bf16[896,224]{0,1:T(8,128)(2,1)S(1)}, bf16[896,224]{0,1:T(8,128)(2,1)}, u32[]{:S(2)}) copy-start(bf16[896,224]{0,1:T(8,128)(2,1)} %param.7) | copy-start | bytes 1204228
  15.2 11.9 %collective-permute-start.6 = (bf16[224,896]{1,0:T(8,128)(2,1)}, bf16[224,896]{1,0:T(8,128)(2,1)S(1)}, u32[]{:S(2)}, u32[]{:S(2)}) collective-permute-start(bf16[224,896]{1,0:T(8,128)(2,1)} %bitcast.3), channel_id=1, source_target_pairs={{0,8},{2,10},{8,16},{10,18},{16,24},{18,26},{24,28},{26,30},{28,20... | collective-permute-start | bytes 1204232 | tf_op jit(solution)/shard_map/ppermute | solution.py:126
  17.8 10.1 %collective-permute-start.5 = (bf16[224,896]{1,0:T(8,128)(2,1)}, bf16[224,896]{1,0:T(8,128)(2,1)S(1)}, u32[]{:S(2)}, u32[]{:S(2)}) collective-permute-start(bf16[224,896]{1,0:T(8,128)(2,1)} %bitcast.4), channel_id=1, source_target_pairs={{0,4},{2,6},{8,0},{10,2},{16,8},{18,10},{24,16},{26,18},{28,24},{3... | collective-permute-start | bytes 1204232 | tf_op jit(solution)/shard_map/ppermute | solution.py:126
  17.8 1.0 %copy-start.1 = (bf16[256,896]{1,0:T(8,128)(2,1)S(1)}, bf16[256,896]{1,0:T(8,128)(2,1)}, u32[]{:S(2)}) copy-start(bf16[256,896]{1,0:T(8,128)(2,1)} %refs_0_.1) | copy-start | bytes 1376260
  27.9 10.0 %collective-permute-start.7 = (bf16[224,896]{1,0:T(8,128)(2,1)S(1)}, bf16[224,896]{1,0:T(8,128)(2,1)S(1)}, u32[]{:S(2)}, u32[]{:S(2)}) collective-permute-start(bf16[224,896]{1,0:T(8,128)(2,1)S(1)} %collective-permute-done.5.refs_2_), channel_id=1, source_target_pairs={{0,4},{2,6},{8,0},{10,2},{16,8},{18,10},{24,16},{26,18},{28,24},{3... | collective-permute-start | bytes 1204232 | tf_op jit(solution)/shard_map/ppermute | solution.py:126
  28.9 10.2 %collective-permute-start.8 = (bf16[224,896]{1,0:T(8,128)(2,1)S(1)}, bf16[224,896]{1,0:T(8,128)(2,1)S(1)}, u32[]{:S(2)}, u32[]{:S(2)}) collective-permute-start(bf16[224,896]{1,0:T(8,128)(2,1)S(1)} %collective-permute-done.6.refs_3_), channel_id=1, source_target_pairs={{0,8},{2,10},{8,16},{10,18},{16,24},{18,26},{24,28},{26,30},{28,20... | collective-permute-start | bytes 1204232 | tf_op jit(solution)/shard_map/ppermute | solution.py:126
  30.0 9.1 %collective-permute-start.11 = (bf16[224,896]{1,0:T(8,128)(2,1)S(1)}, bf16[224,896]{1,0:T(8,128)(2,1)S(1)}, u32[]{:S(2)}, u32[]{:S(2)}) collective-permute-start(bf16[224,896]{1,0:T(8,128)(2,1)S(1)} %bitcast.5), channel_id=1, source_target_pairs={{0,2},{2,0},{4,6},{6,4},{8,10},{10,8},{12,14},{14,12},{16,18},{18,... | collective-permute-start | bytes 1204232 | tf_op jit(solution)/shard_map/ppermute | solution.py:36
  30.0 10.5 %collective-permute-start.12 = (bf16[224,896]{1,0:T(8,128)(2,1)S(1)}, bf16[224,896]{1,0:T(8,128)(2,1)S(1)}, u32[]{:S(2)}, u32[]{:S(2)}) collective-permute-start(bf16[224,896]{1,0:T(8,128)(2,1)S(1)} %collective-permute-done.5.refs_2_), channel_id=1, source_target_pairs={{0,2},{2,0},{4,6},{6,4},{8,10},{10,8},{12,14},{14,12},{16,18},{18,... | collective-permute-start | bytes 1204232 | tf_op jit(solution)/shard_map/ppermute | solution.py:36
  30.5 10.6 %collective-permute-start.13 = (bf16[224,896]{1,0:T(8,128)(2,1)S(1)}, bf16[224,896]{1,0:T(8,128)(2,1)S(1)}, u32[]{:S(2)}, u32[]{:S(2)}) collective-permute-start(bf16[224,896]{1,0:T(8,128)(2,1)S(1)} %collective-permute-done.6.refs_3_), channel_id=1, source_target_pairs={{0,2},{2,0},{4,6},{6,4},{8,10},{10,8},{12,14},{14,12},{16,18},{18,... | collective-permute-start | bytes 1204232 | tf_op jit(solution)/shard_map/ppermute | solution.py:36
  37.9 3.2 %collective-permute-start.14 = (bf16[224,896]{1,0:T(8,128)(2,1)S(1)}, bf16[224,896]{1,0:T(8,128)(2,1)S(1)}, u32[]{:S(2)}, u32[]{:S(2)}) collective-permute-start(bf16[224,896]{1,0:T(8,128)(2,1)S(1)} %collective-permute-done.7.refs_4_), channel_id=1, source_target_pairs={{0,2},{2,0},{4,6},{6,4},{8,10},{10,8},{12,14},{14,12},{16,18},{18,... | collective-permute-start | bytes 1204232 | tf_op jit(solution)/shard_map/ppermute | solution.py:36
  39.0 2.0 %collective-permute-start.15 = (bf16[224,896]{1,0:T(8,128)(2,1)S(1)}, bf16[224,896]{1,0:T(8,128)(2,1)S(1)}, u32[]{:S(2)}, u32[]{:S(2)}) collective-permute-start(bf16[224,896]{1,0:T(8,128)(2,1)S(1)} %collective-permute-done.8.refs_5_), channel_id=1, source_target_pairs={{0,2},{2,0},{4,6},{6,4},{8,10},{10,8},{12,14},{14,12},{16,18},{18,... | collective-permute-start | bytes 1204232 | tf_op jit(solution)/shard_map/ppermute | solution.py:36
  39.0 11.7 %collective-permute-start.9 = (bf16[224,896]{1,0:T(8,128)(2,1)S(1)}, bf16[224,896]{1,0:T(8,128)(2,1)S(1)}, u32[]{:S(2)}, u32[]{:S(2)}) collective-permute-start(bf16[224,896]{1,0:T(8,128)(2,1)S(1)} %collective-permute-done.7.refs_4_), channel_id=1, source_target_pairs={{0,4},{2,6},{8,0},{10,2},{16,8},{18,10},{24,16},{26,18},{28,24},{3... | collective-permute-start | bytes 1204232 | tf_op jit(solution)/shard_map/ppermute | solution.py:126
  40.5 11.4 %collective-permute-start.10 = (bf16[224,896]{1,0:T(8,128)(2,1)S(1)}, bf16[224,896]{1,0:T(8,128)(2,1)S(1)}, u32[]{:S(2)}, u32[]{:S(2)}) collective-permute-start(bf16[224,896]{1,0:T(8,128)(2,1)S(1)} %collective-permute-done.8.refs_5_), channel_id=1, source_target_pairs={{0,8},{2,10},{8,16},{10,18},{16,24},{18,26},{24,28},{26,30},{28,20... | collective-permute-start | bytes 1204232 | tf_op jit(solution)/shard_map/ppermute | solution.py:126
  41.7 10.2 %collective-permute-start.16 = (bf16[256,448]{1,0:T(8,128)(2,1)S(1)}, bf16[256,448]{1,0:T(8,128)(2,1)S(1)}, u32[]{:S(2)}, u32[]{:S(2)}) collective-permute-start(bf16[256,448]{1,0:T(8,128)(2,1)S(1)} %shard_map.47), channel_id=1, source_target_pairs={{0,1},{1,0},{2,3},{3,2},{4,5},{5,4},{6,7},{7,6},{8,9},{9,8},{10,11... | collective-permute-start | bytes 688136 | tf_op jit(solution)/shard_map/ppermute | solution.py:256
  51.9 6.4 %collective-permute-start.17 = (bf16[112,896]{1,0:T(8,128)(2,1)S(1)}, bf16[112,896]{1,0:T(8,128)(2,1)S(1)}, u32[]{:S(2)}, u32[]{:S(2)}) collective-permute-start(bf16[112,896]{1,0:T(8,128)(2,1)S(1)} %slice.6), channel_id=1, source_target_pairs={{0,4},{2,6},{8,0},{10,2},{16,8},{18,10},{24,16},{26,18},{28,24},{3... | collective-permute-start | bytes 602120 | tf_op jit(solution)/shard_map/ppermute | solution.py:126
  52.8 6.1 %collective-permute-start.18 = (bf16[112,896]{1,0:T(8,128)(2,1)S(1)}, bf16[112,896]{1,0:T(8,128)(2,1)S(1)}, u32[]{:S(2)}, u32[]{:S(2)}) collective-permute-start(bf16[112,896]{1,0:T(8,128)(2,1)S(1)} %slice.7), channel_id=1, source_target_pairs={{0,8},{2,10},{8,16},{10,18},{16,24},{18,26},{24,28},{26,30},{28,20... | collective-permute-start | bytes 602120 | tf_op jit(solution)/shard_map/ppermute | solution.py:126
  54.1 4.9 %collective-permute-start.19 = (bf16[224,896]{1,0:T(8,128)(2,1)S(1)}, bf16[224,896]{1,0:T(8,128)(2,1)S(1)}, u32[]{:S(2)}, u32[]{:S(2)}) collective-permute-start(bf16[224,896]{1,0:T(8,128)(2,1)S(1)} %collective-permute-done.9.refs_6_), channel_id=1, source_target_pairs={{0,2},{2,0},{4,6},{6,4},{8,10},{10,8},{12,14},{14,12},{16,18},{18,... | collective-permute-start | bytes 1204232 | tf_op jit(solution)/shard_map/ppermute | solution.py:36
  54.1 4.9 %collective-permute-start.20 = (bf16[224,896]{1,0:T(8,128)(2,1)S(1)}, bf16[224,896]{1,0:T(8,128)(2,1)S(1)}, u32[]{:S(2)}, u32[]{:S(2)}) collective-permute-start(bf16[224,896]{1,0:T(8,128)(2,1)S(1)} %collective-permute-done.10.refs_7_), channel_id=1, source_target_pairs={{0,2},{2,0},{4,6},{6,4},{8,10},{10,8},{12,14},{14,12},{16,18},{18,... | collective-permute-start | bytes 1204232 | tf_op jit(solution)/shard_map/ppermute | solution.py:36
  58.9 2.7 %collective-permute-start.21 = (bf16[224,896]{1,0:T(8,128)(2,1)S(1)}, bf16[224,896]{1,0:T(8,128)(2,1)S(1)}, u32[]{:S(2)}, u32[]{:S(2)}) collective-permute-start(bf16[224,896]{1,0:T(8,128)(2,1)S(1)} %constant_dynamic-update-slice_fusion.refs_8_), channel_id=1, source_target_pairs={{0,2},{2,0},{4,6},{6,4},{8,10},{10,8},{12,14},{14,12},{16,18},{18,... | collective-permute-start | bytes 1204232 | tf_op jit(solution)/shard_map/ppermute | solution.py:36
  60.0 13.4 %collective-permute-start.22 = (bf16[256,896]{1,0:T(8,128)(2,1)S(1)}, bf16[256,896]{1,0:T(8,128)(2,1)S(1)}, u32[]{:S(2)}, u32[]{:S(2)}) collective-permute-start(bf16[256,896]{1,0:T(8,128)(2,1)S(1)} %shard_map.49), channel_id=1, source_target_pairs={{0,1},{1,0},{2,3},{3,2},{4,5},{5,4},{6,7},{7,6},{8,9},{9,8},{10,11... | collective-permute-start | bytes 1376264 | tf_op jit(solution)/shard_map/ppermute | solution.py:256
  62.1 16.3 %collective-permute-start.23 = (bf16[256,448]{1,0:T(8,128)(2,1)S(1)}, bf16[256,448]{1,0:T(8,128)(2,1)S(1)}, u32[]{:S(2)}, u32[]{:S(2)}) collective-permute-start(bf16[256,448]{1,0:T(8,128)(2,1)S(1)} %shard_map.50), channel_id=1, source_target_pairs={{0,1},{1,0},{2,3},{3,2},{4,5},{5,4},{6,7},{7,6},{8,9},{9,8},{10,11... | collective-permute-start | bytes 688136 | tf_op jit(solution)/shard_map/ppermute | solution.py:256

commit v2 on v1

v2 whole, which is shorter than its diff:
```python
import functools
import math

import jax
import jax.numpy as jnp
from jax import lax
from jax.experimental import pallas as pl
from jax.experimental.pallas import tpu as pltpu
from jax.sharding import PartitionSpec as P

HD = 128
BLK = 256

masked_score = -1e30
vmem_limit = 20 * 2**20
in_vmem = pl.BlockSpec(memory_space=pltpu.VMEM)


def call_kernel(body, out_shape, operands, scratch=()):
    many = isinstance(out_shape, (list, tuple))
    return pl.pallas_call(
        body,
        out_shape=out_shape,
        in_specs=[in_vmem] * len(operands),
        out_specs=[in_vmem] * len(out_shape) if many else in_vmem,
        scratch_shapes=list(scratch),
        compiler_params=pltpu.CompilerParams(vmem_limit_bytes=vmem_limit),
        cost_estimate=pl.CostEstimate(flops=1, bytes_accessed=1, transcendentals=0),
    )(*operands)


def flip(value, mask):
    pairs = [(source, source ^ mask) for source in range(lax.axis_size("seq"))]
    return lax.ppermute(value, "seq", pairs)


def attention_body(blocks, heads, *refs):
    query_ref, block_refs, out_ref = refs[0], refs[1 : 1 + blocks], refs[1 + blocks]
    rank = lax.axis_index("seq")
    inside = jnp.logical_and(rank > 0, rank < lax.axis_size("seq") - 1)
    bias = jnp.where(inside, 0.0, masked_score).astype(jnp.float32)
    scale = math.log2(math.e) / math.sqrt(HD)

    def scores_of(head):
        query = query_ref[:, head * HD : (head + 1) * HD]
        scores = [
            lax.dot_general(
                query, ref[0], (((1,), (1,)), ((), ())), preferred_element_type=jnp.float32
            )
            for ref in block_refs
        ]
        scores[-1] = scores[-1] + bias
        return scores

    scores = scores_of(0)
    for head in range(heads):
        later = scores_of(head + 1) if head + 1 < heads else None
        peak = jnp.max(functools.reduce(jnp.maximum, scores), axis=1, keepdims=True) * scale
        weights = [jnp.exp2(part * scale - peak) for part in scores]
        weight_sum = jnp.sum(functools.reduce(jnp.add, weights), axis=1, keepdims=True)
        numerator = functools.reduce(
            jnp.add,
            [
                jnp.dot(part.astype(jnp.bfloat16), ref[1], preferred_element_type=jnp.float32)
                for part, ref in zip(weights, block_refs)
            ],
        )
        out_ref[:, head * HD : (head + 1) * HD] = (numerator / weight_sum).astype(jnp.bfloat16)
        scores = later


def attend(queries, pieces):
    blocks, width = len(pieces), queries.shape[1]
    return call_kernel(
        functools.partial(attention_body, blocks, width // HD),
        jax.ShapeDtypeStruct(queries.shape, jnp.bfloat16),
        [queries, *pieces],
    )


def exchange_blocks(rows):
    count = lax.axis_size("seq")
    bits = count.bit_length() - 1
    outer = [(i, i + 1) for i in range(1, count - 1, 2)]
    outer = outer + [(j, i) for i, j in outer]
    far = [flip(rows, 1 << bit) for bit in range(bits - 1, 0, -1)]
    rows = after(rows, far[-1])
    return [rows] + far + [flip(rows, 1), lax.ppermute(rows, "seq", outer)]


def after(value, earlier):
    return lax.optimization_barrier((value, earlier))[0]


class Ring:
    def __init__(self):
        self.count = lax.axis_size("seq")
        self.layers = self.count // 4
        self.chips = self.count // 2

    def place(self, index):
        layer = jnp.where(index < self.layers, index, self.chips - 1 - index)
        return layer, (index >= self.layers).astype(jnp.int32)

    def index(self):
        rank = lax.axis_index("seq")
        layer = rank // 4
        return jnp.where(rank // 2 % 2 == 0, layer, self.chips - 1 - layer)

    def shift(self, value, step):
        def rank_of(index):
            index = index % self.chips
            return 4 * index if index < self.layers else 4 * (self.chips - 1 - index) + 2

        pairs = [
            (rank_of(index) + core, rank_of(index + step) + core)
            for index in range(self.chips)
            for core in (0, 1)
        ]
        return lax.ppermute(value, "seq", pairs)

    def offsets(self):
        steps = [0]
        for step in range(1, self.chips // 2):
            steps += [step, -step]
        return steps + [self.chips // 2]

    def side_and_slot(self, offset):
        layer, across = self.place(lax.rem(self.index() + offset + self.chips, self.chips))
        per_side = self.layers // 2
        return layer // per_side, 2 * lax.rem(layer, per_side) + across

    def ranks(self, side, offsets):
        before, answer = jnp.int32(0), []
        for offset in offsets:
            belongs = self.side_and_slot(offset)[0] == side
            answer.append((belongs, before))
            before = before + belongs.astype(jnp.int32)
        return answer


def hold(held, slot, ref):
    step = ref.shape[0]
    held[pl.ds(pl.multiple_of(slot * step, 16), step), :] = ref[...]


def times(weight, rows_ref):
    return lax.dot_general(
        weight, rows_ref[...], (((1,), (1,)), ((), ())), preferred_element_type=jnp.float32
    )


def sent_body(first, width, offsets, *refs):
    (mine_ref, theirs_ref), parts = refs[:2], refs[2 : 2 + len(offsets)]
    to_same_ref, to_other_ref, held = refs[2 + len(offsets) :]
    ranks = Ring().ranks(1 - lax.axis_index("head"), offsets)
    for (belongs, rank), ref in zip(ranks, parts):
        for slot in range(width):

            @pl.when(jnp.logical_and(belongs, rank == first + slot))
            def _():
                hold(held, slot, ref)

    to_same_ref[...] = times(held[...], mine_ref).astype(jnp.bfloat16)
    to_other_ref[...] = times(held[...], theirs_ref).astype(jnp.bfloat16)


def sent(rows, first, width, offsets, parts):
    step, depth = parts[0].shape
    shape = jax.ShapeDtypeStruct((width * step, rows[0].shape[0]), jnp.bfloat16)
    return call_kernel(
        functools.partial(sent_body, first, width, offsets),
        [shape, shape],
        [*rows, *parts[: len(offsets)]],
        scratch=[pltpu.VMEM((width * step, depth), jnp.bfloat16)],
    )


def kept_body(offsets, *refs):
    (mine_ref, theirs_ref), parts = refs[:2], refs[2 : 2 + len(offsets)]
    keep_ref, to_core_ref, held = refs[2 + len(offsets) :]
    ring, head = Ring(), lax.axis_index("head")
    for offset, ref in zip(offsets, parts):
        side, slot = ring.side_and_slot(offset)

        @pl.when(side == head)
        def _():
            hold(held, slot, ref)

    keep_ref[...] = times(held[...], mine_ref)
    to_core_ref[...] = times(held[...], theirs_ref).astype(jnp.bfloat16)


def kept(rows, offsets, parts):
    step, depth = parts[0].shape
    shape = (step * len(offsets) // 2, rows[0].shape[0])
    return call_kernel(
        functools.partial(kept_body, offsets),
        [jax.ShapeDtypeStruct(shape, jnp.float32), jax.ShapeDtypeStruct(shape, jnp.bfloat16)],
        [*rows, *parts],
        scratch=[pltpu.VMEM((shape[0], depth), jnp.bfloat16)],
    )


def total_body(offsets, widths, *refs):
    keep_ref, from_core_ref, received, out_ref, turned = refs[0], refs[1], refs[2:-2], *refs[-2:]
    ring = Ring()
    slots = len(offsets) // 2
    step = keep_ref.shape[0] // slots
    core = lax.axis_index("seq") % 2
    ranks = ring.ranks(lax.axis_index("head"), offsets)
    entry = 0
    for same_ref, other_ref, width in zip(received[0::2], received[1::2], widths):
        for at in range(width):
            slot = jnp.int32(0)
            for offset, (belongs, rank) in zip(offsets, ranks):
                here = jnp.logical_and(belongs, rank == entry)
                slot = jnp.where(here, ring.side_and_slot(offset)[1], slot)
            entry += 1
            rows = pl.ds(pl.multiple_of(slot * step, 16), step)
            there = slice(at * step, (at + 1) * step)
            for where, kept_ref, ref in (
                (core, keep_ref, same_ref),
                (1 - core, from_core_ref, other_ref),
            ):
                both = kept_ref[rows, :].astype(jnp.float32) + ref[there, :].astype(jnp.float32)
                start = pl.multiple_of((2 * slot + where) * step, 16)
                turned[pl.ds(start, step), :] = both.astype(jnp.bfloat16)
    tokens = keep_ref.shape[1]
    row = lax.broadcasted_iota(jnp.int32, (tokens, tokens), 0)
    column = lax.broadcasted_iota(jnp.int32, (tokens, tokens), 1)
    identity = jnp.where(row == column, 1.0, 0.0).astype(jnp.bfloat16)
    out_ref[...] = times(identity, turned).astype(jnp.bfloat16)


def total(keep, from_core, received, widths, offsets):
    columns, rows = keep.shape
    return call_kernel(
        functools.partial(total_body, offsets, widths),
        jax.ShapeDtypeStruct((rows, 2 * columns), jnp.bfloat16),
        [keep, from_core, *received],
        scratch=[pltpu.VMEM((2 * columns, rows), jnp.bfloat16)],
    )


def project_on_ring(queries, kv, out_weight):
    ring = Ring()
    shard = out_weight.T
    half = shard.shape[0] // 2
    count = lax.axis_size("seq")
    offsets, widths = ring.offsets(), (1, 2, 1)

    def both_ways(onward, back):
        return [ring.shift(onward, -1), ring.shift(back, 1)]

    def swap(products):
        same, other = products
        crossed = [(2 * i + h, 2 * (i ^ 1) + 1 - h) for i in range(count) for h in range(2)]
        return [
            lax.ppermute(same, "head", [(0, 1), (1, 0)]),
            lax.ppermute(other, ("seq", "head"), crossed),
        ]

    pair = both_ways(shard, shard)
    parts = [shard, *pair]
    pieces = exchange_blocks(kv)
    pair, pieces[1:] = lax.optimization_barrier((pair, pieces[1:]))
    pair = both_ways(*pair)
    parts += pair
    attended = attend(queries, pieces)
    rows = [attended, flip(attended, 1)]
    first = swap(sent(rows, 0, 1, offsets[:5], parts))
    pair, attended = lax.optimization_barrier((pair, attended))
    rows[0] = attended
    pair = both_ways(*pair)
    parts += pair
    second = swap(sent(rows, 1, 2, offsets[:7], parts))
    pair, first = lax.optimization_barrier((pair, first))
    opposite = both_ways(pair[0][:half], pair[1][half:])
    parts.append(jnp.concatenate(opposite, axis=0))
    parts[-1], second = lax.optimization_barrier((parts[-1], second))
    product = sent(rows, 3, 1, offsets, parts)
    rows[0], product = lax.optimization_barrier((rows[0], product))
    third = swap(product)
    keep, to_core = kept(rows, offsets, parts)
    return total(keep, flip(to_core, 1), [*first, *second, *third], widths, offsets)


def project_gathered(attended, out_weight):
    terms = jnp.dot(
        attended,
        lax.all_gather(out_weight, "seq", axis=1, tiled=True),
        preferred_element_type=jnp.float32,
    )
    return lax.psum_scatter(terms.astype(jnp.bfloat16), "head", scatter_dimension=1, tiled=True)


def local(queries, key_rows, value_rows, out_weight):
    kv = jnp.stack([key_rows, value_rows])
    chips = lax.axis_size("seq") // 2
    if chips == 8 and lax.axis_size("head") == 2 and out_weight.shape[1] % 32 == 0:
        return project_on_ring(queries, kv, out_weight)
    attended = attend(queries, exchange_blocks(kv))
    return project_gathered(attended, out_weight)


def solution(mesh):
    in_specs = (P("seq", "head"), P("seq", "head"), P("seq", "head"), P("head", "seq"))
    out_specs = P("seq", "head")
    return jax.shard_map(local, mesh=mesh, in_specs=in_specs, out_specs=out_specs, check_vma=False)
```

time: 80.1 us -> 72.1 us (0.900)
  waiting for transfers between devices: 45.5 us -> 36.6 us
  starting transfers between devices: 22.9 us -> 24.1 us
    ppermute x8, waiting for transfers between devices: 26.3 us -> 8.83 us  [shift(): return lax.ppermute(value, 'seq', pairs)]
    ppermute x12 -> x6, waiting for transfers between devices: 5.22 us -> 10.2 us  [flip(): return lax.ppermute(value, 'seq', pairs)]
    ppermute x4 -> x7, waiting for transfers between devices: 14 us -> 17.6 us  [the longest x3 12.1 us: swap(): lax.ppermute(same, 'head', [(0, 1), (1, 0)])]
    ppermute x8, starting transfers between devices: 8.81 us -> 11.5 us  [shift(): return lax.ppermute(value, 'seq', pairs)]
    ppermute x12 -> x6, starting transfers between devices: 9.52 us -> 7.15 us  [flip(): return lax.ppermute(value, 'seq', pairs)]
    ppermute x4 -> x7, starting transfers between devices: 4.53 us -> 5.49 us  [the longest x3 4.83 us: swap(): lax.ppermute(same, 'head', [(0, 1), (1, 0)])]
  transfers between devices with their start and end apart: 24 -> 21, of which waited for: 11 -> 15; matrix products, arithmetic and copies ran while one was open for 0% -> 1% of each run, Pallas kernels for 10% -> 8%
where the time goes in v2:
time: 72.1 us; the launch traced here: 71.8 us
  waiting for transfers between devices  36.6 us (51%)
  starting transfers between devices  24.1 us (33%)
  Pallas kernels  9.04 us (13%)
  local copies, waits for them, and re-layouts  1.06 us (1%)
  other arithmetic  0.92 us (1%)
    ppermute x3, waiting for transfers between devices, swap(): lax.ppermute(same, 'head', [(0, 1), (1, 0)])  12.1 us
    ppermute x8, starting transfers between devices, shift(): return lax.ppermute(value, 'seq', pairs)  11.5 us
    ppermute x6, waiting for transfers between devices, flip(): return lax.ppermute(value, 'seq', pairs)  10.2 us
    pallas_call x6, Pallas kernels, call_kernel(): pl.pallas_call(body, out_shape=out_shape, in_specs=[in_vmem] * len(operan...  9.04 us
    ppermute x8, waiting for transfers between devices, shift(): return lax.ppermute(value, 'seq', pairs)  8.83 us
    ppermute x6, starting transfers between devices, flip(): return lax.ppermute(value, 'seq', pairs)  7.15 us
    ppermute x3, waiting for transfers between devices, swap(): lax.ppermute(other, ('seq', 'head'), crossed)  5.42 us
    ppermute x3, starting transfers between devices, swap(): lax.ppermute(same, 'head', [(0, 1), (1, 0)])  4.83 us
  transfers between devices with their start and end apart: 21, of which 15 were waited for; matrix products, arithmetic and copies ran while one was open for 1% of the time, Pallas kernels for 8%

profile of v2, /device:TPU:0, one launch (start us, length us, event | category | flops | bytes accessed | tf_op | source)
XLA Modules:
  0.0 71.8 jit_solution(6331485787753040205)
XLA Ops:
  0.0 3.0 %collective-permute-start.1 = (bf16[224,896]{1,0:T(8,128)(2,1)}, bf16[224,896]{1,0:T(8,128)(2,1)S(1)}, u32[]{:S(2)}, u32[]{:S(2)}) collective-permute-start(bf16[224,896]{1,0:T(8,128)(2,1)} %bitcast.3), channel_id=1, source_target_pairs={{0,8},{2,10},{8,16},{10,18},{16,24},{18,26},{24,28},{26,30},{28,20... | collective-permute-start | bytes 1204232 | tf_op jit(solution)/shard_map/ppermute | solution.py:120
  3.0 0.9 %pad_maximum_fusion.1.refs_1_ = bf16[2,256,128]{2,1,0:T(8,128)(2,1)S(1)} fusion(bf16[1,256,128]{2,1,0:T(8,128)(2,1)} %bitcast.9, bf16[1,256,128]{2,1,0:T(8,128)(2,1)} %bitcast.10), kind=kLoop, calls=%fused_computation.1 | loop fusion | flops 65536 | bytes 262144 | tf_op jit(solution)/shard_map/stack | solution.py:299
  3.9 2.0 %collective-permute-start.4 = (bf16[2,256,128]{2,1,0:T(8,128)(2,1)S(1)}, bf16[2,256,128]{2,1,0:T(8,128)(2,1)S(1)}, u32[]{:S(2)}, u32[]{:S(2)}) collective-permute-start(bf16[2,256,128]{2,1,0:T(8,128)(2,1)S(1)} %pad_maximum_fusion.1.refs_1_), channel_id=1, source_target_pairs={{0,4},{2,6},{4,0},{6,2},{8,12},{10,14},{12,8},{14,10},{16,20},{18,... | collective-permute-start | bytes 393224 | tf_op jit(solution)/shard_map/ppermute | solution.py:34
  5.9 1.6 %collective-permute-start.3 = (bf16[2,256,128]{2,1,0:T(8,128)(2,1)S(1)}, bf16[2,256,128]{2,1,0:T(8,128)(2,1)S(1)}, u32[]{:S(2)}, u32[]{:S(2)}) collective-permute-start(bf16[2,256,128]{2,1,0:T(8,128)(2,1)S(1)} %pad_maximum_fusion.1.refs_1_), channel_id=1, source_target_pairs={{0,8},{2,10},{4,12},{6,14},{8,0},{10,2},{12,4},{14,6},{16,24},{18,... | collective-permute-start | bytes 393224 | tf_op jit(solution)/shard_map/ppermute | solution.py:34
  7.5 2.6 %collective-permute-start.2 = (bf16[2,256,128]{2,1,0:T(8,128)(2,1)S(1)}, bf16[2,256,128]{2,1,0:T(8,128)(2,1)S(1)}, u32[]{:S(2)}, u32[]{:S(2)}) collective-permute-start(bf16[2,256,128]{2,1,0:T(8,128)(2,1)S(1)} %pad_maximum_fusion.1.refs_1_), channel_id=1, source_target_pairs={{0,16},{2,18},{4,20},{6,22},{8,24},{10,26},{12,28},{14,30},{16,0},... | collective-permute-start | bytes 393224 | tf_op jit(solution)/shard_map/ppermute | solution.py:34
  10.1 5.1 %collective-permute-done.4.refs_4_ = bf16[2,256,128]{2,1,0:T(8,128)(2,1)S(1)} collective-permute-done((bf16[2,256,128]{2,1,0:T(8,128)(2,1)S(1)}, bf16[2,256,128]{2,1,0:T(8,128)(2,1)S(1)}, u32[]{:S(2)}, u32[]{:S(2)}) %collective-permute-start.4) | collective-permute-done | bytes 131104 | tf_op jit(solution)/shard_map/ppermute | solution.py:34
  15.2 0.7 collective-permute-start.6
  15.9 3.7 %collective-permute-done.3.refs_3_ = bf16[2,256,128]{2,1,0:T(8,128)(2,1)S(1)} collective-permute-done((bf16[2,256,128]{2,1,0:T(8,128)(2,1)S(1)}, bf16[2,256,128]{2,1,0:T(8,128)(2,1)S(1)}, u32[]{:S(2)}, u32[]{:S(2)}) %collective-permute-start.3) | collective-permute-done | bytes 131104 | tf_op jit(solution)/shard_map/ppermute | solution.py:34
  19.6 1.3 %collective-permute-done.5.refs_5_ = bf16[2,256,128]{2,1,0:T(8,128)(2,1)S(1)} collective-permute-done((bf16[2,256,128]{2,1,0:T(8,128)(2,1)S(1)}, bf16[2,256,128]{2,1,0:T(8,128)(2,1)S(1)}, u32[]{:S(2)}, u32[]{:S(2)}) %collective-permute-start.5) | collective-permute-done | bytes 131104 | tf_op jit(solution)/shard_map/ppermute | solution.py:34
  21.0 3.9 %collective-permute-start.7 = (bf16[224,896]{1,0:T(8,128)(2,1)S(1)}, bf16[224,896]{1,0:T(8,128)(2,1)S(1)}, u32[]{:S(2)}, u32[]{:S(2)}) collective-permute-start(bf16[224,896]{1,0:T(8,128)(2,1)S(1)} %collective-permute-done.refs_3_), channel_id=1, source_target_pairs={{0,4},{2,6},{8,0},{10,2},{16,8},{18,10},{24,16},{26,18},{28,24},{3... | collective-permute-start | bytes 1204232 | tf_op jit(solution)/shard_map/ppermute | solution.py:120
  24.9 1.0 %copy-done.1 = bf16[256,896]{1,0:T(8,128)(2,1)S(1)} copy-done((bf16[256,896]{1,0:T(8,128)(2,1)S(1)}, bf16[256,896]{1,0:T(8,128)(2,1)}, u32[]{:S(2)}) %copy-start.1) | copy-done | bytes 458776
  25.9 4.1 %shard_map.46.refs_0_ = bf16[256,896]{1,0:T(8,128)(2,1)S(1)} custom-call(bf16[256,896]{1,0:T(8,128)(2,1)S(1)} %copy-done.1, bf16[2,256,128]{2,1,0:T(8,128)(2,1)S(1)} %pad_maximum_fusion.1.refs_1_, bf16[2,256,128]{2,1,0:T(8,128)(2,1)S(1)} %collective-permute-done.2.refs_2_, bf16[2,256,128]{2,1,0:T(8,128)(2,1)S(1)} %collective-permute-done.3.refs_3_, ...), custom_call_target="tpu_custom_call" | custom-call | flops 1 | bytes 1 | tf_op jit(solution)/shard_map/pallas_call | solution.py:21
  30.1 2.5 %collective-permute-done.7.refs_5_ = bf16[224,896]{1,0:T(8,128)(2,1)S(1)} collective-permute-done((bf16[224,896]{1,0:T(8,128)(2,1)S(1)}, bf16[224,896]{1,0:T(8,128)(2,1)S(1)}, u32[]{:S(2)}, u32[]{:S(2)}) %collective-permute-start.7) | collective-permute-done | bytes 401440 | tf_op jit(solution)/shard_map/ppermute | solution.py:120
  32.6 1.7 %collective-permute-done.8.refs_6_ = bf16[224,896]{1,0:T(8,128)(2,1)S(1)} collective-permute-done((bf16[224,896]{1,0:T(8,128)(2,1)S(1)}, bf16[224,896]{1,0:T(8,128)(2,1)S(1)}, u32[]{:S(2)}, u32[]{:S(2)}) %collective-permute-start.8) | collective-permute-done | bytes 401440 | tf_op jit(solution)/shard_map/ppermute | solution.py:120
  34.3 2.5 %collective-permute-start.10 = (bf16[224,896]{1,0:T(8,128)(2,1)S(1)}, bf16[224,896]{1,0:T(8,128)(2,1)S(1)}, u32[]{:S(2)}, u32[]{:S(2)}) collective-permute-start(bf16[224,896]{1,0:T(8,128)(2,1)S(1)} %collective-permute-done.7.refs_5_), channel_id=1, source_target_pairs={{0,4},{2,6},{8,0},{10,2},{16,8},{18,10},{24,16},{26,18},{28,24},{3... | collective-permute-start | bytes 1204232 | tf_op jit(solution)/shard_map/ppermute | solution.py:120
  37.4 1.6 %collective-permute-start.12 = (bf16[224,256]{1,0:T(8,128)(2,1)S(1)}, bf16[224,256]{1,0:T(8,128)(2,1)S(1)}, u32[]{:S(2)}, u32[]{:S(2)}) collective-permute-start(bf16[224,256]{1,0:T(8,128)(2,1)S(1)} %get-tuple-element.45), channel_id=1, source_target_pairs={{0,1},{1,0},{2,3},{3,2},{4,5},{5,4},{6,7},{7,6},{8,9},{9,8},{10,11... | collective-permute-start | bytes 344072 | tf_op jit(solution)/shard_map/ppermute | solution.py:260
  39.0 3.6 %collective-permute-done.12.refs_2_ = bf16[224,256]{1,0:T(8,128)(2,1)S(1)} collective-permute-done((bf16[224,256]{1,0:T(8,128)(2,1)S(1)}, bf16[224,256]{1,0:T(8,128)(2,1)S(1)}, u32[]{:S(2)}, u32[]{:S(2)}) %collective-permute-start.12) | collective-permute-done | bytes 114720 | tf_op jit(solution)/shard_map/ppermute | solution.py:260
  42.5 1.9 %collective-permute-done.13.refs_3_ = bf16[224,256]{1,0:T(8,128)(2,1)S(1)} collective-permute-done((bf16[224,256]{1,0:T(8,128)(2,1)S(1)}, bf16[224,256]{1,0:T(8,128)(2,1)S(1)}, u32[]{:S(2)}, u32[]{:S(2)}) %collective-permute-start.13) | collective-permute-done | bytes 114720 | tf_op jit(solution)/shard_map/ppermute | solution.py:261
  44.4 0.9 %collective-permute-done.10.refs_7_ = bf16[224,896]{1,0:T(8,128)(2,1)S(1)} collective-permute-done((bf16[224,896]{1,0:T(8,128)(2,1)S(1)}, bf16[224,896]{1,0:T(8,128)(2,1)S(1)}, u32[]{:S(2)}, u32[]{:S(2)}) %collective-permute-start.10) | collective-permute-done | bytes 401440 | tf_op jit(solution)/shard_map/ppermute | solution.py:120
  45.3 2.2 %collective-permute-done.11.refs_8_ = bf16[224,896]{1,0:T(8,128)(2,1)S(1)} collective-permute-done((bf16[224,896]{1,0:T(8,128)(2,1)S(1)}, bf16[224,896]{1,0:T(8,128)(2,1)S(1)}, u32[]{:S(2)}, u32[]{:S(2)}) %collective-permute-start.11) | collective-permute-done | bytes 401440 | tf_op jit(solution)/shard_map/ppermute | solution.py:120
  47.9 1.7 %collective-permute-start.14 = (bf16[112,896]{1,0:T(8,128)(2,1)S(1)}, bf16[112,896]{1,0:T(8,128)(2,1)S(1)}, u32[]{:S(2)}, u32[]{:S(2)}) collective-permute-start(bf16[112,896]{1,0:T(8,128)(2,1)S(1)} %slice.6), channel_id=1, source_target_pairs={{0,4},{2,6},{8,0},{10,2},{16,8},{18,10},{24,16},{26,18},{28,24},{3... | collective-permute-start | bytes 602120 | tf_op jit(solution)/shard_map/ppermute | solution.py:120
  49.7 0.7 %shard_map.48 = (bf16[448,256]{1,0:T(8,128)(2,1)S(1)}, bf16[448,256]{1,0:T(8,128)(2,1)S(1)}) custom-call(bf16[256,896]{1,0:T(8,128)(2,1)S(1)} %shard_map.46.refs_0_, bf16[256,896]{1,0:T(8,128)(2,1)S(1)} %collective-permute-done.9.refs_1_, bf16[224,896]{1,0:T(8,128)(2,1)S(1)} %bitcast.6, bf16[224,896]{1,0:T(8,128)(2,1)S(1)} %collective-permute-done.refs_3_, ...), custom_call_target="tpu_custom_call" | custom-call | flops 1 | bytes 1 | tf_op jit(solution)/shard_map/pallas_call | solution.py:21
  50.4 1.8 %collective-permute-start.16 = (bf16[448,256]{1,0:T(8,128)(2,1)S(1)}, bf16[448,256]{1,0:T(8,128)(2,1)S(1)}, u32[]{:S(2)}, u32[]{:S(2)}) collective-permute-start(bf16[448,256]{1,0:T(8,128)(2,1)S(1)} %get-tuple-element.49), channel_id=1, source_target_pairs={{0,1},{1,0},{2,3},{3,2},{4,5},{5,4},{6,7},{7,6},{8,9},{9,8},{10,11... | collective-permute-start | bytes 688136 | tf_op jit(solution)/shard_map/ppermute | solution.py:260
  52.2 1.2 %collective-permute-done.15 = bf16[112,896]{1,0:T(8,128)(2,1)S(1)} collective-permute-done((bf16[112,896]{1,0:T(8,128)(2,1)S(1)}, bf16[112,896]{1,0:T(8,128)(2,1)S(1)}, u32[]{:S(2)}, u32[]{:S(2)}) %collective-permute-start.15) | collective-permute-done | bytes 200736 | tf_op jit(solution)/shard_map/ppermute | solution.py:120
  53.7 4.2 %collective-permute-done.16.refs_4_ = bf16[448,256]{1,0:T(8,128)(2,1)S(1)} collective-permute-done((bf16[448,256]{1,0:T(8,128)(2,1)S(1)}, bf16[448,256]{1,0:T(8,128)(2,1)S(1)}, u32[]{:S(2)}, u32[]{:S(2)}) %collective-permute-start.16) | collective-permute-done | bytes 229408 | tf_op jit(solution)/shard_map/ppermute | solution.py:260
  57.9 2.5 %collective-permute-done.17.refs_5_ = bf16[448,256]{1,0:T(8,128)(2,1)S(1)} collective-permute-done((bf16[448,256]{1,0:T(8,128)(2,1)S(1)}, bf16[448,256]{1,0:T(8,128)(2,1)S(1)}, u32[]{:S(2)}, u32[]{:S(2)}) %collective-permute-start.17) | collective-permute-done | bytes 229408 | tf_op jit(solution)/shard_map/ppermute | solution.py:261
  60.9 1.4 %shard_map.50 = (f32[896,256]{1,0:T(8,128)S(1)}, bf16[896,256]{1,0:T(8,128)(2,1)S(1)}) custom-call(bf16[256,896]{1,0:T(8,128)(2,1)S(1)} %shard_map.46.refs_0_, bf16[256,896]{1,0:T(8,128)(2,1)S(1)} %collective-permute-done.9.refs_1_, bf16[224,896]{1,0:T(8,128)(2,1)S(1)} %bitcast.8, bf16[224,896]{1,0:T(8,128)(2,1)S(1)} %collective-permute-done.refs_3_, ...), custom_call_target="tpu_custom_call" | custom-call | flops 1 | bytes 1 | tf_op jit(solution)/shard_map/pallas_call | solution.py:21
  62.3 0.9 %collective-permute-start.18 = (bf16[896,256]{1,0:T(8,128)(2,1)S(1)}, bf16[896,256]{1,0:T(8,128)(2,1)S(1)}, u32[]{:S(2)}, u32[]{:S(2)}) collective-permute-start(bf16[896,256]{1,0:T(8,128)(2,1)S(1)} %get-tuple-element.56), channel_id=1, source_target_pairs={{0,2},{2,0},{4,6},{6,4},{8,10},{10,8},{12,14},{14,12},{16,18},{18,... | collective-permute-start | bytes 1376264 | tf_op jit(solution)/shard_map/ppermute | solution.py:34
  63.2 1.5 %collective-permute-start.19 = (bf16[224,256]{1,0:T(8,128)(2,1)S(1)}, bf16[224,256]{1,0:T(8,128)(2,1)S(1)}, u32[]{:S(2)}, u32[]{:S(2)}) collective-permute-start(bf16[224,256]{1,0:T(8,128)(2,1)S(1)} %get-tuple-element.61), channel_id=1, source_target_pairs={{0,1},{1,0},{2,3},{3,2},{4,5},{5,4},{6,7},{7,6},{8,9},{9,8},{10,11... | collective-permute-start | bytes 344072 | tf_op jit(solution)/shard_map/ppermute | solution.py:260
  64.7 4.3 %collective-permute-done.19.refs_6_ = bf16[224,256]{1,0:T(8,128)(2,1)S(1)} collective-permute-done((bf16[224,256]{1,0:T(8,128)(2,1)S(1)}, bf16[224,256]{1,0:T(8,128)(2,1)S(1)}, u32[]{:S(2)}, u32[]{:S(2)}) %collective-permute-start.19) | collective-permute-done | bytes 114720 | tf_op jit(solution)/shard_map/ppermute | solution.py:260
  69.0 1.1 %collective-permute-done.20.refs_7_ = bf16[224,256]{1,0:T(8,128)(2,1)S(1)} collective-permute-done((bf16[224,256]{1,0:T(8,128)(2,1)S(1)}, bf16[224,256]{1,0:T(8,128)(2,1)S(1)}, u32[]{:S(2)}, u32[]{:S(2)}) %collective-permute-start.20) | collective-permute-done | bytes 114720 | tf_op jit(solution)/shard_map/ppermute | solution.py:261
  70.1 1.7 %shard_map.51 = bf16[256,1792]{1,0:T(8,128)(2,1)} custom-call(f32[896,256]{1,0:T(8,128)S(1)} %get-tuple-element.55.refs_0_, bf16[896,256]{1,0:T(8,128)(2,1)S(1)} %collective-permute-done.18.refs_1_, bf16[224,256]{1,0:T(8,128)(2,1)S(1)} %collective-permute-done.12.refs_2_, bf16[224,256]{1,0:T(8,128)(2,1)S(1)} %collective-permute-done.13.refs_3_, ...), custom_call_target="tpu_custom_call" | custom-call | flops 1 | bytes 1 | tf_op jit(solution)/shard_map/pallas_call | solution.py:21
  (24 shorter events, 1.9 us)
Async XLA Ops:
  0.0 21.0 %collective-permute-start.1 = (bf16[224,896]{1,0:T(8,128)(2,1)}, bf16[224,896]{1,0:T(8,128)(2,1)S(1)}, u32[]{:S(2)}, u32[]{:S(2)}) collective-permute-start(bf16[224,896]{1,0:T(8,128)(2,1)} %bitcast.3), channel_id=1, source_target_pairs={{0,8},{2,10},{8,16},{10,18},{16,24},{18,26},{24,28},{26,30},{28,20... | collective-permute-start | bytes 1204232 | tf_op jit(solution)/shard_map/ppermute | solution.py:120
  3.0 17.9 %collective-permute-start = (bf16[224,896]{1,0:T(8,128)(2,1)}, bf16[224,896]{1,0:T(8,128)(2,1)S(1)}, u32[]{:S(2)}, u32[]{:S(2)}) collective-permute-start(bf16[224,896]{1,0:T(8,128)(2,1)} %bitcast.4), channel_id=1, source_target_pairs={{0,4},{2,6},{8,0},{10,2},{16,8},{18,10},{24,16},{26,18},{28,24},{3... | collective-permute-start | bytes 1204232 | tf_op jit(solution)/shard_map/ppermute | solution.py:120
  3.9 32.9 %copy-start = (bf16[896,224]{0,1:T(8,128)(2,1)S(1)}, bf16[896,224]{0,1:T(8,128)(2,1)}, u32[]{:S(2)}) copy-start(bf16[896,224]{0,1:T(8,128)(2,1)} %param.7) | copy-start | bytes 1204228
  3.9 11.3 %collective-permute-start.4 = (bf16[2,256,128]{2,1,0:T(8,128)(2,1)S(1)}, bf16[2,256,128]{2,1,0:T(8,128)(2,1)S(1)}, u32[]{:S(2)}, u32[]{:S(2)}) collective-permute-start(bf16[2,256,128]{2,1,0:T(8,128)(2,1)S(1)} %pad_maximum_fusion.1.refs_1_), channel_id=1, source_target_pairs={{0,4},{2,6},{4,0},{6,2},{8,12},{10,14},{12,8},{14,10},{16,20},{18,... | collective-permute-start | bytes 393224 | tf_op jit(solution)/shard_map/ppermute | solution.py:34
  5.9 13.7 %collective-permute-start.3 = (bf16[2,256,128]{2,1,0:T(8,128)(2,1)S(1)}, bf16[2,256,128]{2,1,0:T(8,128)(2,1)S(1)}, u32[]{:S(2)}, u32[]{:S(2)}) collective-permute-start(bf16[2,256,128]{2,1,0:T(8,128)(2,1)S(1)} %pad_maximum_fusion.1.refs_1_), channel_id=1, source_target_pairs={{0,8},{2,10},{4,12},{6,14},{8,0},{10,2},{12,4},{14,6},{16,24},{18,... | collective-permute-start | bytes 393224 | tf_op jit(solution)/shard_map/ppermute | solution.py:34
  7.5 12.1 %collective-permute-start.2 = (bf16[2,256,128]{2,1,0:T(8,128)(2,1)S(1)}, bf16[2,256,128]{2,1,0:T(8,128)(2,1)S(1)}, u32[]{:S(2)}, u32[]{:S(2)}) collective-permute-start(bf16[2,256,128]{2,1,0:T(8,128)(2,1)S(1)} %pad_maximum_fusion.1.refs_1_), channel_id=1, source_target_pairs={{0,16},{2,18},{4,20},{6,22},{8,24},{10,26},{12,28},{14,30},{16,0},... | collective-permute-start | bytes 393224 | tf_op jit(solution)/shard_map/ppermute | solution.py:34
  15.2 4.4 %collective-permute-start.6 = (bf16[2,256,128]{2,1,0:T(8,128)(2,1)S(1)}, bf16[2,256,128]{2,1,0:T(8,128)(2,1)S(1)}, u32[]{:S(2)}, u32[]{:S(2)}) collective-permute-start(bf16[2,256,128]{2,1,0:T(8,128)(2,1)S(1)} %pad_maximum_fusion.1.refs_1_), channel_id=1, source_target_pairs={{2,4},{6,8},{10,12},{14,16},{18,20},{22,24},{26,28},{4,2},{8,6},{1... | collective-permute-start | bytes 393224 | tf_op jit(solution)/shard_map/ppermute | solution.py:88
  19.6 1.3 %collective-permute-start.5 = (bf16[2,256,128]{2,1,0:T(8,128)(2,1)S(1)}, bf16[2,256,128]{2,1,0:T(8,128)(2,1)S(1)}, u32[]{:S(2)}, u32[]{:S(2)}) collective-permute-start(bf16[2,256,128]{2,1,0:T(8,128)(2,1)S(1)} %pad_maximum_fusion.1.refs_1_), channel_id=1, source_target_pairs={{0,2},{2,0},{4,6},{6,4},{8,10},{10,8},{12,14},{14,12},{16,18},{18,... | collective-permute-start | bytes 393224 | tf_op jit(solution)/shard_map/ppermute | solution.py:34
  21.0 11.7 %collective-permute-start.7 = (bf16[224,896]{1,0:T(8,128)(2,1)S(1)}, bf16[224,896]{1,0:T(8,128)(2,1)S(1)}, u32[]{:S(2)}, u32[]{:S(2)}) collective-permute-start(bf16[224,896]{1,0:T(8,128)(2,1)S(1)} %collective-permute-done.refs_3_), channel_id=1, source_target_pairs={{0,4},{2,6},{8,0},{10,2},{16,8},{18,10},{24,16},{26,18},{28,24},{3... | collective-permute-start | bytes 1204232 | tf_op jit(solution)/shard_map/ppermute | solution.py:120
  24.9 9.5 %collective-permute-start.8 = (bf16[224,896]{1,0:T(8,128)(2,1)S(1)}, bf16[224,896]{1,0:T(8,128)(2,1)S(1)}, u32[]{:S(2)}, u32[]{:S(2)}) collective-permute-start(bf16[224,896]{1,0:T(8,128)(2,1)S(1)} %collective-permute-done.1.refs_4_), channel_id=1, source_target_pairs={{0,8},{2,10},{8,16},{10,18},{16,24},{18,26},{24,28},{26,30},{28,20... | collective-permute-start | bytes 1204232 | tf_op jit(solution)/shard_map/ppermute | solution.py:120
  24.9 1.0 %copy-start.1 = (bf16[256,896]{1,0:T(8,128)(2,1)S(1)}, bf16[256,896]{1,0:T(8,128)(2,1)}, u32[]{:S(2)}) copy-start(bf16[256,896]{1,0:T(8,128)(2,1)} %refs_0_.1) | copy-start | bytes 1376260
  30.0 6.8 %collective-permute-start.9 = (bf16[256,896]{1,0:T(8,128)(2,1)S(1)}, bf16[256,896]{1,0:T(8,128)(2,1)S(1)}, u32[]{:S(2)}, u32[]{:S(2)}) collective-permute-start(bf16[256,896]{1,0:T(8,128)(2,1)S(1)} %shard_map.46.refs_0_), channel_id=1, source_target_pairs={{0,2},{2,0},{4,6},{6,4},{8,10},{10,8},{12,14},{14,12},{16,18},{18,... | collective-permute-start | bytes 1376264 | tf_op jit(solution)/shard_map/ppermute | solution.py:34
  34.3 11.0 %collective-permute-start.10 = (bf16[224,896]{1,0:T(8,128)(2,1)S(1)}, bf16[224,896]{1,0:T(8,128)(2,1)S(1)}, u32[]{:S(2)}, u32[]{:S(2)}) collective-permute-start(bf16[224,896]{1,0:T(8,128)(2,1)S(1)} %collective-permute-done.7.refs_5_), channel_id=1, source_target_pairs={{0,4},{2,6},{8,0},{10,2},{16,8},{18,10},{24,16},{26,18},{28,24},{3... | collective-permute-start | bytes 1204232 | tf_op jit(solution)/shard_map/ppermute | solution.py:120
  36.8 10.7 %collective-permute-start.11 = (bf16[224,896]{1,0:T(8,128)(2,1)S(1)}, bf16[224,896]{1,0:T(8,128)(2,1)S(1)}, u32[]{:S(2)}, u32[]{:S(2)}) collective-permute-start(bf16[224,896]{1,0:T(8,128)(2,1)S(1)} %collective-permute-done.8.refs_6_), channel_id=1, source_target_pairs={{0,8},{2,10},{8,16},{10,18},{16,24},{18,26},{24,28},{26,30},{28,20... | collective-permute-start | bytes 1204232 | tf_op jit(solution)/shard_map/ppermute | solution.py:120
  37.4 5.1 %collective-permute-start.12 = (bf16[224,256]{1,0:T(8,128)(2,1)S(1)}, bf16[224,256]{1,0:T(8,128)(2,1)S(1)}, u32[]{:S(2)}, u32[]{:S(2)}) collective-permute-start(bf16[224,256]{1,0:T(8,128)(2,1)S(1)} %get-tuple-element.45), channel_id=1, source_target_pairs={{0,1},{1,0},{2,3},{3,2},{4,5},{5,4},{6,7},{7,6},{8,9},{9,8},{10,11... | collective-permute-start | bytes 344072 | tf_op jit(solution)/shard_map/ppermute | solution.py:260
  39.0 5.4 %collective-permute-start.13 = (bf16[224,256]{1,0:T(8,128)(2,1)S(1)}, bf16[224,256]{1,0:T(8,128)(2,1)S(1)}, u32[]{:S(2)}, u32[]{:S(2)}) collective-permute-start(bf16[224,256]{1,0:T(8,128)(2,1)S(1)} %get-tuple-element.46), channel_id=1, source_target_pairs={{0,3},{1,2},{2,1},{3,0},{4,7},{5,6},{6,5},{7,4},{8,11},{9,10},{10,... | collective-permute-start | bytes 344072 | tf_op jit(solution)/shard_map/ppermute | solution.py:261
  47.6 5.8 %collective-permute-start.15 = (bf16[112,896]{1,0:T(8,128)(2,1)S(1)}, bf16[112,896]{1,0:T(8,128)(2,1)S(1)}, u32[]{:S(2)}, u32[]{:S(2)}) collective-permute-start(bf16[112,896]{1,0:T(8,128)(2,1)S(1)} %slice.7), channel_id=1, source_target_pairs={{0,8},{2,10},{8,16},{10,18},{16,24},{18,26},{24,28},{26,30},{28,20... | collective-permute-start | bytes 602120 | tf_op jit(solution)/shard_map/ppermute | solution.py:120
  47.9 5.7 %collective-permute-start.14 = (bf16[112,896]{1,0:T(8,128)(2,1)S(1)}, bf16[112,896]{1,0:T(8,128)(2,1)S(1)}, u32[]{:S(2)}, u32[]{:S(2)}) collective-permute-start(bf16[112,896]{1,0:T(8,128)(2,1)S(1)} %slice.6), channel_id=1, source_target_pairs={{0,4},{2,6},{8,0},{10,2},{16,8},{18,10},{24,16},{26,18},{28,24},{3... | collective-permute-start | bytes 602120 | tf_op jit(solution)/shard_map/ppermute | solution.py:120
  50.4 7.5 %collective-permute-start.16 = (bf16[448,256]{1,0:T(8,128)(2,1)S(1)}, bf16[448,256]{1,0:T(8,128)(2,1)S(1)}, u32[]{:S(2)}, u32[]{:S(2)}) collective-permute-start(bf16[448,256]{1,0:T(8,128)(2,1)S(1)} %get-tuple-element.49), channel_id=1, source_target_pairs={{0,1},{1,0},{2,3},{3,2},{4,5},{5,4},{6,7},{7,6},{8,9},{9,8},{10,11... | collective-permute-start | bytes 688136 | tf_op jit(solution)/shard_map/ppermute | solution.py:260
  52.2 8.2 %collective-permute-start.17 = (bf16[448,256]{1,0:T(8,128)(2,1)S(1)}, bf16[448,256]{1,0:T(8,128)(2,1)S(1)}, u32[]{:S(2)}, u32[]{:S(2)}) collective-permute-start(bf16[448,256]{1,0:T(8,128)(2,1)S(1)} %get-tuple-element.50), channel_id=1, source_target_pairs={{0,3},{1,2},{2,1},{3,0},{4,7},{5,6},{6,5},{7,4},{8,11},{9,10},{10,... | collective-permute-start | bytes 688136 | tf_op jit(solution)/shard_map/ppermute | solution.py:261
  62.3 7.8 %collective-permute-start.18 = (bf16[896,256]{1,0:T(8,128)(2,1)S(1)}, bf16[896,256]{1,0:T(8,128)(2,1)S(1)}, u32[]{:S(2)}, u32[]{:S(2)}) collective-permute-start(bf16[896,256]{1,0:T(8,128)(2,1)S(1)} %get-tuple-element.56), channel_id=1, source_target_pairs={{0,2},{2,0},{4,6},{6,4},{8,10},{10,8},{12,14},{14,12},{16,18},{18,... | collective-permute-start | bytes 1376264 | tf_op jit(solution)/shard_map/ppermute | solution.py:34
  63.2 5.8 %collective-permute-start.19 = (bf16[224,256]{1,0:T(8,128)(2,1)S(1)}, bf16[224,256]{1,0:T(8,128)(2,1)S(1)}, u32[]{:S(2)}, u32[]{:S(2)}) collective-permute-start(bf16[224,256]{1,0:T(8,128)(2,1)S(1)} %get-tuple-element.61), channel_id=1, source_target_pairs={{0,1},{1,0},{2,3},{3,2},{4,5},{5,4},{6,7},{7,6},{8,9},{9,8},{10,11... | collective-permute-start | bytes 344072 | tf_op jit(solution)/shard_map/ppermute | solution.py:260
  64.7 5.4 %collective-permute-start.20 = (bf16[224,256]{1,0:T(8,128)(2,1)S(1)}, bf16[224,256]{1,0:T(8,128)(2,1)S(1)}, u32[]{:S(2)}, u32[]{:S(2)}) collective-permute-start(bf16[224,256]{1,0:T(8,128)(2,1)S(1)} %get-tuple-element.62), channel_id=1, source_target_pairs={{0,3},{1,2},{2,1},{3,0},{4,7},{5,6},{6,5},{7,4},{8,11},{9,10},{10,... | collective-permute-start | bytes 344072 | tf_op jit(solution)/shard_map/ppermute | solution.py:261

commit v3 on v2

--- a/solution.py
+++ b/solution.py
@@ -78,14 +78,24 @@
     )
 
 
-def exchange_blocks(rows):
+def staged_body(from_ref, to_ref):
+    to_ref[...] = from_ref[...]
+
+
+def staged(value):
+    shape = jax.ShapeDtypeStruct(value.shape, value.dtype)
+    return call_kernel(staged_body, shape, [value])
+
+
+def exchange_blocks(rows, early=()):
     count = lax.axis_size("seq")
     bits = count.bit_length() - 1
     outer = [(i, i + 1) for i in range(1, count - 1, 2)]
     outer = outer + [(j, i) for i, j in outer]
-    far = [flip(rows, 1 << bit) for bit in range(bits - 1, 0, -1)]
-    rows = after(rows, far[-1])
-    return [rows] + far + [flip(rows, 1), lax.ppermute(rows, "seq", outer)]
+    far = [flip(rows, 1 << bit) for bit in range(bits - 1, 1, -1)]
+    beside = lax.ppermute(rows, "seq", outer)
+    rows = after(rows, (far[-1], early))
+    return [rows, flip(rows, 1), flip(rows, 2)] + far + [beside]
 
 
 def after(value, earlier):
@@ -139,9 +149,14 @@
         return answer
 
 
-def hold(held, slot, ref):
-    step = ref.shape[0]
-    held[pl.ds(pl.multiple_of(slot * step, 16), step), :] = ref[...]
+def hold(held, start, refs):
+    for ref in refs:
+        held[pl.ds(pl.multiple_of(start, 16), ref.shape[0]), :] = ref[...]
+        start = start + ref.shape[0]
+
+
+def grouped(refs, offsets):
+    return [refs[at : at + 1] if at < len(offsets) - 1 else refs[at:] for at in range(len(offsets))]
 
 
 def times(weight, rows_ref):
@@ -151,15 +166,16 @@
 
 
 def sent_body(first, width, offsets, *refs):
-    (mine_ref, theirs_ref), parts = refs[:2], refs[2 : 2 + len(offsets)]
-    to_same_ref, to_other_ref, held = refs[2 + len(offsets) :]
+    (mine_ref, theirs_ref), parts = refs[:2], grouped(refs[2:-3], offsets)
+    to_same_ref, to_other_ref, held = refs[-3:]
+    step = held.shape[0] // width
     ranks = Ring().ranks(1 - lax.axis_index("head"), offsets)
-    for (belongs, rank), ref in zip(ranks, parts):
+    for (belongs, rank), part in zip(ranks, parts):
         for slot in range(width):
 
             @pl.when(jnp.logical_and(belongs, rank == first + slot))
             def _():
-                hold(held, slot, ref)
+                hold(held, slot * step, part)
 
     to_same_ref[...] = times(held[...], mine_ref).astype(jnp.bfloat16)
     to_other_ref[...] = times(held[...], theirs_ref).astype(jnp.bfloat16)
@@ -171,45 +187,52 @@
     return call_kernel(
         functools.partial(sent_body, first, width, offsets),
         [shape, shape],
-        [*rows, *parts[: len(offsets)]],
+        [*rows, *parts],
         scratch=[pltpu.VMEM((width * step, depth), jnp.bfloat16)],
     )
 
 
 def kept_body(offsets, *refs):
-    (mine_ref, theirs_ref), parts = refs[:2], refs[2 : 2 + len(offsets)]
-    keep_ref, to_core_ref, held = refs[2 + len(offsets) :]
+    rows_ref, parts, (out_ref, held) = refs[0], grouped(refs[1:-2], offsets), refs[-2:]
+    step = 2 * held.shape[0] // len(offsets)
     ring, head = Ring(), lax.axis_index("head")
-    for offset, ref in zip(offsets, parts):
+    for offset, part in zip(offsets, parts):
         side, slot = ring.side_and_slot(offset)
 
         @pl.when(side == head)
         def _():
-            hold(held, slot, ref)
-
-    keep_ref[...] = times(held[...], mine_ref)
-    to_core_ref[...] = times(held[...], theirs_ref).astype(jnp.bfloat16)
-
-
-def kept(rows, offsets, parts):
+            hold(held, slot * step, part)
+
+    out_ref[...] = times(held[...], rows_ref).astype(out_ref.dtype)
+
+
+def kept(rows, offsets, parts, dtype):
     step, depth = parts[0].shape
-    shape = (step * len(offsets) // 2, rows[0].shape[0])
+    shape = (step * len(offsets) // 2, rows.shape[0])
     return call_kernel(
         functools.partial(kept_body, offsets),
-        [jax.ShapeDtypeStruct(shape, jnp.float32), jax.ShapeDtypeStruct(shape, jnp.bfloat16)],
-        [*rows, *parts],
+        jax.ShapeDtypeStruct(shape, dtype),
+        [rows, *parts],
         scratch=[pltpu.VMEM((shape[0], depth), jnp.bfloat16)],
     )
 
 
-def total_body(offsets, widths, *refs):
-    keep_ref, from_core_ref, received, out_ref, turned = refs[0], refs[1], refs[2:-2], *refs[-2:]
+def total_body(offsets, widths, first, *refs):
     ring = Ring()
+    keep_ref, from_core_ref = refs[:2]
+    (*received, out_ref, turned) = refs[2:]
+    done_ref = received.pop(0) if first else None
     slots = len(offsets) // 2
     step = keep_ref.shape[0] // slots
     core = lax.axis_index("seq") % 2
     ranks = ring.ranks(lax.axis_index("head"), offsets)
-    entry = 0
+    tokens = keep_ref.shape[1]
+    row = lax.broadcasted_iota(jnp.int32, (tokens, tokens), 0)
+    column = lax.broadcasted_iota(jnp.int32, (tokens, tokens), 1)
+    identity = jnp.where(row == column, 1.0, 0.0).astype(jnp.bfloat16)
+    if not first:
+        turned[...] = jnp.zeros(turned.shape, turned.dtype)
+    entry, slot = first, None
     for same_ref, other_ref, width in zip(received[0::2], received[1::2], widths):
         for at in range(width):
             slot = jnp.int32(0)
@@ -224,22 +247,29 @@
                 (1 - core, from_core_ref, other_ref),
             ):
                 both = kept_ref[rows, :].astype(jnp.float32) + ref[there, :].astype(jnp.float32)
-                start = pl.multiple_of((2 * slot + where) * step, 16)
-                turned[pl.ds(start, step), :] = both.astype(jnp.bfloat16)
-    tokens = keep_ref.shape[1]
-    row = lax.broadcasted_iota(jnp.int32, (tokens, tokens), 0)
-    column = lax.broadcasted_iota(jnp.int32, (tokens, tokens), 1)
-    identity = jnp.where(row == column, 1.0, 0.0).astype(jnp.bfloat16)
-    out_ref[...] = times(identity, turned).astype(jnp.bfloat16)
-
-
-def total(keep, from_core, received, widths, offsets):
+                start = where * step if first else (2 * slot + where) * step
+                turned[pl.ds(pl.multiple_of(start, 16), step), :] = both.astype(jnp.bfloat16)
+    values = times(identity, turned).astype(jnp.bfloat16)
+    if not first:
+        out_ref[...] = values
+        return
+    out_ref[...] = done_ref[...]
+    for at in range(slots):
+
+        @pl.when(slot == at)
+        def _():
+            out_ref[:, 2 * at * step : 2 * (at + 1) * step] = values
+
+
+def total(keep, from_core, received, widths, offsets, done=None):
     columns, rows = keep.shape
+    first = 0 if done is None else len(offsets) // 2 - sum(widths)
+    held = 2 * columns if done is None else 4 * columns // len(offsets)
     return call_kernel(
-        functools.partial(total_body, offsets, widths),
+        functools.partial(total_body, offsets, widths, first),
         jax.ShapeDtypeStruct((rows, 2 * columns), jnp.bfloat16),
-        [keep, from_core, *received],
-        scratch=[pltpu.VMEM((2 * columns, rows), jnp.bfloat16)],
+        [keep, from_core, *([] if done is None else [done]), *received],
+        scratch=[pltpu.VMEM((held, rows), jnp.bfloat16)],
     )
 
 
@@ -263,7 +293,8 @@
 
     pair = both_ways(shard, shard)
     parts = [shard, *pair]
-    pieces = exchange_blocks(kv)
+    queries = staged(queries)
+    pieces = exchange_blocks(kv, queries)
     pair, pieces[1:] = lax.optimization_barrier((pair, pieces[1:]))
     pair = both_ways(*pair)
     parts += pair
@@ -274,16 +305,20 @@
     rows[0] = attended
     pair = both_ways(*pair)
     parts += pair
-    second = swap(sent(rows, 1, 2, offsets[:7], parts))
-    pair, first = lax.optimization_barrier((pair, first))
+    product = sent(rows, 1, 2, offsets[:7], parts)
+    pair, first, product = lax.optimization_barrier((pair, first, product))
+    second = swap(product)
     opposite = both_ways(pair[0][:half], pair[1][half:])
-    parts.append(jnp.concatenate(opposite, axis=0))
-    parts[-1], second = lax.optimization_barrier((parts[-1], second))
+    parts += opposite
+    parts[-2:], second = lax.optimization_barrier((parts[-2:], second))
     product = sent(rows, 3, 1, offsets, parts)
-    rows[0], product = lax.optimization_barrier((rows[0], product))
+    rows, product = lax.optimization_barrier((rows, product))
     third = swap(product)
-    keep, to_core = kept(rows, offsets, parts)
-    return total(keep, flip(to_core, 1), [*first, *second, *third], widths, offsets)
+    to_core = kept(rows[1], offsets, parts, jnp.bfloat16)
+    keep = kept(rows[0], offsets, parts, jnp.float32)
+    from_core = flip(to_core, 1)
+    done = total(keep, from_core, [*first, *second], widths[:2], offsets)
+    return total(keep, from_core, third, widths[2:], offsets, done)
 
 
 def project_gathered(attended, out_weight):

time: 72.1 us -> 66.6 us (0.924)
  waiting for transfers between devices: 36.6 us -> 31.3 us
  starting transfers between devices: 24.1 us -> 23.2 us
  Pallas kernels: 9.04 us -> 9.83 us
    ppermute x3, waiting for transfers between devices: 12.1 us -> 2.73 us  [swap(): lax.ppermute(same, 'head', [(0, 1), (1, 0)])]
    ppermute x8, waiting for transfers between devices: 8.83 us -> 16.8 us  [shift(): return lax.ppermute(value, 'seq', pairs)]
    ppermute x3, waiting for transfers between devices: 5.42 us -> 1.85 us  [swap(): lax.ppermute(other, ('seq', 'head'), crossed)]
    ppermute x8, starting transfers between devices: 11.5 us -> 9.21 us  [shift(): return lax.ppermute(value, 'seq', pairs)]
    ppermute x6, starting transfers between devices: 7.15 us -> 8.6 us  [flip(): return lax.ppermute(value, 'seq', pairs)]
    pallas_call x6 -> x9, Pallas kernels: 9.04 us -> 9.83 us  [call_kernel(): pl.pallas_call(body, out_shape=out_shape, in_specs=[in_vmem] * len(operan...]
  transfers between devices with their start and end apart: 21 -> 21, of which waited for: 15 -> 12; matrix products, arithmetic and copies ran while one was open for 1% -> 1% of each run, Pallas kernels for 8% -> 11%
where the time goes in v3:
time: 66.6 us; the launch traced here: 66.3 us
  waiting for transfers between devices  31.3 us (47%)
  starting transfers between devices  23.2 us (35%)
  Pallas kernels  9.83 us (15%)
  local copies, waits for them, and re-layouts  1.06 us (2%)
  other arithmetic  0.88 us (1%)
    ppermute x8, waiting for transfers between devices, shift(): return lax.ppermute(value, 'seq', pairs)  16.8 us
    ppermute x6, waiting for transfers between devices, flip(): return lax.ppermute(value, 'seq', pairs)  9.92 us
    pallas_call x9, Pallas kernels, call_kernel(): pl.pallas_call(body, out_shape=out_shape, in_specs=[in_vmem] * len(operan...  9.83 us
    ppermute x8, starting transfers between devices, shift(): return lax.ppermute(value, 'seq', pairs)  9.21 us
    ppermute x6, starting transfers between devices, flip(): return lax.ppermute(value, 'seq', pairs)  8.6 us
    ppermute x3, starting transfers between devices, swap(): lax.ppermute(same, 'head', [(0, 1), (1, 0)])  4.69 us
    ppermute x3, waiting for transfers between devices, swap(): lax.ppermute(same, 'head', [(0, 1), (1, 0)])  2.73 us
    ppermute x3, waiting for transfers between devices, swap(): lax.ppermute(other, ('seq', 'head'), crossed)  1.85 us
  transfers between devices with their start and end apart: 21, of which 12 were waited for; matrix products, arithmetic and copies ran while one was open for 1% of the time, Pallas kernels for 11%

profile of v3, /device:TPU:0, one launch (start us, length us, event | category | flops | bytes accessed | tf_op | source)
XLA Modules:
  0.0 66.3 jit_solution(16507145637315855676)
XLA Ops:
  0.0 3.0 %collective-permute-start.1 = (bf16[224,896]{1,0:T(8,128)(2,1)}, bf16[224,896]{1,0:T(8,128)(2,1)S(1)}, u32[]{:S(2)}, u32[]{:S(2)}) collective-permute-start(bf16[224,896]{1,0:T(8,128)(2,1)} %bitcast.3), channel_id=1, source_target_pairs={{0,8},{2,10},{8,16},{10,18},{16,24},{18,26},{24,28},{26,30},{28,20... | collective-permute-start | bytes 1204232 | tf_op jit(solution)/shard_map/ppermute | solution.py:130
  3.0 0.9 %pad_maximum_fusion.refs_1_ = bf16[2,256,128]{2,1,0:T(8,128)(2,1)S(1)} fusion(bf16[1,256,128]{2,1,0:T(8,128)(2,1)} %bitcast.10, bf16[1,256,128]{2,1,0:T(8,128)(2,1)} %bitcast.11), kind=kLoop, calls=%fused_computation | loop fusion | flops 65536 | bytes 262144 | tf_op jit(solution)/shard_map/stack | solution.py:334
  3.9 2.1 %collective-permute-start.2 = (bf16[2,256,128]{2,1,0:T(8,128)(2,1)S(1)}, bf16[2,256,128]{2,1,0:T(8,128)(2,1)S(1)}, u32[]{:S(2)}, u32[]{:S(2)}) collective-permute-start(bf16[2,256,128]{2,1,0:T(8,128)(2,1)S(1)} %pad_maximum_fusion.refs_1_), channel_id=1, source_target_pairs={{0,8},{2,10},{4,12},{6,14},{8,0},{10,2},{12,4},{14,6},{16,24},{18,... | collective-permute-start | bytes 393224 | tf_op jit(solution)/shard_map/ppermute | solution.py:34
  6.0 0.7 collective-permute-start.6
  6.7 3.9 %collective-permute-start.5 = (bf16[2,256,128]{2,1,0:T(8,128)(2,1)S(1)}, bf16[2,256,128]{2,1,0:T(8,128)(2,1)S(1)}, u32[]{:S(2)}, u32[]{:S(2)}) collective-permute-start(bf16[2,256,128]{2,1,0:T(8,128)(2,1)S(1)} %pad_maximum_fusion.refs_1_), channel_id=1, source_target_pairs={{0,16},{2,18},{4,20},{6,22},{8,24},{10,26},{12,28},{14,30},{16,0},... | collective-permute-start | bytes 393224 | tf_op jit(solution)/shard_map/ppermute | solution.py:34
  10.6 1.0 %copy-done.1 = bf16[256,896]{1,0:T(8,128)(2,1)S(1)} copy-done((bf16[256,896]{1,0:T(8,128)(2,1)S(1)}, bf16[256,896]{1,0:T(8,128)(2,1)}, u32[]{:S(2)}) %copy-start.1) | copy-done | bytes 458776
  11.6 6.6 %collective-permute-done.2.refs_5_ = bf16[2,256,128]{2,1,0:T(8,128)(2,1)S(1)} collective-permute-done((bf16[2,256,128]{2,1,0:T(8,128)(2,1)S(1)}, bf16[2,256,128]{2,1,0:T(8,128)(2,1)S(1)}, u32[]{:S(2)}, u32[]{:S(2)}) %collective-permute-start.2) | collective-permute-done | bytes 131104 | tf_op jit(solution)/shard_map/ppermute | solution.py:34
  18.2 1.6 %collective-permute-start.4 = (bf16[2,256,128]{2,1,0:T(8,128)(2,1)S(1)}, bf16[2,256,128]{2,1,0:T(8,128)(2,1)S(1)}, u32[]{:S(2)}, u32[]{:S(2)}) collective-permute-start(bf16[2,256,128]{2,1,0:T(8,128)(2,1)S(1)} %pad_maximum_fusion.refs_1_), channel_id=1, source_target_pairs={{0,4},{2,6},{4,0},{6,2},{8,12},{10,14},{12,8},{14,10},{16,20},{18,... | collective-permute-start | bytes 393224 | tf_op jit(solution)/shard_map/ppermute | solution.py:34
  19.8 0.9 %collective-permute-done.5.refs_4_ = bf16[2,256,128]{2,1,0:T(8,128)(2,1)S(1)} collective-permute-done((bf16[2,256,128]{2,1,0:T(8,128)(2,1)S(1)}, bf16[2,256,128]{2,1,0:T(8,128)(2,1)S(1)}, u32[]{:S(2)}, u32[]{:S(2)}) %collective-permute-start.5) | collective-permute-done | bytes 131104 | tf_op jit(solution)/shard_map/ppermute | solution.py:34
  20.7 2.5 %collective-permute-done.4.refs_3_ = bf16[2,256,128]{2,1,0:T(8,128)(2,1)S(1)} collective-permute-done((bf16[2,256,128]{2,1,0:T(8,128)(2,1)S(1)}, bf16[2,256,128]{2,1,0:T(8,128)(2,1)S(1)}, u32[]{:S(2)}, u32[]{:S(2)}) %collective-permute-start.4) | collective-permute-done | bytes 131104 | tf_op jit(solution)/shard_map/ppermute | solution.py:34
  23.2 1.7 %collective-permute-start.7 = (bf16[224,896]{1,0:T(8,128)(2,1)S(1)}, bf16[224,896]{1,0:T(8,128)(2,1)S(1)}, u32[]{:S(2)}, u32[]{:S(2)}) collective-permute-start(bf16[224,896]{1,0:T(8,128)(2,1)S(1)} %collective-permute-done.refs_3_.refs_2_), channel_id=1, source_target_pairs={{0,4},{2,6},{8,0},{10,2},{16,8},{18,10},{24,16},{26,18},{28,24},{3... | collective-permute-start | bytes 1204232 | tf_op jit(solution)/shard_map/ppermute | solution.py:130
  25.3 4.1 %shard_map.47.refs_0_ = bf16[256,896]{1,0:T(8,128)(2,1)S(1)} custom-call(bf16[256,896]{1,0:T(8,128)(2,1)S(1)} %shard_map.46.refs_0_, bf16[2,256,128]{2,1,0:T(8,128)(2,1)S(1)} %pad_maximum_fusion.refs_1_, bf16[2,256,128]{2,1,0:T(8,128)(2,1)S(1)} %collective-permute-done.3.refs_2_, bf16[2,256,128]{2,1,0:T(8,128)(2,1)S(1)} %collective-permute-done.4.refs_3_, ...), custom_call_target="tpu_custom_call" | custom-call | flops 1 | bytes 1 | tf_op jit(solution)/shard_map/pallas_call | solution.py:21
  29.5 3.0 %collective-permute-done.7.refs_5_.refs_4_ = bf16[224,896]{1,0:T(8,128)(2,1)S(1)} collective-permute-done((bf16[224,896]{1,0:T(8,128)(2,1)S(1)}, bf16[224,896]{1,0:T(8,128)(2,1)S(1)}, u32[]{:S(2)}, u32[]{:S(2)}) %collective-permute-start.7) | collective-permute-done | bytes 401440 | tf_op jit(solution)/shard_map/ppermute | solution.py:130
  32.5 2.1 %collective-permute-done.8.refs_6_.refs_5_ = bf16[224,896]{1,0:T(8,128)(2,1)S(1)} collective-permute-done((bf16[224,896]{1,0:T(8,128)(2,1)S(1)}, bf16[224,896]{1,0:T(8,128)(2,1)S(1)}, u32[]{:S(2)}, u32[]{:S(2)}) %collective-permute-start.8) | collective-permute-done | bytes 401440 | tf_op jit(solution)/shard_map/ppermute | solution.py:130
  34.9 1.7 %collective-permute-start.11 = (bf16[224,896]{1,0:T(8,128)(2,1)S(1)}, bf16[224,896]{1,0:T(8,128)(2,1)S(1)}, u32[]{:S(2)}, u32[]{:S(2)}) collective-permute-start(bf16[224,896]{1,0:T(8,128)(2,1)S(1)} %collective-permute-done.8.refs_6_.refs_5_), channel_id=1, source_target_pairs={{0,8},{2,10},{8,16},{10,18},{16,24},{18,26},{24,28},{26,30},{28,20... | collective-permute-start | bytes 1204232 | tf_op jit(solution)/shard_map/ppermute | solution.py:130
  37.1 1.6 %collective-permute-start.12 = (bf16[224,256]{1,0:T(8,128)(2,1)S(1)}, bf16[224,256]{1,0:T(8,128)(2,1)S(1)}, u32[]{:S(2)}, u32[]{:S(2)}) collective-permute-start(bf16[224,256]{1,0:T(8,128)(2,1)S(1)} %get-tuple-element.47), channel_id=1, source_target_pairs={{0,1},{1,0},{2,3},{3,2},{4,5},{5,4},{6,7},{7,6},{8,9},{9,8},{10,11... | collective-permute-start | bytes 344072 | tf_op jit(solution)/shard_map/ppermute | solution.py:290
  38.7 4.7 %collective-permute-done.10.refs_7_.refs_6_ = bf16[224,896]{1,0:T(8,128)(2,1)S(1)} collective-permute-done((bf16[224,896]{1,0:T(8,128)(2,1)S(1)}, bf16[224,896]{1,0:T(8,128)(2,1)S(1)}, u32[]{:S(2)}, u32[]{:S(2)}) %collective-permute-start.10) | collective-permute-done | bytes 401440 | tf_op jit(solution)/shard_map/ppermute | solution.py:130
  43.7 0.7 %shard_map.49 = (bf16[448,256]{1,0:T(8,128)(2,1)S(1)}, bf16[448,256]{1,0:T(8,128)(2,1)S(1)}) custom-call(bf16[256,896]{1,0:T(8,128)(2,1)S(1)} %shard_map.47.refs_0_, bf16[256,896]{1,0:T(8,128)(2,1)S(1)} %collective-permute-done.9.refs_1_.refs_0_, bf16[224,896]{1,0:T(8,128)(2,1)S(1)} %bitcast.6, bf16[224,896]{1,0:T(8,128)(2,1)S(1)} %collective-permute-done.refs_3_.refs_2_, ...), custom_call_target="tpu_custom_call" | custom-call | flops 1 | bytes 1 | tf_op jit(solution)/shard_map/pallas_call | solution.py:21
  44.5 1.6 %collective-permute-start.16 = (bf16[448,256]{1,0:T(8,128)(2,1)S(1)}, bf16[448,256]{1,0:T(8,128)(2,1)S(1)}, u32[]{:S(2)}, u32[]{:S(2)}) collective-permute-start(bf16[448,256]{1,0:T(8,128)(2,1)S(1)} %get-tuple-element.53), channel_id=1, source_target_pairs={{0,1},{1,0},{2,3},{3,2},{4,5},{5,4},{6,7},{7,6},{8,9},{9,8},{10,11... | collective-permute-start | bytes 688136 | tf_op jit(solution)/shard_map/ppermute | solution.py:290
  46.2 1.5 %collective-permute-start.15 = (bf16[112,896]{1,0:T(8,128)(2,1)S(1)}, bf16[112,896]{1,0:T(8,128)(2,1)S(1)}, u32[]{:S(2)}, u32[]{:S(2)}) collective-permute-start(bf16[112,896]{1,0:T(8,128)(2,1)S(1)} %slice.7), channel_id=1, source_target_pairs={{0,8},{2,10},{8,16},{10,18},{16,24},{18,26},{24,28},{26,30},{28,20... | collective-permute-start | bytes 602120 | tf_op jit(solution)/shard_map/ppermute | solution.py:130
  47.7 0.6 collective-permute-start.14
  48.2 5.4 %collective-permute-done.15.refs_10_.refs_9_ = bf16[112,896]{1,0:T(8,128)(2,1)S(1)} collective-permute-done((bf16[112,896]{1,0:T(8,128)(2,1)S(1)}, bf16[112,896]{1,0:T(8,128)(2,1)S(1)}, u32[]{:S(2)}, u32[]{:S(2)}) %collective-permute-start.15) | collective-permute-done | bytes 200736 | tf_op jit(solution)/shard_map/ppermute | solution.py:130
  53.7 1.2 %collective-permute-done.14.refs_9_.refs_8_ = bf16[112,896]{1,0:T(8,128)(2,1)S(1)} collective-permute-done((bf16[112,896]{1,0:T(8,128)(2,1)S(1)}, bf16[112,896]{1,0:T(8,128)(2,1)S(1)}, u32[]{:S(2)}, u32[]{:S(2)}) %collective-permute-start.14) | collective-permute-done | bytes 200736 | tf_op jit(solution)/shard_map/ppermute | solution.py:130
  54.9 0.8 %collective-permute-done.17.refs_5_ = bf16[448,256]{1,0:T(8,128)(2,1)S(1)} collective-permute-done((bf16[448,256]{1,0:T(8,128)(2,1)S(1)}, bf16[448,256]{1,0:T(8,128)(2,1)S(1)}, u32[]{:S(2)}, u32[]{:S(2)}) %collective-permute-start.17) | collective-permute-done | bytes 229408 | tf_op jit(solution)/shard_map/ppermute | solution.py:291
  56.2 0.9 %shard_map.52 = bf16[896,256]{1,0:T(8,128)(2,1)S(1)} custom-call(bf16[256,896]{1,0:T(8,128)(2,1)S(1)} %collective-permute-done.9.refs_1_.refs_0_, bf16[224,896]{1,0:T(8,128)(2,1)S(1)} %bitcast.8, bf16[224,896]{1,0:T(8,128)(2,1)S(1)} %collective-permute-done.refs_3_.refs_2_, bf16[224,896]{1,0:T(8,128)(2,1)S(1)} %collective-permute-done.1.refs_4_.refs_3_, ...), custom_call_target="tpu_custom_call" | custom-call | flops 1 | bytes 1 | tf_op jit(solution)/shard_map/pallas_call | solution.py:21
  57.1 0.9 %collective-permute-start.18 = (bf16[896,256]{1,0:T(8,128)(2,1)S(1)}, bf16[896,256]{1,0:T(8,128)(2,1)S(1)}, u32[]{:S(2)}, u32[]{:S(2)}) collective-permute-start(bf16[896,256]{1,0:T(8,128)(2,1)S(1)} %shard_map.52), channel_id=1, source_target_pairs={{0,2},{2,0},{4,6},{6,4},{8,10},{10,8},{12,14},{14,12},{16,18},{18,... | collective-permute-start | bytes 1376264 | tf_op jit(solution)/shard_map/ppermute | solution.py:34
  58.1 1.5 %collective-permute-start.19 = (bf16[224,256]{1,0:T(8,128)(2,1)S(1)}, bf16[224,256]{1,0:T(8,128)(2,1)S(1)}, u32[]{:S(2)}, u32[]{:S(2)}) collective-permute-start(bf16[224,256]{1,0:T(8,128)(2,1)S(1)} %get-tuple-element.65), channel_id=1, source_target_pairs={{0,1},{1,0},{2,3},{3,2},{4,5},{5,4},{6,7},{7,6},{8,9},{9,8},{10,11... | collective-permute-start | bytes 344072 | tf_op jit(solution)/shard_map/ppermute | solution.py:290
  59.5 0.9 %shard_map.51.refs_0_ = f32[896,256]{1,0:T(8,128)S(1)} custom-call(bf16[256,896]{1,0:T(8,128)(2,1)S(1)} %shard_map.47.refs_0_, bf16[224,896]{1,0:T(8,128)(2,1)S(1)} %bitcast.9, bf16[224,896]{1,0:T(8,128)(2,1)S(1)} %collective-permute-done.refs_3_.refs_2_, bf16[224,896]{1,0:T(8,128)(2,1)S(1)} %collective-permute-done.1.refs_4_.refs_3_, ...), custom_call_target="tpu_custom_call" | custom-call | flops 1 | bytes 1 | tf_op jit(solution)/shard_map/pallas_call | solution.py:21
  60.4 0.7 %shard_map.53.refs_2_ = bf16[256,1792]{1,0:T(8,128)(2,1)S(1)} custom-call(f32[896,256]{1,0:T(8,128)S(1)} %shard_map.51.refs_0_, bf16[896,256]{1,0:T(8,128)(2,1)S(1)} %collective-permute-done.18.refs_1_, bf16[224,256]{1,0:T(8,128)(2,1)S(1)} %collective-permute-done.12.refs_2_, bf16[224,256]{1,0:T(8,128)(2,1)S(1)} %collective-permute-done.13.refs_3_, ...), custom_call_target="tpu_custom_call" | custom-call | flops 1 | bytes 1 | tf_op jit(solution)/shard_map/pallas_call | solution.py:21
  61.2 2.7 %collective-permute-done.19.refs_3_ = bf16[224,256]{1,0:T(8,128)(2,1)S(1)} collective-permute-done((bf16[224,256]{1,0:T(8,128)(2,1)S(1)}, bf16[224,256]{1,0:T(8,128)(2,1)S(1)}, u32[]{:S(2)}, u32[]{:S(2)}) %collective-permute-start.19) | collective-permute-done | bytes 114720 | tf_op jit(solution)/shard_map/ppermute | solution.py:290
  63.9 1.1 %collective-permute-done.20.refs_4_ = bf16[224,256]{1,0:T(8,128)(2,1)S(1)} collective-permute-done((bf16[224,256]{1,0:T(8,128)(2,1)S(1)}, bf16[224,256]{1,0:T(8,128)(2,1)S(1)}, u32[]{:S(2)}, u32[]{:S(2)}) %collective-permute-start.20) | collective-permute-done | bytes 114720 | tf_op jit(solution)/shard_map/ppermute | solution.py:291
  64.9 1.4 %shard_map.54 = bf16[256,1792]{1,0:T(8,128)(2,1)} custom-call(f32[896,256]{1,0:T(8,128)S(1)} %shard_map.51.refs_0_, bf16[896,256]{1,0:T(8,128)(2,1)S(1)} %collective-permute-done.18.refs_1_, bf16[256,1792]{1,0:T(8,128)(2,1)S(1)} %shard_map.53.refs_2_, bf16[224,256]{1,0:T(8,128)(2,1)S(1)} %collective-permute-done.19.refs_3_, ...), custom_call_target="tpu_custom_call" | custom-call | flops 1 | bytes 1 | tf_op jit(solution)/shard_map/pallas_call | solution.py:21
  (26 shorter events, 2.2 us)
Async XLA Ops:
  0.0 23.2 %collective-permute-start.1 = (bf16[224,896]{1,0:T(8,128)(2,1)}, bf16[224,896]{1,0:T(8,128)(2,1)S(1)}, u32[]{:S(2)}, u32[]{:S(2)}) collective-permute-start(bf16[224,896]{1,0:T(8,128)(2,1)} %bitcast.3), channel_id=1, source_target_pairs={{0,8},{2,10},{8,16},{10,18},{16,24},{18,26},{24,28},{26,30},{28,20... | collective-permute-start | bytes 1204232 | tf_op jit(solution)/shard_map/ppermute | solution.py:130
  3.0 20.2 %collective-permute-start = (bf16[224,896]{1,0:T(8,128)(2,1)}, bf16[224,896]{1,0:T(8,128)(2,1)S(1)}, u32[]{:S(2)}, u32[]{:S(2)}) collective-permute-start(bf16[224,896]{1,0:T(8,128)(2,1)} %bitcast.4), channel_id=1, source_target_pairs={{0,4},{2,6},{8,0},{10,2},{16,8},{18,10},{24,16},{26,18},{28,24},{3... | collective-permute-start | bytes 1204232 | tf_op jit(solution)/shard_map/ppermute | solution.py:130
  3.9 14.3 %collective-permute-start.2 = (bf16[2,256,128]{2,1,0:T(8,128)(2,1)S(1)}, bf16[2,256,128]{2,1,0:T(8,128)(2,1)S(1)}, u32[]{:S(2)}, u32[]{:S(2)}) collective-permute-start(bf16[2,256,128]{2,1,0:T(8,128)(2,1)S(1)} %pad_maximum_fusion.refs_1_), channel_id=1, source_target_pairs={{0,8},{2,10},{4,12},{6,14},{8,0},{10,2},{12,4},{14,6},{16,24},{18,... | collective-permute-start | bytes 393224 | tf_op jit(solution)/shard_map/ppermute | solution.py:34
  6.0 13.8 %collective-permute-start.6 = (bf16[2,256,128]{2,1,0:T(8,128)(2,1)S(1)}, bf16[2,256,128]{2,1,0:T(8,128)(2,1)S(1)}, u32[]{:S(2)}, u32[]{:S(2)}) collective-permute-start(bf16[2,256,128]{2,1,0:T(8,128)(2,1)S(1)} %pad_maximum_fusion.refs_1_), channel_id=1, source_target_pairs={{2,4},{6,8},{10,12},{14,16},{18,20},{22,24},{26,28},{4,2},{8,6},{1... | collective-permute-start | bytes 393224 | tf_op jit(solution)/shard_map/ppermute | solution.py:96
  6.7 14.0 %collective-permute-start.5 = (bf16[2,256,128]{2,1,0:T(8,128)(2,1)S(1)}, bf16[2,256,128]{2,1,0:T(8,128)(2,1)S(1)}, u32[]{:S(2)}, u32[]{:S(2)}) collective-permute-start(bf16[2,256,128]{2,1,0:T(8,128)(2,1)S(1)} %pad_maximum_fusion.refs_1_), channel_id=1, source_target_pairs={{0,16},{2,18},{4,20},{6,22},{8,24},{10,26},{12,28},{14,30},{16,0},... | collective-permute-start | bytes 393224 | tf_op jit(solution)/shard_map/ppermute | solution.py:34
  10.6 1.0 %copy-start.1 = (bf16[256,896]{1,0:T(8,128)(2,1)S(1)}, bf16[256,896]{1,0:T(8,128)(2,1)}, u32[]{:S(2)}) copy-start(bf16[256,896]{1,0:T(8,128)(2,1)} %from_ref.1) | copy-start | bytes 1376260
  11.6 25.0 %copy-start = (bf16[896,224]{0,1:T(8,128)(2,1)S(1)}, bf16[896,224]{0,1:T(8,128)(2,1)}, u32[]{:S(2)}) copy-start(bf16[896,224]{0,1:T(8,128)(2,1)} %param.7) | copy-start | bytes 1204228
  18.2 5.0 %collective-permute-start.4 = (bf16[2,256,128]{2,1,0:T(8,128)(2,1)S(1)}, bf16[2,256,128]{2,1,0:T(8,128)(2,1)S(1)}, u32[]{:S(2)}, u32[]{:S(2)}) collective-permute-start(bf16[2,256,128]{2,1,0:T(8,128)(2,1)S(1)} %pad_maximum_fusion.refs_1_), channel_id=1, source_target_pairs={{0,4},{2,6},{4,0},{6,2},{8,12},{10,14},{12,8},{14,10},{16,20},{18,... | collective-permute-start | bytes 393224 | tf_op jit(solution)/shard_map/ppermute | solution.py:34
  19.8 3.4 %collective-permute-start.3 = (bf16[2,256,128]{2,1,0:T(8,128)(2,1)S(1)}, bf16[2,256,128]{2,1,0:T(8,128)(2,1)S(1)}, u32[]{:S(2)}, u32[]{:S(2)}) collective-permute-start(bf16[2,256,128]{2,1,0:T(8,128)(2,1)S(1)} %pad_maximum_fusion.refs_1_), channel_id=1, source_target_pairs={{0,2},{2,0},{4,6},{6,4},{8,10},{10,8},{12,14},{14,12},{16,18},{18,... | collective-permute-start | bytes 393224 | tf_op jit(solution)/shard_map/ppermute | solution.py:34
  23.2 9.3 %collective-permute-start.7 = (bf16[224,896]{1,0:T(8,128)(2,1)S(1)}, bf16[224,896]{1,0:T(8,128)(2,1)S(1)}, u32[]{:S(2)}, u32[]{:S(2)}) collective-permute-start(bf16[224,896]{1,0:T(8,128)(2,1)S(1)} %collective-permute-done.refs_3_.refs_2_), channel_id=1, source_target_pairs={{0,4},{2,6},{8,0},{10,2},{16,8},{18,10},{24,16},{26,18},{28,24},{3... | collective-permute-start | bytes 1204232 | tf_op jit(solution)/shard_map/ppermute | solution.py:130
  24.8 9.8 %collective-permute-start.8 = (bf16[224,896]{1,0:T(8,128)(2,1)S(1)}, bf16[224,896]{1,0:T(8,128)(2,1)S(1)}, u32[]{:S(2)}, u32[]{:S(2)}) collective-permute-start(bf16[224,896]{1,0:T(8,128)(2,1)S(1)} %collective-permute-done.1.refs_4_.refs_3_), channel_id=1, source_target_pairs={{0,8},{2,10},{8,16},{10,18},{16,24},{18,26},{24,28},{26,30},{28,20... | collective-permute-start | bytes 1204232 | tf_op jit(solution)/shard_map/ppermute | solution.py:130
  29.4 7.2 %collective-permute-start.9 = (bf16[256,896]{1,0:T(8,128)(2,1)S(1)}, bf16[256,896]{1,0:T(8,128)(2,1)S(1)}, u32[]{:S(2)}, u32[]{:S(2)}) collective-permute-start(bf16[256,896]{1,0:T(8,128)(2,1)S(1)} %shard_map.47.refs_0_), channel_id=1, source_target_pairs={{0,2},{2,0},{4,6},{6,4},{8,10},{10,8},{12,14},{14,12},{16,18},{18,... | collective-permute-start | bytes 1376264 | tf_op jit(solution)/shard_map/ppermute | solution.py:34
  34.6 8.8 %collective-permute-start.10 = (bf16[224,896]{1,0:T(8,128)(2,1)S(1)}, bf16[224,896]{1,0:T(8,128)(2,1)S(1)}, u32[]{:S(2)}, u32[]{:S(2)}) collective-permute-start(bf16[224,896]{1,0:T(8,128)(2,1)S(1)} %collective-permute-done.7.refs_5_.refs_4_), channel_id=1, source_target_pairs={{0,4},{2,6},{8,0},{10,2},{16,8},{18,10},{24,16},{26,18},{28,24},{3... | collective-permute-start | bytes 1204232 | tf_op jit(solution)/shard_map/ppermute | solution.py:130
  34.9 8.8 %collective-permute-start.11 = (bf16[224,896]{1,0:T(8,128)(2,1)S(1)}, bf16[224,896]{1,0:T(8,128)(2,1)S(1)}, u32[]{:S(2)}, u32[]{:S(2)}) collective-permute-start(bf16[224,896]{1,0:T(8,128)(2,1)S(1)} %collective-permute-done.8.refs_6_.refs_5_), channel_id=1, source_target_pairs={{0,8},{2,10},{8,16},{10,18},{16,24},{18,26},{24,28},{26,30},{28,20... | collective-permute-start | bytes 1204232 | tf_op jit(solution)/shard_map/ppermute | solution.py:130
  37.1 7.3 %collective-permute-start.12 = (bf16[224,256]{1,0:T(8,128)(2,1)S(1)}, bf16[224,256]{1,0:T(8,128)(2,1)S(1)}, u32[]{:S(2)}, u32[]{:S(2)}) collective-permute-start(bf16[224,256]{1,0:T(8,128)(2,1)S(1)} %get-tuple-element.47), channel_id=1, source_target_pairs={{0,1},{1,0},{2,3},{3,2},{4,5},{5,4},{6,7},{7,6},{8,9},{9,8},{10,11... | collective-permute-start | bytes 344072 | tf_op jit(solution)/shard_map/ppermute | solution.py:290
  38.7 5.7 %collective-permute-start.13 = (bf16[224,256]{1,0:T(8,128)(2,1)S(1)}, bf16[224,256]{1,0:T(8,128)(2,1)S(1)}, u32[]{:S(2)}, u32[]{:S(2)}) collective-permute-start(bf16[224,256]{1,0:T(8,128)(2,1)S(1)} %get-tuple-element.48), channel_id=1, source_target_pairs={{0,3},{1,2},{2,1},{3,0},{4,7},{5,6},{6,5},{7,4},{8,11},{9,10},{10,... | collective-permute-start | bytes 344072 | tf_op jit(solution)/shard_map/ppermute | solution.py:291
  44.5 10.4 %collective-permute-start.16 = (bf16[448,256]{1,0:T(8,128)(2,1)S(1)}, bf16[448,256]{1,0:T(8,128)(2,1)S(1)}, u32[]{:S(2)}, u32[]{:S(2)}) collective-permute-start(bf16[448,256]{1,0:T(8,128)(2,1)S(1)} %get-tuple-element.53), channel_id=1, source_target_pairs={{0,1},{1,0},{2,3},{3,2},{4,5},{5,4},{6,7},{7,6},{8,9},{9,8},{10,11... | collective-permute-start | bytes 688136 | tf_op jit(solution)/shard_map/ppermute | solution.py:290
  46.1 9.6 %collective-permute-start.17 = (bf16[448,256]{1,0:T(8,128)(2,1)S(1)}, bf16[448,256]{1,0:T(8,128)(2,1)S(1)}, u32[]{:S(2)}, u32[]{:S(2)}) collective-permute-start(bf16[448,256]{1,0:T(8,128)(2,1)S(1)} %get-tuple-element.54), channel_id=1, source_target_pairs={{0,3},{1,2},{2,1},{3,0},{4,7},{5,6},{6,5},{7,4},{8,11},{9,10},{10,... | collective-permute-start | bytes 688136 | tf_op jit(solution)/shard_map/ppermute | solution.py:291
  46.2 7.5 %collective-permute-start.15 = (bf16[112,896]{1,0:T(8,128)(2,1)S(1)}, bf16[112,896]{1,0:T(8,128)(2,1)S(1)}, u32[]{:S(2)}, u32[]{:S(2)}) collective-permute-start(bf16[112,896]{1,0:T(8,128)(2,1)S(1)} %slice.7), channel_id=1, source_target_pairs={{0,8},{2,10},{8,16},{10,18},{16,24},{18,26},{24,28},{26,30},{28,20... | collective-permute-start | bytes 602120 | tf_op jit(solution)/shard_map/ppermute | solution.py:130
  47.7 7.2 %collective-permute-start.14 = (bf16[112,896]{1,0:T(8,128)(2,1)S(1)}, bf16[112,896]{1,0:T(8,128)(2,1)S(1)}, u32[]{:S(2)}, u32[]{:S(2)}) collective-permute-start(bf16[112,896]{1,0:T(8,128)(2,1)S(1)} %slice.6), channel_id=1, source_target_pairs={{0,4},{2,6},{8,0},{10,2},{16,8},{18,10},{24,16},{26,18},{28,24},{3... | collective-permute-start | bytes 602120 | tf_op jit(solution)/shard_map/ppermute | solution.py:130
  57.1 3.3 %collective-permute-start.18 = (bf16[896,256]{1,0:T(8,128)(2,1)S(1)}, bf16[896,256]{1,0:T(8,128)(2,1)S(1)}, u32[]{:S(2)}, u32[]{:S(2)}) collective-permute-start(bf16[896,256]{1,0:T(8,128)(2,1)S(1)} %shard_map.52), channel_id=1, source_target_pairs={{0,2},{2,0},{4,6},{6,4},{8,10},{10,8},{12,14},{14,12},{16,18},{18,... | collective-permute-start | bytes 1376264 | tf_op jit(solution)/shard_map/ppermute | solution.py:34
  58.1 5.8 %collective-permute-start.19 = (bf16[224,256]{1,0:T(8,128)(2,1)S(1)}, bf16[224,256]{1,0:T(8,128)(2,1)S(1)}, u32[]{:S(2)}, u32[]{:S(2)}) collective-permute-start(bf16[224,256]{1,0:T(8,128)(2,1)S(1)} %get-tuple-element.65), channel_id=1, source_target_pairs={{0,1},{1,0},{2,3},{3,2},{4,5},{5,4},{6,7},{7,6},{8,9},{9,8},{10,11... | collective-permute-start | bytes 344072 | tf_op jit(solution)/shard_map/ppermute | solution.py:290
  59.5 5.4 %collective-permute-start.20 = (bf16[224,256]{1,0:T(8,128)(2,1)S(1)}, bf16[224,256]{1,0:T(8,128)(2,1)S(1)}, u32[]{:S(2)}, u32[]{:S(2)}) collective-permute-start(bf16[224,256]{1,0:T(8,128)(2,1)S(1)} %get-tuple-element.66), channel_id=1, source_target_pairs={{0,3},{1,2},{2,1},{3,0},{4,7},{5,6},{6,5},{7,4},{8,11},{9,10},{10,... | collective-permute-start | bytes 344072 | tf_op jit(solution)/shard_map/ppermute | solution.py:291

commit v4 on v3

--- a/solution.py
+++ b/solution.py
@@ -94,7 +94,7 @@
     outer = outer + [(j, i) for i, j in outer]
     far = [flip(rows, 1 << bit) for bit in range(bits - 1, 1, -1)]
     beside = lax.ppermute(rows, "seq", outer)
-    rows = after(rows, (far[-1], early))
+    rows = after(rows, early)
     return [rows, flip(rows, 1), flip(rows, 2)] + far + [beside]
 
 
@@ -294,19 +294,18 @@
     pair = both_ways(shard, shard)
     parts = [shard, *pair]
     queries = staged(queries)
-    pieces = exchange_blocks(kv, queries)
+    pieces = exchange_blocks(kv, (queries, pair[0]))
     pair, pieces[1:] = lax.optimization_barrier((pair, pieces[1:]))
     pair = both_ways(*pair)
     parts += pair
     attended = attend(queries, pieces)
     rows = [attended, flip(attended, 1)]
     first = swap(sent(rows, 0, 1, offsets[:5], parts))
-    pair, attended = lax.optimization_barrier((pair, attended))
-    rows[0] = attended
+    pair = [after(shard, attended) for shard in pair]
     pair = both_ways(*pair)
     parts += pair
     product = sent(rows, 1, 2, offsets[:7], parts)
-    pair, first, product = lax.optimization_barrier((pair, first, product))
+    pair = [after(shard, (first, product)) for shard in pair]
     second = swap(product)
     opposite = both_ways(pair[0][:half], pair[1][half:])
     parts += opposite

time: 66.6 us -> 63.3 us (0.950)
  waiting for transfers between devices: 31.3 us -> 26.2 us
  starting transfers between devices: 23.2 us -> 24.5 us
    ppermute x6, waiting for transfers between devices: 9.92 us -> 4.22 us  [flip(): return lax.ppermute(value, 'seq', pairs)]
    ppermute x8, starting transfers between devices: 9.21 us -> 11 us  [shift(): return lax.ppermute(value, 'seq', pairs)]
    ppermute x8, waiting for transfers between devices: 16.8 us -> 18.2 us  [shift(): return lax.ppermute(value, 'seq', pairs)]
    ppermute x3, waiting for transfers between devices: 1.85 us -> 1.01 us  [swap(): lax.ppermute(other, ('seq', 'head'), crossed)]
  transfers between devices with their start and end apart: 21 -> 21, of which waited for: 12 -> 9; matrix products, arithmetic and copies ran while one was open for 1% -> 1% of each run, Pallas kernels for 11% -> 11%
where the time goes in v4:
time: 63.3 us; the launch traced here: 62.7 us
  waiting for transfers between devices  26.2 us (41%)
  starting transfers between devices  24.5 us (39%)
  Pallas kernels  9.92 us (16%)
  local copies, waits for them, and re-layouts  1.06 us (2%)
  other arithmetic  0.88 us (1%)
    ppermute x8, waiting for transfers between devices, shift(): return lax.ppermute(value, 'seq', pairs)  18.2 us
    ppermute x8, starting transfers between devices, shift(): return lax.ppermute(value, 'seq', pairs)  11 us
    pallas_call x9, Pallas kernels, call_kernel(): pl.pallas_call(body, out_shape=out_shape, in_specs=[in_vmem] * len(operan...  9.92 us
    ppermute x6, starting transfers between devices, flip(): return lax.ppermute(value, 'seq', pairs)  8.15 us
    ppermute x3, starting transfers between devices, swap(): lax.ppermute(same, 'head', [(0, 1), (1, 0)])  4.67 us
    ppermute x6, waiting for transfers between devices, flip(): return lax.ppermute(value, 'seq', pairs)  4.22 us
    ppermute x3, waiting for transfers between devices, swap(): lax.ppermute(same, 'head', [(0, 1), (1, 0)])  2.76 us
  transfers between devices with their start and end apart: 21, of which 9 were waited for; matrix products, arithmetic and copies ran while one was open for 1% of the time, Pallas kernels for 11%

profile of v4, /device:TPU:0, one launch (start us, length us, event | category | flops | bytes accessed | tf_op | source)
XLA Modules:
  0.0 62.7 jit_solution(349816339310758163)
XLA Ops:
  0.0 2.9 %collective-permute-start = (bf16[224,896]{1,0:T(8,128)(2,1)}, bf16[224,896]{1,0:T(8,128)(2,1)S(1)}, u32[]{:S(2)}, u32[]{:S(2)}) collective-permute-start(bf16[224,896]{1,0:T(8,128)(2,1)} %bitcast.3), channel_id=1, source_target_pairs={{0,4},{2,6},{8,0},{10,2},{16,8},{18,10},{24,16},{26,18},{28,24},{3... | collective-permute-start | bytes 1204232 | tf_op jit(solution)/shard_map/ppermute | solution.py:130
  3.0 0.9 %pad_maximum_fusion.refs_1_ = bf16[2,256,128]{2,1,0:T(8,128)(2,1)S(1)} fusion(bf16[1,256,128]{2,1,0:T(8,128)(2,1)} %bitcast.10, bf16[1,256,128]{2,1,0:T(8,128)(2,1)} %bitcast.11), kind=kLoop, calls=%fused_computation | loop fusion | flops 65536 | bytes 262144 | tf_op jit(solution)/shard_map/stack | solution.py:333
  3.9 0.7 %collective-permute-start.6 = (bf16[2,256,128]{2,1,0:T(8,128)(2,1)S(1)}, bf16[2,256,128]{2,1,0:T(8,128)(2,1)S(1)}, u32[]{:S(2)}, u32[]{:S(2)}) collective-permute-start(bf16[2,256,128]{2,1,0:T(8,128)(2,1)S(1)} %pad_maximum_fusion.refs_1_), channel_id=1, source_target_pairs={{2,4},{6,8},{10,12},{14,16},{18,20},{22,24},{26,28},{4,2},{8,6},{1... | collective-permute-start | bytes 393224 | tf_op jit(solution)/shard_map/ppermute | solution.py:96
  4.6 3.6 %collective-permute-start.5 = (bf16[2,256,128]{2,1,0:T(8,128)(2,1)S(1)}, bf16[2,256,128]{2,1,0:T(8,128)(2,1)S(1)}, u32[]{:S(2)}, u32[]{:S(2)}) collective-permute-start(bf16[2,256,128]{2,1,0:T(8,128)(2,1)S(1)} %pad_maximum_fusion.refs_1_), channel_id=1, source_target_pairs={{0,8},{2,10},{4,12},{6,14},{8,0},{10,2},{12,4},{14,6},{16,24},{18,... | collective-permute-start | bytes 393224 | tf_op jit(solution)/shard_map/ppermute | solution.py:34
  8.2 2.6 %collective-permute-start.4 = (bf16[2,256,128]{2,1,0:T(8,128)(2,1)S(1)}, bf16[2,256,128]{2,1,0:T(8,128)(2,1)S(1)}, u32[]{:S(2)}, u32[]{:S(2)}) collective-permute-start(bf16[2,256,128]{2,1,0:T(8,128)(2,1)S(1)} %pad_maximum_fusion.refs_1_), channel_id=1, source_target_pairs={{0,16},{2,18},{4,20},{6,22},{8,24},{10,26},{12,28},{14,30},{16,0},... | collective-permute-start | bytes 393224 | tf_op jit(solution)/shard_map/ppermute | solution.py:34
  10.8 1.0 %copy-done.1 = bf16[256,896]{1,0:T(8,128)(2,1)S(1)} copy-done((bf16[256,896]{1,0:T(8,128)(2,1)S(1)}, bf16[256,896]{1,0:T(8,128)(2,1)}, u32[]{:S(2)}) %copy-start.1) | copy-done | bytes 458776
  11.8 2.1 %collective-permute-done.refs_3_.refs_2_ = bf16[224,896]{1,0:T(8,128)(2,1)S(1)} collective-permute-done((bf16[224,896]{1,0:T(8,128)(2,1)}, bf16[224,896]{1,0:T(8,128)(2,1)S(1)}, u32[]{:S(2)}, u32[]{:S(2)}) %collective-permute-start) | collective-permute-done | bytes 401440 | tf_op jit(solution)/shard_map/ppermute | solution.py:130
  13.9 1.4 %collective-permute-start.3 = (bf16[2,256,128]{2,1,0:T(8,128)(2,1)S(1)}, bf16[2,256,128]{2,1,0:T(8,128)(2,1)S(1)}, u32[]{:S(2)}, u32[]{:S(2)}) collective-permute-start(bf16[2,256,128]{2,1,0:T(8,128)(2,1)S(1)} %pad_maximum_fusion.refs_1_), channel_id=1, source_target_pairs={{0,4},{2,6},{4,0},{6,2},{8,12},{10,14},{12,8},{14,10},{16,20},{18,... | collective-permute-start | bytes 393224 | tf_op jit(solution)/shard_map/ppermute | solution.py:34
  15.3 4.2 %collective-permute-done.5.refs_5_ = bf16[2,256,128]{2,1,0:T(8,128)(2,1)S(1)} collective-permute-done((bf16[2,256,128]{2,1,0:T(8,128)(2,1)S(1)}, bf16[2,256,128]{2,1,0:T(8,128)(2,1)S(1)}, u32[]{:S(2)}, u32[]{:S(2)}) %collective-permute-start.5) | collective-permute-done | bytes 131104 | tf_op jit(solution)/shard_map/ppermute | solution.py:34
  19.6 1.6 %collective-permute-start.8 = (bf16[224,896]{1,0:T(8,128)(2,1)S(1)}, bf16[224,896]{1,0:T(8,128)(2,1)S(1)}, u32[]{:S(2)}, u32[]{:S(2)}) collective-permute-start(bf16[224,896]{1,0:T(8,128)(2,1)S(1)} %collective-permute-done.refs_3_.refs_2_), channel_id=1, source_target_pairs={{0,4},{2,6},{8,0},{10,2},{16,8},{18,10},{24,16},{26,18},{28,24},{3... | collective-permute-start | bytes 1204232 | tf_op jit(solution)/shard_map/ppermute | solution.py:130
  21.2 1.3 %collective-permute-start.9 = (bf16[224,896]{1,0:T(8,128)(2,1)S(1)}, bf16[224,896]{1,0:T(8,128)(2,1)S(1)}, u32[]{:S(2)}, u32[]{:S(2)}) collective-permute-start(bf16[224,896]{1,0:T(8,128)(2,1)S(1)} %collective-permute-done.1.refs_4_.refs_3_), channel_id=1, source_target_pairs={{0,8},{2,10},{8,16},{10,18},{16,24},{18,26},{24,28},{26,30},{28,20... | collective-permute-start | bytes 1204232 | tf_op jit(solution)/shard_map/ppermute | solution.py:130
  22.4 4.1 %shard_map.47.refs_0_ = bf16[256,896]{1,0:T(8,128)(2,1)S(1)} custom-call(bf16[256,896]{1,0:T(8,128)(2,1)S(1)} %shard_map.46.refs_0_, bf16[2,256,128]{2,1,0:T(8,128)(2,1)S(1)} %pad_maximum_fusion.refs_1_, bf16[2,256,128]{2,1,0:T(8,128)(2,1)S(1)} %collective-permute-done.2.refs_2_, bf16[2,256,128]{2,1,0:T(8,128)(2,1)S(1)} %collective-permute-done.3.refs_3_, ...), custom_call_target="tpu_custom_call" | custom-call | flops 1 | bytes 1 | tf_op jit(solution)/shard_map/pallas_call | solution.py:21
  26.6 2.6 %collective-permute-done.8.refs_5_.refs_4_ = bf16[224,896]{1,0:T(8,128)(2,1)S(1)} collective-permute-done((bf16[224,896]{1,0:T(8,128)(2,1)S(1)}, bf16[224,896]{1,0:T(8,128)(2,1)S(1)}, u32[]{:S(2)}, u32[]{:S(2)}) %collective-permute-start.8) | collective-permute-done | bytes 401440 | tf_op jit(solution)/shard_map/ppermute | solution.py:130
  29.2 2.5 %collective-permute-start.10 = (bf16[224,896]{1,0:T(8,128)(2,1)S(1)}, bf16[224,896]{1,0:T(8,128)(2,1)S(1)}, u32[]{:S(2)}, u32[]{:S(2)}) collective-permute-start(bf16[224,896]{1,0:T(8,128)(2,1)S(1)} %collective-permute-done.8.refs_5_.refs_4_), channel_id=1, source_target_pairs={{0,4},{2,6},{8,0},{10,2},{16,8},{18,10},{24,16},{26,18},{28,24},{3... | collective-permute-start | bytes 1204232 | tf_op jit(solution)/shard_map/ppermute | solution.py:130
  31.7 0.6 shard_map.48
  32.3 1.6 %collective-permute-start.12 = (bf16[224,256]{1,0:T(8,128)(2,1)S(1)}, bf16[224,256]{1,0:T(8,128)(2,1)S(1)}, u32[]{:S(2)}, u32[]{:S(2)}) collective-permute-start(bf16[224,256]{1,0:T(8,128)(2,1)S(1)} %get-tuple-element.41), channel_id=1, source_target_pairs={{0,1},{1,0},{2,3},{3,2},{4,5},{5,4},{6,7},{7,6},{8,9},{9,8},{10,11... | collective-permute-start | bytes 344072 | tf_op jit(solution)/shard_map/ppermute | solution.py:290
  33.9 5.0 %collective-permute-done.10.refs_7_.refs_6_ = bf16[224,896]{1,0:T(8,128)(2,1)S(1)} collective-permute-done((bf16[224,896]{1,0:T(8,128)(2,1)S(1)}, bf16[224,896]{1,0:T(8,128)(2,1)S(1)}, u32[]{:S(2)}, u32[]{:S(2)}) %collective-permute-start.10) | collective-permute-done | bytes 401440 | tf_op jit(solution)/shard_map/ppermute | solution.py:130
  38.9 2.5 %collective-permute-done.11.refs_8_.refs_7_ = bf16[224,896]{1,0:T(8,128)(2,1)S(1)} collective-permute-done((bf16[224,896]{1,0:T(8,128)(2,1)S(1)}, bf16[224,896]{1,0:T(8,128)(2,1)S(1)}, u32[]{:S(2)}, u32[]{:S(2)}) %collective-permute-start.11) | collective-permute-done | bytes 401440 | tf_op jit(solution)/shard_map/ppermute | solution.py:130
  41.4 0.7 %shard_map.49 = (bf16[448,256]{1,0:T(8,128)(2,1)S(1)}, bf16[448,256]{1,0:T(8,128)(2,1)S(1)}) custom-call(bf16[256,896]{1,0:T(8,128)(2,1)S(1)} %shard_map.47.refs_0_, bf16[256,896]{1,0:T(8,128)(2,1)S(1)} %collective-permute-done.7.refs_1_.refs_0_, bf16[224,896]{1,0:T(8,128)(2,1)S(1)} %bitcast.6, bf16[224,896]{1,0:T(8,128)(2,1)S(1)} %collective-permute-done.refs_3_.refs_2_, ...), custom_call_target="tpu_custom_call" | custom-call | flops 1 | bytes 1 | tf_op jit(solution)/shard_map/pallas_call | solution.py:21
  42.1 1.6 %collective-permute-start.16 = (bf16[448,256]{1,0:T(8,128)(2,1)S(1)}, bf16[448,256]{1,0:T(8,128)(2,1)S(1)}, u32[]{:S(2)}, u32[]{:S(2)}) collective-permute-start(bf16[448,256]{1,0:T(8,128)(2,1)S(1)} %get-tuple-element.43), channel_id=1, source_target_pairs={{0,1},{1,0},{2,3},{3,2},{4,5},{5,4},{6,7},{7,6},{8,9},{9,8},{10,11... | collective-permute-start | bytes 688136 | tf_op jit(solution)/shard_map/ppermute | solution.py:290
  43.8 1.5 %collective-permute-start.15 = (bf16[112,896]{1,0:T(8,128)(2,1)S(1)}, bf16[112,896]{1,0:T(8,128)(2,1)S(1)}, u32[]{:S(2)}, u32[]{:S(2)}) collective-permute-start(bf16[112,896]{1,0:T(8,128)(2,1)S(1)} %slice.7), channel_id=1, source_target_pairs={{0,8},{2,10},{8,16},{10,18},{16,24},{18,26},{24,28},{26,30},{28,20... | collective-permute-start | bytes 602120 | tf_op jit(solution)/shard_map/ppermute | solution.py:130
  45.3 1.1 %collective-permute-start.14 = (bf16[112,896]{1,0:T(8,128)(2,1)S(1)}, bf16[112,896]{1,0:T(8,128)(2,1)S(1)}, u32[]{:S(2)}, u32[]{:S(2)}) collective-permute-start(bf16[112,896]{1,0:T(8,128)(2,1)S(1)} %slice.6), channel_id=1, source_target_pairs={{0,4},{2,6},{8,0},{10,2},{16,8},{18,10},{24,16},{26,18},{28,24},{3... | collective-permute-start | bytes 602120 | tf_op jit(solution)/shard_map/ppermute | solution.py:130
  46.4 5.7 %collective-permute-done.15.refs_10_.refs_9_ = bf16[112,896]{1,0:T(8,128)(2,1)S(1)} collective-permute-done((bf16[112,896]{1,0:T(8,128)(2,1)S(1)}, bf16[112,896]{1,0:T(8,128)(2,1)S(1)}, u32[]{:S(2)}, u32[]{:S(2)}) %collective-permute-start.15) | collective-permute-done | bytes 200736 | tf_op jit(solution)/shard_map/ppermute | solution.py:130
  52.0 0.5 collective-permute-done.14.refs_9_.refs_8_
  52.5 0.5 shard_map.50
  53.0 0.9 %shard_map.52 = bf16[896,256]{1,0:T(8,128)(2,1)S(1)} custom-call(bf16[256,896]{1,0:T(8,128)(2,1)S(1)} %collective-permute-done.7.refs_1_.refs_0_, bf16[224,896]{1,0:T(8,128)(2,1)S(1)} %bitcast.8, bf16[224,896]{1,0:T(8,128)(2,1)S(1)} %collective-permute-done.refs_3_.refs_2_, bf16[224,896]{1,0:T(8,128)(2,1)S(1)} %collective-permute-done.1.refs_4_.refs_3_, ...), custom_call_target="tpu_custom_call" | custom-call | flops 1 | bytes 1 | tf_op jit(solution)/shard_map/pallas_call | solution.py:21
  54.4 1.5 %collective-permute-start.19 = (bf16[224,256]{1,0:T(8,128)(2,1)S(1)}, bf16[224,256]{1,0:T(8,128)(2,1)S(1)}, u32[]{:S(2)}, u32[]{:S(2)}) collective-permute-start(bf16[224,256]{1,0:T(8,128)(2,1)S(1)} %get-tuple-element.55), channel_id=1, source_target_pairs={{0,1},{1,0},{2,3},{3,2},{4,5},{5,4},{6,7},{7,6},{8,9},{9,8},{10,11... | collective-permute-start | bytes 344072 | tf_op jit(solution)/shard_map/ppermute | solution.py:290
  55.9 0.9 %shard_map.51.refs_0_ = f32[896,256]{1,0:T(8,128)S(1)} custom-call(bf16[256,896]{1,0:T(8,128)(2,1)S(1)} %shard_map.47.refs_0_, bf16[224,896]{1,0:T(8,128)(2,1)S(1)} %bitcast.9, bf16[224,896]{1,0:T(8,128)(2,1)S(1)} %collective-permute-done.refs_3_.refs_2_, bf16[224,896]{1,0:T(8,128)(2,1)S(1)} %collective-permute-done.1.refs_4_.refs_3_, ...), custom_call_target="tpu_custom_call" | custom-call | flops 1 | bytes 1 | tf_op jit(solution)/shard_map/pallas_call | solution.py:21
  56.9 0.7 %shard_map.53.refs_2_ = bf16[256,1792]{1,0:T(8,128)(2,1)S(1)} custom-call(f32[896,256]{1,0:T(8,128)S(1)} %shard_map.51.refs_0_, bf16[896,256]{1,0:T(8,128)(2,1)S(1)} %collective-permute-done.18.refs_1_, bf16[224,256]{1,0:T(8,128)(2,1)S(1)} %collective-permute-done.12.refs_2_, bf16[224,256]{1,0:T(8,128)(2,1)S(1)} %collective-permute-done.13.refs_3_, ...), custom_call_target="tpu_custom_call" | custom-call | flops 1 | bytes 1 | tf_op jit(solution)/shard_map/pallas_call | solution.py:21
  57.6 2.8 %collective-permute-done.19.refs_3_ = bf16[224,256]{1,0:T(8,128)(2,1)S(1)} collective-permute-done((bf16[224,256]{1,0:T(8,128)(2,1)S(1)}, bf16[224,256]{1,0:T(8,128)(2,1)S(1)}, u32[]{:S(2)}, u32[]{:S(2)}) %collective-permute-start.19) | collective-permute-done | bytes 114720 | tf_op jit(solution)/shard_map/ppermute | solution.py:290
  60.3 1.0 %collective-permute-done.20.refs_4_ = bf16[224,256]{1,0:T(8,128)(2,1)S(1)} collective-permute-done((bf16[224,256]{1,0:T(8,128)(2,1)S(1)}, bf16[224,256]{1,0:T(8,128)(2,1)S(1)}, u32[]{:S(2)}, u32[]{:S(2)}) %collective-permute-start.20) | collective-permute-done | bytes 114720 | tf_op jit(solution)/shard_map/ppermute | solution.py:291
  61.3 1.4 %shard_map.54 = bf16[256,1792]{1,0:T(8,128)(2,1)} custom-call(f32[896,256]{1,0:T(8,128)S(1)} %shard_map.51.refs_0_, bf16[896,256]{1,0:T(8,128)(2,1)S(1)} %collective-permute-done.18.refs_1_, bf16[256,1792]{1,0:T(8,128)(2,1)S(1)} %shard_map.53.refs_2_, bf16[224,256]{1,0:T(8,128)(2,1)S(1)} %collective-permute-done.19.refs_3_, ...), custom_call_target="tpu_custom_call" | custom-call | flops 1 | bytes 1 | tf_op jit(solution)/shard_map/pallas_call | solution.py:21
  (26 shorter events, 0.8 us)
Async XLA Ops:
  0.0 13.9 %collective-permute-start = (bf16[224,896]{1,0:T(8,128)(2,1)}, bf16[224,896]{1,0:T(8,128)(2,1)S(1)}, u32[]{:S(2)}, u32[]{:S(2)}) collective-permute-start(bf16[224,896]{1,0:T(8,128)(2,1)} %bitcast.3), channel_id=1, source_target_pairs={{0,4},{2,6},{8,0},{10,2},{16,8},{18,10},{24,16},{26,18},{28,24},{3... | collective-permute-start | bytes 1204232 | tf_op jit(solution)/shard_map/ppermute | solution.py:130
  2.9 16.6 %collective-permute-start.1 = (bf16[224,896]{1,0:T(8,128)(2,1)}, bf16[224,896]{1,0:T(8,128)(2,1)S(1)}, u32[]{:S(2)}, u32[]{:S(2)}) collective-permute-start(bf16[224,896]{1,0:T(8,128)(2,1)} %bitcast.4), channel_id=1, source_target_pairs={{0,8},{2,10},{8,16},{10,18},{16,24},{18,26},{24,28},{26,30},{28,20... | collective-permute-start | bytes 1204232 | tf_op jit(solution)/shard_map/ppermute | solution.py:130
  3.9 11.4 %collective-permute-start.6 = (bf16[2,256,128]{2,1,0:T(8,128)(2,1)S(1)}, bf16[2,256,128]{2,1,0:T(8,128)(2,1)S(1)}, u32[]{:S(2)}, u32[]{:S(2)}) collective-permute-start(bf16[2,256,128]{2,1,0:T(8,128)(2,1)S(1)} %pad_maximum_fusion.refs_1_), channel_id=1, source_target_pairs={{2,4},{6,8},{10,12},{14,16},{18,20},{22,24},{26,28},{4,2},{8,6},{1... | collective-permute-start | bytes 393224 | tf_op jit(solution)/shard_map/ppermute | solution.py:96
  4.6 15.0 %collective-permute-start.5 = (bf16[2,256,128]{2,1,0:T(8,128)(2,1)S(1)}, bf16[2,256,128]{2,1,0:T(8,128)(2,1)S(1)}, u32[]{:S(2)}, u32[]{:S(2)}) collective-permute-start(bf16[2,256,128]{2,1,0:T(8,128)(2,1)S(1)} %pad_maximum_fusion.refs_1_), channel_id=1, source_target_pairs={{0,8},{2,10},{4,12},{6,14},{8,0},{10,2},{12,4},{14,6},{16,24},{18,... | collective-permute-start | bytes 393224 | tf_op jit(solution)/shard_map/ppermute | solution.py:34
  8.2 11.4 %collective-permute-start.4 = (bf16[2,256,128]{2,1,0:T(8,128)(2,1)S(1)}, bf16[2,256,128]{2,1,0:T(8,128)(2,1)S(1)}, u32[]{:S(2)}, u32[]{:S(2)}) collective-permute-start(bf16[2,256,128]{2,1,0:T(8,128)(2,1)S(1)} %pad_maximum_fusion.refs_1_), channel_id=1, source_target_pairs={{0,16},{2,18},{4,20},{6,22},{8,24},{10,26},{12,28},{14,30},{16,0},... | collective-permute-start | bytes 393224 | tf_op jit(solution)/shard_map/ppermute | solution.py:34
  10.8 1.0 %copy-start.1 = (bf16[256,896]{1,0:T(8,128)(2,1)S(1)}, bf16[256,896]{1,0:T(8,128)(2,1)}, u32[]{:S(2)}) copy-start(bf16[256,896]{1,0:T(8,128)(2,1)} %from_ref.1) | copy-start | bytes 1376260
  11.8 19.9 %copy-start = (bf16[896,224]{0,1:T(8,128)(2,1)S(1)}, bf16[896,224]{0,1:T(8,128)(2,1)}, u32[]{:S(2)}) copy-start(bf16[896,224]{0,1:T(8,128)(2,1)} %param.7) | copy-start | bytes 1204228
  13.9 5.7 %collective-permute-start.3 = (bf16[2,256,128]{2,1,0:T(8,128)(2,1)S(1)}, bf16[2,256,128]{2,1,0:T(8,128)(2,1)S(1)}, u32[]{:S(2)}, u32[]{:S(2)}) collective-permute-start(bf16[2,256,128]{2,1,0:T(8,128)(2,1)S(1)} %pad_maximum_fusion.refs_1_), channel_id=1, source_target_pairs={{0,4},{2,6},{4,0},{6,2},{8,12},{10,14},{12,8},{14,10},{16,20},{18,... | collective-permute-start | bytes 393224 | tf_op jit(solution)/shard_map/ppermute | solution.py:34
  15.3 4.2 %collective-permute-start.2 = (bf16[2,256,128]{2,1,0:T(8,128)(2,1)S(1)}, bf16[2,256,128]{2,1,0:T(8,128)(2,1)S(1)}, u32[]{:S(2)}, u32[]{:S(2)}) collective-permute-start(bf16[2,256,128]{2,1,0:T(8,128)(2,1)S(1)} %pad_maximum_fusion.refs_1_), channel_id=1, source_target_pairs={{0,2},{2,0},{4,6},{6,4},{8,10},{10,8},{12,14},{14,12},{16,18},{18,... | collective-permute-start | bytes 393224 | tf_op jit(solution)/shard_map/ppermute | solution.py:34
  19.6 9.7 %collective-permute-start.8 = (bf16[224,896]{1,0:T(8,128)(2,1)S(1)}, bf16[224,896]{1,0:T(8,128)(2,1)S(1)}, u32[]{:S(2)}, u32[]{:S(2)}) collective-permute-start(bf16[224,896]{1,0:T(8,128)(2,1)S(1)} %collective-permute-done.refs_3_.refs_2_), channel_id=1, source_target_pairs={{0,4},{2,6},{8,0},{10,2},{16,8},{18,10},{24,16},{26,18},{28,24},{3... | collective-permute-start | bytes 1204232 | tf_op jit(solution)/shard_map/ppermute | solution.py:130
  21.2 10.6 %collective-permute-start.9 = (bf16[224,896]{1,0:T(8,128)(2,1)S(1)}, bf16[224,896]{1,0:T(8,128)(2,1)S(1)}, u32[]{:S(2)}, u32[]{:S(2)}) collective-permute-start(bf16[224,896]{1,0:T(8,128)(2,1)S(1)} %collective-permute-done.1.refs_4_.refs_3_), channel_id=1, source_target_pairs={{0,8},{2,10},{8,16},{10,18},{16,24},{18,26},{24,28},{26,30},{28,20... | collective-permute-start | bytes 1204232 | tf_op jit(solution)/shard_map/ppermute | solution.py:130
  26.6 5.2 %collective-permute-start.7 = (bf16[256,896]{1,0:T(8,128)(2,1)S(1)}, bf16[256,896]{1,0:T(8,128)(2,1)S(1)}, u32[]{:S(2)}, u32[]{:S(2)}) collective-permute-start(bf16[256,896]{1,0:T(8,128)(2,1)S(1)} %shard_map.47.refs_0_), channel_id=1, source_target_pairs={{0,2},{2,0},{4,6},{6,4},{8,10},{10,8},{12,14},{14,12},{16,18},{18,... | collective-permute-start | bytes 1376264 | tf_op jit(solution)/shard_map/ppermute | solution.py:34
  29.2 9.6 %collective-permute-start.10 = (bf16[224,896]{1,0:T(8,128)(2,1)S(1)}, bf16[224,896]{1,0:T(8,128)(2,1)S(1)}, u32[]{:S(2)}, u32[]{:S(2)}) collective-permute-start(bf16[224,896]{1,0:T(8,128)(2,1)S(1)} %collective-permute-done.8.refs_5_.refs_4_), channel_id=1, source_target_pairs={{0,4},{2,6},{8,0},{10,2},{16,8},{18,10},{24,16},{26,18},{28,24},{3... | collective-permute-start | bytes 1204232 | tf_op jit(solution)/shard_map/ppermute | solution.py:130
  31.7 9.6 %collective-permute-start.11 = (bf16[224,896]{1,0:T(8,128)(2,1)S(1)}, bf16[224,896]{1,0:T(8,128)(2,1)S(1)}, u32[]{:S(2)}, u32[]{:S(2)}) collective-permute-start(bf16[224,896]{1,0:T(8,128)(2,1)S(1)} %collective-permute-done.9.refs_6_.refs_5_), channel_id=1, source_target_pairs={{0,8},{2,10},{8,16},{10,18},{16,24},{18,26},{24,28},{26,30},{28,20... | collective-permute-start | bytes 1204232 | tf_op jit(solution)/shard_map/ppermute | solution.py:130
  32.3 11.4 %collective-permute-start.12 = (bf16[224,256]{1,0:T(8,128)(2,1)S(1)}, bf16[224,256]{1,0:T(8,128)(2,1)S(1)}, u32[]{:S(2)}, u32[]{:S(2)}) collective-permute-start(bf16[224,256]{1,0:T(8,128)(2,1)S(1)} %get-tuple-element.41), channel_id=1, source_target_pairs={{0,1},{1,0},{2,3},{3,2},{4,5},{5,4},{6,7},{7,6},{8,9},{9,8},{10,11... | collective-permute-start | bytes 344072 | tf_op jit(solution)/shard_map/ppermute | solution.py:290
  33.9 9.8 %collective-permute-start.13 = (bf16[224,256]{1,0:T(8,128)(2,1)S(1)}, bf16[224,256]{1,0:T(8,128)(2,1)S(1)}, u32[]{:S(2)}, u32[]{:S(2)}) collective-permute-start(bf16[224,256]{1,0:T(8,128)(2,1)S(1)} %get-tuple-element.42), channel_id=1, source_target_pairs={{0,3},{1,2},{2,1},{3,0},{4,7},{5,6},{6,5},{7,4},{8,11},{9,10},{10,... | collective-permute-start | bytes 344072 | tf_op jit(solution)/shard_map/ppermute | solution.py:291
  42.1 10.4 %collective-permute-start.16 = (bf16[448,256]{1,0:T(8,128)(2,1)S(1)}, bf16[448,256]{1,0:T(8,128)(2,1)S(1)}, u32[]{:S(2)}, u32[]{:S(2)}) collective-permute-start(bf16[448,256]{1,0:T(8,128)(2,1)S(1)} %get-tuple-element.43), channel_id=1, source_target_pairs={{0,1},{1,0},{2,3},{3,2},{4,5},{5,4},{6,7},{7,6},{8,9},{9,8},{10,11... | collective-permute-start | bytes 688136 | tf_op jit(solution)/shard_map/ppermute | solution.py:290
  43.7 8.8 %collective-permute-start.17 = (bf16[448,256]{1,0:T(8,128)(2,1)S(1)}, bf16[448,256]{1,0:T(8,128)(2,1)S(1)}, u32[]{:S(2)}, u32[]{:S(2)}) collective-permute-start(bf16[448,256]{1,0:T(8,128)(2,1)S(1)} %get-tuple-element.44), channel_id=1, source_target_pairs={{0,3},{1,2},{2,1},{3,0},{4,7},{5,6},{6,5},{7,4},{8,11},{9,10},{10,... | collective-permute-start | bytes 688136 | tf_op jit(solution)/shard_map/ppermute | solution.py:291
  43.8 8.3 %collective-permute-start.15 = (bf16[112,896]{1,0:T(8,128)(2,1)S(1)}, bf16[112,896]{1,0:T(8,128)(2,1)S(1)}, u32[]{:S(2)}, u32[]{:S(2)}) collective-permute-start(bf16[112,896]{1,0:T(8,128)(2,1)S(1)} %slice.7), channel_id=1, source_target_pairs={{0,8},{2,10},{8,16},{10,18},{16,24},{18,26},{24,28},{26,30},{28,20... | collective-permute-start | bytes 602120 | tf_op jit(solution)/shard_map/ppermute | solution.py:130
  45.3 7.2 %collective-permute-start.14 = (bf16[112,896]{1,0:T(8,128)(2,1)S(1)}, bf16[112,896]{1,0:T(8,128)(2,1)S(1)}, u32[]{:S(2)}, u32[]{:S(2)}) collective-permute-start(bf16[112,896]{1,0:T(8,128)(2,1)S(1)} %slice.6), channel_id=1, source_target_pairs={{0,4},{2,6},{8,0},{10,2},{16,8},{18,10},{24,16},{26,18},{28,24},{3... | collective-permute-start | bytes 602120 | tf_op jit(solution)/shard_map/ppermute | solution.py:130
  54.0 2.9 %collective-permute-start.18 = (bf16[896,256]{1,0:T(8,128)(2,1)S(1)}, bf16[896,256]{1,0:T(8,128)(2,1)S(1)}, u32[]{:S(2)}, u32[]{:S(2)}) collective-permute-start(bf16[896,256]{1,0:T(8,128)(2,1)S(1)} %shard_map.52), channel_id=1, source_target_pairs={{0,2},{2,0},{4,6},{6,4},{8,10},{10,8},{12,14},{14,12},{16,18},{18,... | collective-permute-start | bytes 1376264 | tf_op jit(solution)/shard_map/ppermute | solution.py:34
  54.4 5.9 %collective-permute-start.19 = (bf16[224,256]{1,0:T(8,128)(2,1)S(1)}, bf16[224,256]{1,0:T(8,128)(2,1)S(1)}, u32[]{:S(2)}, u32[]{:S(2)}) collective-permute-start(bf16[224,256]{1,0:T(8,128)(2,1)S(1)} %get-tuple-element.55), channel_id=1, source_target_pairs={{0,1},{1,0},{2,3},{3,2},{4,5},{5,4},{6,7},{7,6},{8,9},{9,8},{10,11... | collective-permute-start | bytes 344072 | tf_op jit(solution)/shard_map/ppermute | solution.py:290
  55.9 5.4 %collective-permute-start.20 = (bf16[224,256]{1,0:T(8,128)(2,1)S(1)}, bf16[224,256]{1,0:T(8,128)(2,1)S(1)}, u32[]{:S(2)}, u32[]{:S(2)}) collective-permute-start(bf16[224,256]{1,0:T(8,128)(2,1)S(1)} %get-tuple-element.56), channel_id=1, source_target_pairs={{0,3},{1,2},{2,1},{3,0},{4,7},{5,6},{6,5},{7,4},{8,11},{9,10},{10,... | collective-permute-start | bytes 344072 | tf_op jit(solution)/shard_map/ppermute | solution.py:291

commit v5 on v4

--- a/solution.py
+++ b/solution.py
@@ -192,10 +192,47 @@
     )
 
 
+def last_body(offsets, *refs):
+    (mine_ref, theirs_ref, before_ref), parts = refs[:3], grouped(refs[3:-4], offsets)
+    to_same_ref, to_other_ref, to_core_ref, held = refs[-4:]
+    ring, head = Ring(), lax.axis_index("head")
+    rank = len(offsets) // 2 - 1
+    for (belongs, before), part in zip(ring.ranks(1 - head, offsets), parts):
+
+        @pl.when(jnp.logical_and(belongs, before == rank))
+        def _():
+            hold(held, 0, part)
+
+    to_same_ref[...] = times(held[...], mine_ref).astype(jnp.bfloat16)
+    to_other_ref[...] = times(held[...], theirs_ref).astype(jnp.bfloat16)
+    to_core_ref[...] = before_ref[...]
+    side, slot = ring.side_and_slot(offsets[-1])
+
+    @pl.when(side == head)
+    def _():
+        hold(held, 0, parts[-1])
+        there = pl.ds(pl.multiple_of(slot * held.shape[0], 16), held.shape[0])
+        to_core_ref[there, :] = times(held[...], theirs_ref).astype(jnp.bfloat16)
+
+
+def last(rows, before, offsets, parts):
+    step, depth = parts[0].shape
+    shape = jax.ShapeDtypeStruct((step, rows[0].shape[0]), jnp.bfloat16)
+    to_same, to_other, to_core = call_kernel(
+        functools.partial(last_body, offsets),
+        [shape, shape, jax.ShapeDtypeStruct(before.shape, before.dtype)],
+        [*rows, before, *parts],
+        scratch=[pltpu.VMEM((step, depth), jnp.bfloat16)],
+    )
+    return [to_same, to_other], to_core
+
+
 def kept_body(offsets, *refs):
     rows_ref, parts, (out_ref, held) = refs[0], grouped(refs[1:-2], offsets), refs[-2:]
-    step = 2 * held.shape[0] // len(offsets)
     ring, head = Ring(), lax.axis_index("head")
+    step = held.shape[0] // (ring.chips // 2)
+    if len(offsets) < ring.chips:
+        held[...] = jnp.zeros(held.shape, held.dtype)
     for offset, part in zip(offsets, parts):
         side, slot = ring.side_and_slot(offset)
 
@@ -208,7 +245,7 @@
 
 def kept(rows, offsets, parts, dtype):
     step, depth = parts[0].shape
-    shape = (step * len(offsets) // 2, rows.shape[0])
+    shape = (step * (Ring().chips // 2), rows.shape[0])
     return call_kernel(
         functools.partial(kept_body, offsets),
         jax.ShapeDtypeStruct(shape, dtype),
@@ -307,13 +344,13 @@
     product = sent(rows, 1, 2, offsets[:7], parts)
     pair = [after(shard, (first, product)) for shard in pair]
     second = swap(product)
+    before = kept(rows[1], offsets[:7], parts, jnp.bfloat16)
     opposite = both_ways(pair[0][:half], pair[1][half:])
     parts += opposite
     parts[-2:], second = lax.optimization_barrier((parts[-2:], second))
-    product = sent(rows, 3, 1, offsets, parts)
+    product, to_core = last(rows, before, offsets, parts)
     rows, product = lax.optimization_barrier((rows, product))
     third = swap(product)
-    to_core = kept(rows[1], offsets, parts, jnp.bfloat16)
     keep = kept(rows[0], offsets, parts, jnp.float32)
     from_core = flip(to_core, 1)
     done = total(keep, from_core, [*first, *second], widths[:2], offsets)

time: 63.3 us -> 62.7 us (level)
  waiting for transfers between devices: 26.2 us -> 25.3 us
    ppermute x8, waiting for transfers between devices: 18.2 us -> 17.2 us  [shift(): return lax.ppermute(value, 'seq', pairs)]
    ppermute x3, waiting for transfers between devices: 1.01 us -> 1.72 us  [swap(): lax.ppermute(other, ('seq', 'head'), crossed)]
    ppermute x3, waiting for transfers between devices: 2.76 us -> 2.12 us  [swap(): lax.ppermute(same, 'head', [(0, 1), (1, 0)])]
  transfers between devices with their start and end apart: 21 -> 21, of which waited for: 9 -> 9; matrix products, arithmetic and copies ran while one was open for 1% -> 1% of each run, Pallas kernels for 11% -> 13%
where the time goes in v5:
time: 62.7 us; the launch traced here: 62.2 us
  waiting for transfers between devices  25.3 us (40%)
  starting transfers between devices  24.8 us (40%)
  Pallas kernels  9.97 us (16%)
  local copies, waits for them, and re-layouts  1.06 us (2%)
  other arithmetic  0.88 us (1%)
    ppermute x8, waiting for transfers between devices, shift(): return lax.ppermute(value, 'seq', pairs)  17.2 us
    ppermute x8, starting transfers between devices, shift(): return lax.ppermute(value, 'seq', pairs)  11 us
    pallas_call x9, Pallas kernels, call_kernel(): pl.pallas_call(body, out_shape=out_shape, in_specs=[in_vmem] * len(operan...  9.97 us
    ppermute x6, starting transfers between devices, flip(): return lax.ppermute(value, 'seq', pairs)  8.15 us
    ppermute x3, starting transfers between devices, swap(): lax.ppermute(same, 'head', [(0, 1), (1, 0)])  5.01 us
    ppermute x6, waiting for transfers between devices, flip(): return lax.ppermute(value, 'seq', pairs)  4.22 us
    ppermute x3, waiting for transfers between devices, swap(): lax.ppermute(same, 'head', [(0, 1), (1, 0)])  2.12 us
    ppermute x3, waiting for transfers between devices, swap(): lax.ppermute(other, ('seq', 'head'), crossed)  1.72 us
  transfers between devices with their start and end apart: 21, of which 9 were waited for; matrix products, arithmetic and copies ran while one was open for 1% of the time, Pallas kernels for 13%

profile of v5, /device:TPU:0, one launch (start us, length us, event | category | flops | bytes accessed | tf_op | source)
XLA Modules:
  0.0 62.2 jit_solution(2979429310284982443)
XLA Ops:
  0.0 2.9 %collective-permute-start = (bf16[224,896]{1,0:T(8,128)(2,1)}, bf16[224,896]{1,0:T(8,128)(2,1)S(1)}, u32[]{:S(2)}, u32[]{:S(2)}) collective-permute-start(bf16[224,896]{1,0:T(8,128)(2,1)} %bitcast.3), channel_id=1, source_target_pairs={{0,4},{2,6},{8,0},{10,2},{16,8},{18,10},{24,16},{26,18},{28,24},{3... | collective-permute-start | bytes 1204232 | tf_op jit(solution)/shard_map/ppermute | solution.py:130
  3.0 0.9 %pad_maximum_fusion.refs_1_ = bf16[2,256,128]{2,1,0:T(8,128)(2,1)S(1)} fusion(bf16[1,256,128]{2,1,0:T(8,128)(2,1)} %bitcast.10, bf16[1,256,128]{2,1,0:T(8,128)(2,1)} %bitcast.11), kind=kLoop, calls=%fused_computation | loop fusion | flops 65536 | bytes 262144 | tf_op jit(solution)/shard_map/stack | solution.py:370
  3.9 0.7 %collective-permute-start.6 = (bf16[2,256,128]{2,1,0:T(8,128)(2,1)S(1)}, bf16[2,256,128]{2,1,0:T(8,128)(2,1)S(1)}, u32[]{:S(2)}, u32[]{:S(2)}) collective-permute-start(bf16[2,256,128]{2,1,0:T(8,128)(2,1)S(1)} %pad_maximum_fusion.refs_1_), channel_id=1, source_target_pairs={{2,4},{6,8},{10,12},{14,16},{18,20},{22,24},{26,28},{4,2},{8,6},{1... | collective-permute-start | bytes 393224 | tf_op jit(solution)/shard_map/ppermute | solution.py:96
  4.6 3.6 %collective-permute-start.5 = (bf16[2,256,128]{2,1,0:T(8,128)(2,1)S(1)}, bf16[2,256,128]{2,1,0:T(8,128)(2,1)S(1)}, u32[]{:S(2)}, u32[]{:S(2)}) collective-permute-start(bf16[2,256,128]{2,1,0:T(8,128)(2,1)S(1)} %pad_maximum_fusion.refs_1_), channel_id=1, source_target_pairs={{0,8},{2,10},{4,12},{6,14},{8,0},{10,2},{12,4},{14,6},{16,24},{18,... | collective-permute-start | bytes 393224 | tf_op jit(solution)/shard_map/ppermute | solution.py:34
  8.2 2.6 %collective-permute-start.4 = (bf16[2,256,128]{2,1,0:T(8,128)(2,1)S(1)}, bf16[2,256,128]{2,1,0:T(8,128)(2,1)S(1)}, u32[]{:S(2)}, u32[]{:S(2)}) collective-permute-start(bf16[2,256,128]{2,1,0:T(8,128)(2,1)S(1)} %pad_maximum_fusion.refs_1_), channel_id=1, source_target_pairs={{0,16},{2,18},{4,20},{6,22},{8,24},{10,26},{12,28},{14,30},{16,0},... | collective-permute-start | bytes 393224 | tf_op jit(solution)/shard_map/ppermute | solution.py:34
  10.8 1.0 %copy-done.1 = bf16[256,896]{1,0:T(8,128)(2,1)S(1)} copy-done((bf16[256,896]{1,0:T(8,128)(2,1)S(1)}, bf16[256,896]{1,0:T(8,128)(2,1)}, u32[]{:S(2)}) %copy-start.1) | copy-done | bytes 458776
  11.8 2.1 %collective-permute-done.refs_2_.refs_3_.refs_4_ = bf16[224,896]{1,0:T(8,128)(2,1)S(1)} collective-permute-done((bf16[224,896]{1,0:T(8,128)(2,1)}, bf16[224,896]{1,0:T(8,128)(2,1)S(1)}, u32[]{:S(2)}, u32[]{:S(2)}) %collective-permute-start) | collective-permute-done | bytes 401440 | tf_op jit(solution)/shard_map/ppermute | solution.py:130
  13.9 1.4 %collective-permute-start.3 = (bf16[2,256,128]{2,1,0:T(8,128)(2,1)S(1)}, bf16[2,256,128]{2,1,0:T(8,128)(2,1)S(1)}, u32[]{:S(2)}, u32[]{:S(2)}) collective-permute-start(bf16[2,256,128]{2,1,0:T(8,128)(2,1)S(1)} %pad_maximum_fusion.refs_1_), channel_id=1, source_target_pairs={{0,4},{2,6},{4,0},{6,2},{8,12},{10,14},{12,8},{14,10},{16,20},{18,... | collective-permute-start | bytes 393224 | tf_op jit(solution)/shard_map/ppermute | solution.py:34
  15.3 4.2 %collective-permute-done.5.refs_5_ = bf16[2,256,128]{2,1,0:T(8,128)(2,1)S(1)} collective-permute-done((bf16[2,256,128]{2,1,0:T(8,128)(2,1)S(1)}, bf16[2,256,128]{2,1,0:T(8,128)(2,1)S(1)}, u32[]{:S(2)}, u32[]{:S(2)}) %collective-permute-start.5) | collective-permute-done | bytes 131104 | tf_op jit(solution)/shard_map/ppermute | solution.py:34
  19.6 1.6 %collective-permute-start.8 = (bf16[224,896]{1,0:T(8,128)(2,1)S(1)}, bf16[224,896]{1,0:T(8,128)(2,1)S(1)}, u32[]{:S(2)}, u32[]{:S(2)}) collective-permute-start(bf16[224,896]{1,0:T(8,128)(2,1)S(1)} %collective-permute-done.refs_2_.refs_3_.refs_4_), channel_id=1, source_target_pairs={{0,4},{2,6},{8,0},{10,2},{16,8},{18,10},{24,16},{26,18},{28,24},{3... | collective-permute-start | bytes 1204232 | tf_op jit(solution)/shard_map/ppermute | solution.py:130
  21.2 1.3 %collective-permute-start.9 = (bf16[224,896]{1,0:T(8,128)(2,1)S(1)}, bf16[224,896]{1,0:T(8,128)(2,1)S(1)}, u32[]{:S(2)}, u32[]{:S(2)}) collective-permute-start(bf16[224,896]{1,0:T(8,128)(2,1)S(1)} %collective-permute-done.1.refs_3_.refs_4_.refs_5_), channel_id=1, source_target_pairs={{0,8},{2,10},{8,16},{10,18},{16,24},{18,26},{24,28},{26,30},{28,20... | collective-permute-start | bytes 1204232 | tf_op jit(solution)/shard_map/ppermute | solution.py:130
  22.4 4.1 %shard_map.47.refs_0_ = bf16[256,896]{1,0:T(8,128)(2,1)S(1)} custom-call(bf16[256,896]{1,0:T(8,128)(2,1)S(1)} %shard_map.46.refs_0_, bf16[2,256,128]{2,1,0:T(8,128)(2,1)S(1)} %pad_maximum_fusion.refs_1_, bf16[2,256,128]{2,1,0:T(8,128)(2,1)S(1)} %collective-permute-done.2.refs_2_, bf16[2,256,128]{2,1,0:T(8,128)(2,1)S(1)} %collective-permute-done.3.refs_3_, ...), custom_call_target="tpu_custom_call" | custom-call | flops 1 | bytes 1 | tf_op jit(solution)/shard_map/pallas_call | solution.py:21
  26.6 2.6 %collective-permute-done.8.refs_4_.refs_5_.refs_6_ = bf16[224,896]{1,0:T(8,128)(2,1)S(1)} collective-permute-done((bf16[224,896]{1,0:T(8,128)(2,1)S(1)}, bf16[224,896]{1,0:T(8,128)(2,1)S(1)}, u32[]{:S(2)}, u32[]{:S(2)}) %collective-permute-start.8) | collective-permute-done | bytes 401440 | tf_op jit(solution)/shard_map/ppermute | solution.py:130
  29.2 2.5 %collective-permute-start.10 = (bf16[224,896]{1,0:T(8,128)(2,1)S(1)}, bf16[224,896]{1,0:T(8,128)(2,1)S(1)}, u32[]{:S(2)}, u32[]{:S(2)}) collective-permute-start(bf16[224,896]{1,0:T(8,128)(2,1)S(1)} %collective-permute-done.8.refs_4_.refs_5_.refs_6_), channel_id=1, source_target_pairs={{0,4},{2,6},{8,0},{10,2},{16,8},{18,10},{24,16},{26,18},{28,24},{3... | collective-permute-start | bytes 1204232 | tf_op jit(solution)/shard_map/ppermute | solution.py:130
  31.7 0.6 shard_map.49
  32.3 1.6 %collective-permute-start.12 = (bf16[224,256]{1,0:T(8,128)(2,1)S(1)}, bf16[224,256]{1,0:T(8,128)(2,1)S(1)}, u32[]{:S(2)}, u32[]{:S(2)}) collective-permute-start(bf16[224,256]{1,0:T(8,128)(2,1)S(1)} %get-tuple-element.41), channel_id=1, source_target_pairs={{0,1},{1,0},{2,3},{3,2},{4,5},{5,4},{6,7},{7,6},{8,9},{9,8},{10,11... | collective-permute-start | bytes 344072 | tf_op jit(solution)/shard_map/ppermute | solution.py:327
  33.9 5.0 %collective-permute-done.10.refs_6_.refs_7_.refs_8_ = bf16[224,896]{1,0:T(8,128)(2,1)S(1)} collective-permute-done((bf16[224,896]{1,0:T(8,128)(2,1)S(1)}, bf16[224,896]{1,0:T(8,128)(2,1)S(1)}, u32[]{:S(2)}, u32[]{:S(2)}) %collective-permute-start.10) | collective-permute-done | bytes 401440 | tf_op jit(solution)/shard_map/ppermute | solution.py:130
  38.9 2.5 %collective-permute-done.11.refs_7_.refs_8_.refs_9_ = bf16[224,896]{1,0:T(8,128)(2,1)S(1)} collective-permute-done((bf16[224,896]{1,0:T(8,128)(2,1)S(1)}, bf16[224,896]{1,0:T(8,128)(2,1)S(1)}, u32[]{:S(2)}, u32[]{:S(2)}) %collective-permute-start.11) | collective-permute-done | bytes 401440 | tf_op jit(solution)/shard_map/ppermute | solution.py:130
  41.4 0.7 %shard_map.50 = (bf16[448,256]{1,0:T(8,128)(2,1)S(1)}, bf16[448,256]{1,0:T(8,128)(2,1)S(1)}) custom-call(bf16[256,896]{1,0:T(8,128)(2,1)S(1)} %shard_map.47.refs_0_, bf16[256,896]{1,0:T(8,128)(2,1)S(1)} %collective-permute-done.7.refs_0_.refs_1_, bf16[224,896]{1,0:T(8,128)(2,1)S(1)} %bitcast.6, ...), custom_call_target="tpu_custom_call" | custom-call | flops 1 | bytes 1 | tf_op jit(solution)/shard_map/pallas_call | solution.py:21
  42.1 1.6 %collective-permute-start.16 = (bf16[448,256]{1,0:T(8,128)(2,1)S(1)}, bf16[448,256]{1,0:T(8,128)(2,1)S(1)}, u32[]{:S(2)}, u32[]{:S(2)}) collective-permute-start(bf16[448,256]{1,0:T(8,128)(2,1)S(1)} %get-tuple-element.43), channel_id=1, source_target_pairs={{0,1},{1,0},{2,3},{3,2},{4,5},{5,4},{6,7},{7,6},{8,9},{9,8},{10,11... | collective-permute-start | bytes 688136 | tf_op jit(solution)/shard_map/ppermute | solution.py:327
  43.8 1.5 %collective-permute-start.15 = (bf16[112,896]{1,0:T(8,128)(2,1)S(1)}, bf16[112,896]{1,0:T(8,128)(2,1)S(1)}, u32[]{:S(2)}, u32[]{:S(2)}) collective-permute-start(bf16[112,896]{1,0:T(8,128)(2,1)S(1)} %slice.7), channel_id=1, source_target_pairs={{0,8},{2,10},{8,16},{10,18},{16,24},{18,26},{24,28},{26,30},{28,20... | collective-permute-start | bytes 602120 | tf_op jit(solution)/shard_map/ppermute | solution.py:130
  45.3 1.1 %collective-permute-start.14 = (bf16[112,896]{1,0:T(8,128)(2,1)S(1)}, bf16[112,896]{1,0:T(8,128)(2,1)S(1)}, u32[]{:S(2)}, u32[]{:S(2)}) collective-permute-start(bf16[112,896]{1,0:T(8,128)(2,1)S(1)} %slice.6), channel_id=1, source_target_pairs={{0,4},{2,6},{8,0},{10,2},{16,8},{18,10},{24,16},{26,18},{28,24},{3... | collective-permute-start | bytes 602120 | tf_op jit(solution)/shard_map/ppermute | solution.py:130
  46.4 1.0 %shard_map.48.refs_2_ = bf16[896,256]{1,0:T(8,128)(2,1)S(1)} custom-call(bf16[256,896]{1,0:T(8,128)(2,1)S(1)} %collective-permute-done.7.refs_0_.refs_1_, bf16[224,896]{1,0:T(8,128)(2,1)S(1)} %bitcast.7, bf16[224,896]{1,0:T(8,128)(2,1)S(1)} %collective-permute-done.refs_2_.refs_3_.refs_4_, ...), custom_call_target="tpu_custom_call" | custom-call | flops 1 | bytes 1 | tf_op jit(solution)/shard_map/pallas_call | solution.py:21
  47.4 4.7 %collective-permute-done.15.refs_11_.refs_9_ = bf16[112,896]{1,0:T(8,128)(2,1)S(1)} collective-permute-done((bf16[112,896]{1,0:T(8,128)(2,1)S(1)}, bf16[112,896]{1,0:T(8,128)(2,1)S(1)}, u32[]{:S(2)}, u32[]{:S(2)}) %collective-permute-start.15) | collective-permute-done | bytes 200736 | tf_op jit(solution)/shard_map/ppermute | solution.py:130
  52.0 0.5 collective-permute-done.14.refs_10_.refs_8_
  52.5 0.5 shard_map.51
  53.5 1.8 %collective-permute-start.19 = (bf16[224,256]{1,0:T(8,128)(2,1)S(1)}, bf16[224,256]{1,0:T(8,128)(2,1)S(1)}, u32[]{:S(2)}, u32[]{:S(2)}) collective-permute-start(bf16[224,256]{1,0:T(8,128)(2,1)S(1)} %get-tuple-element.55), channel_id=1, source_target_pairs={{0,1},{1,0},{2,3},{3,2},{4,5},{5,4},{6,7},{7,6},{8,9},{9,8},{10,11... | collective-permute-start | bytes 344072 | tf_op jit(solution)/shard_map/ppermute | solution.py:327
  55.3 0.9 %shard_map.52.refs_0_ = f32[896,256]{1,0:T(8,128)S(1)} custom-call(bf16[256,896]{1,0:T(8,128)(2,1)S(1)} %shard_map.47.refs_0_, bf16[224,896]{1,0:T(8,128)(2,1)S(1)} %bitcast.9, bf16[224,896]{1,0:T(8,128)(2,1)S(1)} %collective-permute-done.refs_2_.refs_3_.refs_4_, bf16[224,896]{1,0:T(8,128)(2,1)S(1)} %collective-permute-done.1.refs_3_.refs_4_.refs_5_, ...), custom_call_target="tpu_custom_call" | custom-call | flops 1 | bytes 1 | tf_op jit(solution)/shard_map/pallas_call | solution.py:21
  56.2 0.7 %shard_map.53.refs_2_ = bf16[256,1792]{1,0:T(8,128)(2,1)S(1)} custom-call(f32[896,256]{1,0:T(8,128)S(1)} %shard_map.52.refs_0_, bf16[896,256]{1,0:T(8,128)(2,1)S(1)} %collective-permute-done.18.refs_1_, bf16[224,256]{1,0:T(8,128)(2,1)S(1)} %collective-permute-done.12.refs_2_, bf16[224,256]{1,0:T(8,128)(2,1)S(1)} %collective-permute-done.13.refs_3_, ...), custom_call_target="tpu_custom_call" | custom-call | flops 1 | bytes 1 | tf_op jit(solution)/shard_map/pallas_call | solution.py:21
  56.9 2.1 %collective-permute-done.19.refs_3_ = bf16[224,256]{1,0:T(8,128)(2,1)S(1)} collective-permute-done((bf16[224,256]{1,0:T(8,128)(2,1)S(1)}, bf16[224,256]{1,0:T(8,128)(2,1)S(1)}, u32[]{:S(2)}, u32[]{:S(2)}) %collective-permute-start.19) | collective-permute-done | bytes 114720 | tf_op jit(solution)/shard_map/ppermute | solution.py:327
  59.1 1.7 %collective-permute-done.20.refs_4_ = bf16[224,256]{1,0:T(8,128)(2,1)S(1)} collective-permute-done((bf16[224,256]{1,0:T(8,128)(2,1)S(1)}, bf16[224,256]{1,0:T(8,128)(2,1)S(1)}, u32[]{:S(2)}, u32[]{:S(2)}) %collective-permute-start.20) | collective-permute-done | bytes 114720 | tf_op jit(solution)/shard_map/ppermute | solution.py:328
  60.8 1.4 %shard_map.54 = bf16[256,1792]{1,0:T(8,128)(2,1)} custom-call(f32[896,256]{1,0:T(8,128)S(1)} %shard_map.52.refs_0_, bf16[896,256]{1,0:T(8,128)(2,1)S(1)} %collective-permute-done.18.refs_1_, bf16[256,1792]{1,0:T(8,128)(2,1)S(1)} %shard_map.53.refs_2_, bf16[224,256]{1,0:T(8,128)(2,1)S(1)} %collective-permute-done.19.refs_3_, ...), custom_call_target="tpu_custom_call" | custom-call | flops 1 | bytes 1 | tf_op jit(solution)/shard_map/pallas_call | solution.py:21
  (26 shorter events, 0.7 us)
Async XLA Ops:
  0.0 13.9 %collective-permute-start = (bf16[224,896]{1,0:T(8,128)(2,1)}, bf16[224,896]{1,0:T(8,128)(2,1)S(1)}, u32[]{:S(2)}, u32[]{:S(2)}) collective-permute-start(bf16[224,896]{1,0:T(8,128)(2,1)} %bitcast.3), channel_id=1, source_target_pairs={{0,4},{2,6},{8,0},{10,2},{16,8},{18,10},{24,16},{26,18},{28,24},{3... | collective-permute-start | bytes 1204232 | tf_op jit(solution)/shard_map/ppermute | solution.py:130
  2.9 16.6 %collective-permute-start.1 = (bf16[224,896]{1,0:T(8,128)(2,1)}, bf16[224,896]{1,0:T(8,128)(2,1)S(1)}, u32[]{:S(2)}, u32[]{:S(2)}) collective-permute-start(bf16[224,896]{1,0:T(8,128)(2,1)} %bitcast.4), channel_id=1, source_target_pairs={{0,8},{2,10},{8,16},{10,18},{16,24},{18,26},{24,28},{26,30},{28,20... | collective-permute-start | bytes 1204232 | tf_op jit(solution)/shard_map/ppermute | solution.py:130
  3.9 11.4 %collective-permute-start.6 = (bf16[2,256,128]{2,1,0:T(8,128)(2,1)S(1)}, bf16[2,256,128]{2,1,0:T(8,128)(2,1)S(1)}, u32[]{:S(2)}, u32[]{:S(2)}) collective-permute-start(bf16[2,256,128]{2,1,0:T(8,128)(2,1)S(1)} %pad_maximum_fusion.refs_1_), channel_id=1, source_target_pairs={{2,4},{6,8},{10,12},{14,16},{18,20},{22,24},{26,28},{4,2},{8,6},{1... | collective-permute-start | bytes 393224 | tf_op jit(solution)/shard_map/ppermute | solution.py:96
  4.6 15.0 %collective-permute-start.5 = (bf16[2,256,128]{2,1,0:T(8,128)(2,1)S(1)}, bf16[2,256,128]{2,1,0:T(8,128)(2,1)S(1)}, u32[]{:S(2)}, u32[]{:S(2)}) collective-permute-start(bf16[2,256,128]{2,1,0:T(8,128)(2,1)S(1)} %pad_maximum_fusion.refs_1_), channel_id=1, source_target_pairs={{0,8},{2,10},{4,12},{6,14},{8,0},{10,2},{12,4},{14,6},{16,24},{18,... | collective-permute-start | bytes 393224 | tf_op jit(solution)/shard_map/ppermute | solution.py:34
  8.2 11.4 %collective-permute-start.4 = (bf16[2,256,128]{2,1,0:T(8,128)(2,1)S(1)}, bf16[2,256,128]{2,1,0:T(8,128)(2,1)S(1)}, u32[]{:S(2)}, u32[]{:S(2)}) collective-permute-start(bf16[2,256,128]{2,1,0:T(8,128)(2,1)S(1)} %pad_maximum_fusion.refs_1_), channel_id=1, source_target_pairs={{0,16},{2,18},{4,20},{6,22},{8,24},{10,26},{12,28},{14,30},{16,0},... | collective-permute-start | bytes 393224 | tf_op jit(solution)/shard_map/ppermute | solution.py:34
  10.8 1.0 %copy-start.1 = (bf16[256,896]{1,0:T(8,128)(2,1)S(1)}, bf16[256,896]{1,0:T(8,128)(2,1)}, u32[]{:S(2)}) copy-start(bf16[256,896]{1,0:T(8,128)(2,1)} %from_ref.1) | copy-start | bytes 1376260
  11.8 19.9 %copy-start = (bf16[896,224]{0,1:T(8,128)(2,1)S(1)}, bf16[896,224]{0,1:T(8,128)(2,1)}, u32[]{:S(2)}) copy-start(bf16[896,224]{0,1:T(8,128)(2,1)} %param.7) | copy-start | bytes 1204228
  13.9 5.7 %collective-permute-start.3 = (bf16[2,256,128]{2,1,0:T(8,128)(2,1)S(1)}, bf16[2,256,128]{2,1,0:T(8,128)(2,1)S(1)}, u32[]{:S(2)}, u32[]{:S(2)}) collective-permute-start(bf16[2,256,128]{2,1,0:T(8,128)(2,1)S(1)} %pad_maximum_fusion.refs_1_), channel_id=1, source_target_pairs={{0,4},{2,6},{4,0},{6,2},{8,12},{10,14},{12,8},{14,10},{16,20},{18,... | collective-permute-start | bytes 393224 | tf_op jit(solution)/shard_map/ppermute | solution.py:34
  15.3 4.2 %collective-permute-start.2 = (bf16[2,256,128]{2,1,0:T(8,128)(2,1)S(1)}, bf16[2,256,128]{2,1,0:T(8,128)(2,1)S(1)}, u32[]{:S(2)}, u32[]{:S(2)}) collective-permute-start(bf16[2,256,128]{2,1,0:T(8,128)(2,1)S(1)} %pad_maximum_fusion.refs_1_), channel_id=1, source_target_pairs={{0,2},{2,0},{4,6},{6,4},{8,10},{10,8},{12,14},{14,12},{16,18},{18,... | collective-permute-start | bytes 393224 | tf_op jit(solution)/shard_map/ppermute | solution.py:34
  19.6 9.7 %collective-permute-start.8 = (bf16[224,896]{1,0:T(8,128)(2,1)S(1)}, bf16[224,896]{1,0:T(8,128)(2,1)S(1)}, u32[]{:S(2)}, u32[]{:S(2)}) collective-permute-start(bf16[224,896]{1,0:T(8,128)(2,1)S(1)} %collective-permute-done.refs_2_.refs_3_.refs_4_), channel_id=1, source_target_pairs={{0,4},{2,6},{8,0},{10,2},{16,8},{18,10},{24,16},{26,18},{28,24},{3... | collective-permute-start | bytes 1204232 | tf_op jit(solution)/shard_map/ppermute | solution.py:130
  21.2 10.6 %collective-permute-start.9 = (bf16[224,896]{1,0:T(8,128)(2,1)S(1)}, bf16[224,896]{1,0:T(8,128)(2,1)S(1)}, u32[]{:S(2)}, u32[]{:S(2)}) collective-permute-start(bf16[224,896]{1,0:T(8,128)(2,1)S(1)} %collective-permute-done.1.refs_3_.refs_4_.refs_5_), channel_id=1, source_target_pairs={{0,8},{2,10},{8,16},{10,18},{16,24},{18,26},{24,28},{26,30},{28,20... | collective-permute-start | bytes 1204232 | tf_op jit(solution)/shard_map/ppermute | solution.py:130
  26.6 5.2 %collective-permute-start.7 = (bf16[256,896]{1,0:T(8,128)(2,1)S(1)}, bf16[256,896]{1,0:T(8,128)(2,1)S(1)}, u32[]{:S(2)}, u32[]{:S(2)}) collective-permute-start(bf16[256,896]{1,0:T(8,128)(2,1)S(1)} %shard_map.47.refs_0_), channel_id=1, source_target_pairs={{0,2},{2,0},{4,6},{6,4},{8,10},{10,8},{12,14},{14,12},{16,18},{18,... | collective-permute-start | bytes 1376264 | tf_op jit(solution)/shard_map/ppermute | solution.py:34
  29.2 9.6 %collective-permute-start.10 = (bf16[224,896]{1,0:T(8,128)(2,1)S(1)}, bf16[224,896]{1,0:T(8,128)(2,1)S(1)}, u32[]{:S(2)}, u32[]{:S(2)}) collective-permute-start(bf16[224,896]{1,0:T(8,128)(2,1)S(1)} %collective-permute-done.8.refs_4_.refs_5_.refs_6_), channel_id=1, source_target_pairs={{0,4},{2,6},{8,0},{10,2},{16,8},{18,10},{24,16},{26,18},{28,24},{3... | collective-permute-start | bytes 1204232 | tf_op jit(solution)/shard_map/ppermute | solution.py:130
  31.7 9.6 %collective-permute-start.11 = (bf16[224,896]{1,0:T(8,128)(2,1)S(1)}, bf16[224,896]{1,0:T(8,128)(2,1)S(1)}, u32[]{:S(2)}, u32[]{:S(2)}) collective-permute-start(bf16[224,896]{1,0:T(8,128)(2,1)S(1)} %collective-permute-done.9.refs_5_.refs_6_.refs_7_), channel_id=1, source_target_pairs={{0,8},{2,10},{8,16},{10,18},{16,24},{18,26},{24,28},{26,30},{28,20... | collective-permute-start | bytes 1204232 | tf_op jit(solution)/shard_map/ppermute | solution.py:130
  32.3 11.4 %collective-permute-start.12 = (bf16[224,256]{1,0:T(8,128)(2,1)S(1)}, bf16[224,256]{1,0:T(8,128)(2,1)S(1)}, u32[]{:S(2)}, u32[]{:S(2)}) collective-permute-start(bf16[224,256]{1,0:T(8,128)(2,1)S(1)} %get-tuple-element.41), channel_id=1, source_target_pairs={{0,1},{1,0},{2,3},{3,2},{4,5},{5,4},{6,7},{7,6},{8,9},{9,8},{10,11... | collective-permute-start | bytes 344072 | tf_op jit(solution)/shard_map/ppermute | solution.py:327
  33.9 9.8 %collective-permute-start.13 = (bf16[224,256]{1,0:T(8,128)(2,1)S(1)}, bf16[224,256]{1,0:T(8,128)(2,1)S(1)}, u32[]{:S(2)}, u32[]{:S(2)}) collective-permute-start(bf16[224,256]{1,0:T(8,128)(2,1)S(1)} %get-tuple-element.42), channel_id=1, source_target_pairs={{0,3},{1,2},{2,1},{3,0},{4,7},{5,6},{6,5},{7,4},{8,11},{9,10},{10,... | collective-permute-start | bytes 344072 | tf_op jit(solution)/shard_map/ppermute | solution.py:328
  42.1 10.4 %collective-permute-start.16 = (bf16[448,256]{1,0:T(8,128)(2,1)S(1)}, bf16[448,256]{1,0:T(8,128)(2,1)S(1)}, u32[]{:S(2)}, u32[]{:S(2)}) collective-permute-start(bf16[448,256]{1,0:T(8,128)(2,1)S(1)} %get-tuple-element.43), channel_id=1, source_target_pairs={{0,1},{1,0},{2,3},{3,2},{4,5},{5,4},{6,7},{7,6},{8,9},{9,8},{10,11... | collective-permute-start | bytes 688136 | tf_op jit(solution)/shard_map/ppermute | solution.py:327
  43.7 8.8 %collective-permute-start.17 = (bf16[448,256]{1,0:T(8,128)(2,1)S(1)}, bf16[448,256]{1,0:T(8,128)(2,1)S(1)}, u32[]{:S(2)}, u32[]{:S(2)}) collective-permute-start(bf16[448,256]{1,0:T(8,128)(2,1)S(1)} %get-tuple-element.44), channel_id=1, source_target_pairs={{0,3},{1,2},{2,1},{3,0},{4,7},{5,6},{6,5},{7,4},{8,11},{9,10},{10,... | collective-permute-start | bytes 688136 | tf_op jit(solution)/shard_map/ppermute | solution.py:328
  43.8 8.3 %collective-permute-start.15 = (bf16[112,896]{1,0:T(8,128)(2,1)S(1)}, bf16[112,896]{1,0:T(8,128)(2,1)S(1)}, u32[]{:S(2)}, u32[]{:S(2)}) collective-permute-start(bf16[112,896]{1,0:T(8,128)(2,1)S(1)} %slice.7), channel_id=1, source_target_pairs={{0,8},{2,10},{8,16},{10,18},{16,24},{18,26},{24,28},{26,30},{28,20... | collective-permute-start | bytes 602120 | tf_op jit(solution)/shard_map/ppermute | solution.py:130
  45.3 7.2 %collective-permute-start.14 = (bf16[112,896]{1,0:T(8,128)(2,1)S(1)}, bf16[112,896]{1,0:T(8,128)(2,1)S(1)}, u32[]{:S(2)}, u32[]{:S(2)}) collective-permute-start(bf16[112,896]{1,0:T(8,128)(2,1)S(1)} %slice.6), channel_id=1, source_target_pairs={{0,4},{2,6},{8,0},{10,2},{16,8},{18,10},{24,16},{26,18},{28,24},{3... | collective-permute-start | bytes 602120 | tf_op jit(solution)/shard_map/ppermute | solution.py:130
  53.0 3.2 %collective-permute-start.18 = (bf16[896,256]{1,0:T(8,128)(2,1)S(1)}, bf16[896,256]{1,0:T(8,128)(2,1)S(1)}, u32[]{:S(2)}, u32[]{:S(2)}) collective-permute-start(bf16[896,256]{1,0:T(8,128)(2,1)S(1)} %get-tuple-element.52), channel_id=1, source_target_pairs={{0,2},{2,0},{4,6},{6,4},{8,10},{10,8},{12,14},{14,12},{16,18},{18,... | collective-permute-start | bytes 1376264 | tf_op jit(solution)/shard_map/ppermute | solution.py:34
  53.5 5.6 %collective-permute-start.19 = (bf16[224,256]{1,0:T(8,128)(2,1)S(1)}, bf16[224,256]{1,0:T(8,128)(2,1)S(1)}, u32[]{:S(2)}, u32[]{:S(2)}) collective-permute-start(bf16[224,256]{1,0:T(8,128)(2,1)S(1)} %get-tuple-element.55), channel_id=1, source_target_pairs={{0,1},{1,0},{2,3},{3,2},{4,5},{5,4},{6,7},{7,6},{8,9},{9,8},{10,11... | collective-permute-start | bytes 344072 | tf_op jit(solution)/shard_map/ppermute | solution.py:327
  55.3 5.5 %collective-permute-start.20 = (bf16[224,256]{1,0:T(8,128)(2,1)S(1)}, bf16[224,256]{1,0:T(8,128)(2,1)S(1)}, u32[]{:S(2)}, u32[]{:S(2)}) collective-permute-start(bf16[224,256]{1,0:T(8,128)(2,1)S(1)} %get-tuple-element.56), channel_id=1, source_target_pairs={{0,3},{1,2},{2,1},{3,0},{4,7},{5,6},{6,5},{7,4},{8,11},{9,10},{10,... | collective-permute-start | bytes 344072 | tf_op jit(solution)/shard_map/ppermute | solution.py:328

commit v6 on v5

--- a/solution.py
+++ b/solution.py
@@ -9,6 +9,7 @@
 from jax.sharding import PartitionSpec as P
 
 HD = 128
+LANES = 128
 BLK = 256
 
 masked_score = -1e30
@@ -16,13 +17,13 @@
 in_vmem = pl.BlockSpec(memory_space=pltpu.VMEM)
 
 
-def call_kernel(body, out_shape, operands, scratch=()):
+def call_kernel(body, out_shape, operands, scratch=(), out_spec=in_vmem):
     many = isinstance(out_shape, (list, tuple))
     return pl.pallas_call(
         body,
         out_shape=out_shape,
         in_specs=[in_vmem] * len(operands),
-        out_specs=[in_vmem] * len(out_shape) if many else in_vmem,
+        out_specs=[out_spec] * len(out_shape) if many else out_spec,
         scratch_shapes=list(scratch),
         compiler_params=pltpu.CompilerParams(vmem_limit_bytes=vmem_limit),
         cost_estimate=pl.CostEstimate(flops=1, bytes_accessed=1, transcendentals=0),
@@ -165,30 +166,31 @@
     )
 
 
-def sent_body(first, width, offsets, *refs):
-    (mine_ref, theirs_ref), parts = refs[:2], grouped(refs[2:-3], offsets)
-    to_same_ref, to_other_ref, held = refs[-3:]
-    step = held.shape[0] // width
+def sent_body(first, offsets, fresh, *refs):
+    (mine_ref, theirs_ref), (to_same_ref, to_other_ref, held) = refs[:2], refs[-3:]
+    before_refs, parts = refs[2 : len(refs) - 3 - len(offsets)], refs[-3 - len(offsets) : -3]
     ranks = Ring().ranks(1 - lax.axis_index("head"), offsets)
-    for (belongs, rank), part in zip(ranks, parts):
-        for slot in range(width):
-
-            @pl.when(jnp.logical_and(belongs, rank == first + slot))
-            def _():
-                hold(held, slot * step, part)
-
-    to_same_ref[...] = times(held[...], mine_ref).astype(jnp.bfloat16)
-    to_other_ref[...] = times(held[...], theirs_ref).astype(jnp.bfloat16)
-
-
-def sent(rows, first, width, offsets, parts):
+    for (belongs, rank), ref in zip(ranks, parts):
+
+        @pl.when(jnp.logical_and(belongs, rank == first))
+        def _():
+            hold(held, 0, [ref])
+
+    for out_ref, before_ref in zip((to_same_ref, to_other_ref), before_refs):
+        out_ref[:fresh, :] = before_ref[...]
+    to_same_ref[fresh:, :] = times(held[...], mine_ref).astype(jnp.bfloat16)
+    to_other_ref[fresh:, :] = times(held[...], theirs_ref).astype(jnp.bfloat16)
+
+
+def sent(rows, first, offsets, parts, before=()):
     step, depth = parts[0].shape
-    shape = jax.ShapeDtypeStruct((width * step, rows[0].shape[0]), jnp.bfloat16)
+    fresh = before[0].shape[0] if before else 0
+    shape = jax.ShapeDtypeStruct((fresh + step, rows[0].shape[0]), jnp.bfloat16)
     return call_kernel(
-        functools.partial(sent_body, first, width, offsets),
+        functools.partial(sent_body, first, offsets, fresh),
         [shape, shape],
-        [*rows, *parts],
-        scratch=[pltpu.VMEM((width * step, depth), jnp.bfloat16)],
+        [*rows, *before, *parts],
+        scratch=[pltpu.VMEM((step, depth), jnp.bfloat16)],
     )
 
 
@@ -254,59 +256,124 @@
     )
 
 
-def total_body(offsets, widths, first, *refs):
+def summed(offsets, entries, keep_ref, from_core_ref, received, turned, alone):
     ring = Ring()
-    keep_ref, from_core_ref = refs[:2]
-    (*received, out_ref, turned) = refs[2:]
-    done_ref = received.pop(0) if first else None
-    slots = len(offsets) // 2
-    step = keep_ref.shape[0] // slots
+    step = 2 * keep_ref.shape[0] // len(offsets)
     core = lax.axis_index("seq") % 2
     ranks = ring.ranks(lax.axis_index("head"), offsets)
-    tokens = keep_ref.shape[1]
+    slot = jnp.int32(0)
+    for entry, same_ref, other_ref, at in zip(entries, *received):
+        slot = jnp.int32(0)
+        for offset, (belongs, rank) in zip(offsets, ranks):
+            here = jnp.logical_and(belongs, rank == entry)
+            slot = jnp.where(here, ring.side_and_slot(offset)[1], slot)
+        rows = pl.ds(pl.multiple_of(slot * step, 16), step)
+        there = slice(at * step, (at + 1) * step)
+        for where, kept_ref, ref in (
+            (core, keep_ref, same_ref),
+            (1 - core, from_core_ref, other_ref),
+        ):
+            both = kept_ref[rows, :].astype(jnp.float32) + ref[there, :].astype(jnp.float32)
+            start = where * step if alone else (2 * slot + where) * step
+            turned[pl.ds(pl.multiple_of(start, 16), step), :] = both.astype(jnp.bfloat16)
+    return slot
+
+
+def by_tokens(turned):
+    tokens = turned.shape[1]
     row = lax.broadcasted_iota(jnp.int32, (tokens, tokens), 0)
     column = lax.broadcasted_iota(jnp.int32, (tokens, tokens), 1)
     identity = jnp.where(row == column, 1.0, 0.0).astype(jnp.bfloat16)
-    if not first:
-        turned[...] = jnp.zeros(turned.shape, turned.dtype)
-    entry, slot = first, None
-    for same_ref, other_ref, width in zip(received[0::2], received[1::2], widths):
-        for at in range(width):
-            slot = jnp.int32(0)
-            for offset, (belongs, rank) in zip(offsets, ranks):
-                here = jnp.logical_and(belongs, rank == entry)
-                slot = jnp.where(here, ring.side_and_slot(offset)[1], slot)
-            entry += 1
-            rows = pl.ds(pl.multiple_of(slot * step, 16), step)
-            there = slice(at * step, (at + 1) * step)
-            for where, kept_ref, ref in (
-                (core, keep_ref, same_ref),
-                (1 - core, from_core_ref, other_ref),
-            ):
-                both = kept_ref[rows, :].astype(jnp.float32) + ref[there, :].astype(jnp.float32)
-                start = where * step if first else (2 * slot + where) * step
-                turned[pl.ds(pl.multiple_of(start, 16), step), :] = both.astype(jnp.bfloat16)
-    values = times(identity, turned).astype(jnp.bfloat16)
-    if not first:
-        out_ref[...] = values
-        return
-    out_ref[...] = done_ref[...]
-    for at in range(slots):
+    return times(identity, turned).astype(jnp.bfloat16)
+
+
+def total_body(offsets, widths, keep_ref, from_core_ref, *refs):
+    (*received, out_ref, turned) = refs
+    turned[...] = jnp.zeros(turned.shape, turned.dtype)
+    pairs = [
+        (same_ref, other_ref, at)
+        for same_ref, other_ref, width in zip(received[0::2], received[1::2], widths)
+        for at in range(width)
+    ]
+    entries = range(len(pairs))
+    summed(offsets, entries, keep_ref, from_core_ref, list(zip(*pairs)), turned, False)
+    out_ref[...] = by_tokens(turned)
+
+
+def total(keep, from_core, received, widths, offsets):
+    columns, rows = keep.shape
+    return call_kernel(
+        functools.partial(total_body, offsets, widths),
+        jax.ShapeDtypeStruct((rows, 2 * columns), jnp.bfloat16),
+        [keep, from_core, *received],
+        scratch=[pltpu.VMEM((2 * columns, rows), jnp.bfloat16)],
+    )
+
+
+def windows(slots, width):
+    answer = []
+    for slot in range(slots):
+        low, high = slot * width, (slot + 1) * width
+        answer.append((low, high, low // LANES * LANES, -(-high // LANES) * LANES))
+    return answer
+
+
+def finish_body(offsets, keep_ref, from_core_ref, done_ref, same_ref, other_ref, out_ref, turned, window, sems):
+    slots = len(offsets) // 2
+    places = windows(slots, turned.shape[0])
+    ring, head = Ring(), lax.axis_index("head")
+    slot = jnp.int32(0)
+    for offset, (belongs, rank) in zip(offsets, ring.ranks(head, offsets)):
+        here = jnp.logical_and(belongs, rank == slots - 1)
+        slot = jnp.where(here, ring.side_and_slot(offset)[1], slot)
+
+    def copies(left, right):
+        sides = [(0, left), (right, out_ref.shape[1])]
+        return [
+            pltpu.make_async_copy(done_ref.at[:, low:high], out_ref.at[:, low:high], sems.at[at])
+            for at, (low, high) in enumerate(sides)
+            if high > low
+        ]
+
+    for at, (_, _, left, right) in enumerate(places):
 
         @pl.when(slot == at)
         def _():
-            out_ref[:, 2 * at * step : 2 * (at + 1) * step] = values
-
-
-def total(keep, from_core, received, widths, offsets, done=None):
+            for copy in copies(left, right):
+                copy.start()
+
+    received = [[same_ref], [other_ref], [0]]
+    summed(offsets, [slots - 1], keep_ref, from_core_ref, received, turned, True)
+    values = by_tokens(turned)
+    for at, (low, high, left, right) in enumerate(places):
+
+        @pl.when(slot == at)
+        def _():
+            held = window.at[:, : right - left]
+            held[...] = done_ref[:, left:right]
+            window[:, low - left : high - left] = values
+            last_copy = pltpu.make_async_copy(held, out_ref.at[:, left:right], sems.at[2])
+            last_copy.start()
+            for copy in copies(left, right):
+                copy.wait()
+            last_copy.wait()
+
+
+def finish(keep, from_core, done, received, offsets):
     columns, rows = keep.shape
-    first = 0 if done is None else len(offsets) // 2 - sum(widths)
-    held = 2 * columns if done is None else 4 * columns // len(offsets)
+    slots = len(offsets) // 2
+    width = 2 * columns // slots
+    widest = max(right - left for _, _, left, right in windows(slots, width))
     return call_kernel(
-        functools.partial(total_body, offsets, widths, first),
+        functools.partial(finish_body, offsets),
         jax.ShapeDtypeStruct((rows, 2 * columns), jnp.bfloat16),
-        [keep, from_core, *([] if done is None else [done]), *received],
-        scratch=[pltpu.VMEM((held, rows), jnp.bfloat16)],
+        [keep, from_core, done, *received],
+        scratch=[
+            pltpu.VMEM((width, rows), jnp.bfloat16),
+            pltpu.VMEM((rows, widest), jnp.bfloat16),
+            pltpu.SemaphoreType.DMA((3,)),
+        ],
+        out_spec=pl.BlockSpec(memory_space=pl.ANY),
     )
 
 
@@ -337,11 +404,12 @@
     parts += pair
     attended = attend(queries, pieces)
     rows = [attended, flip(attended, 1)]
-    first = swap(sent(rows, 0, 1, offsets[:5], parts))
+    first = swap(sent(rows, 0, offsets[:5], parts))
     pair = [after(shard, attended) for shard in pair]
     pair = both_ways(*pair)
     parts += pair
-    product = sent(rows, 1, 2, offsets[:7], parts)
+    product = sent(rows, 1, offsets[:6], parts[:6])
+    product = sent(rows, 2, offsets[:7], parts, product)
     pair = [after(shard, (first, product)) for shard in pair]
     second = swap(product)
     before = kept(rows[1], offsets[:7], parts, jnp.bfloat16)
@@ -352,9 +420,11 @@
     rows, product = lax.optimization_barrier((rows, product))
     third = swap(product)
     keep = kept(rows[0], offsets, parts, jnp.float32)
-    from_core = flip(to_core, 1)
+    step = shard.shape[0]
+    pieces = [to_core[at : at + step] for at in range(0, to_core.shape[0], step)]
+    from_core = jnp.concatenate([flip(piece, 1) for piece in pieces], axis=0)
     done = total(keep, from_core, [*first, *second], widths[:2], offsets)
-    return total(keep, from_core, third, widths[2:], offsets, done)
+    return finish(keep, from_core, done, third, offsets)
 
 
 def project_gathered(attended, out_weight):

time: 62.7 us -> 62.5 us (level)
  waiting for transfers between devices: 25.3 us -> 24.6 us
    ppermute x3, waiting for transfers between devices: 2.12 us -> 0.57 us  [swap(): lax.ppermute(same, 'head', [(0, 1), (1, 0)])]
    ppermute x6 -> x9, waiting for transfers between devices: 4.22 us -> 5.19 us  [flip(): return lax.ppermute(value, 'seq', pairs)]
    ppermute x6 -> x9, starting transfers between devices: 8.15 us -> 8.78 us  [flip(): return lax.ppermute(value, 'seq', pairs)]
    pallas_call x9 -> x10, Pallas kernels: 9.97 us -> 10.1 us  [call_kernel(): pl.pallas_call(body, out_shape=out_shape, in_specs=[in_vmem] * len(operan...]
  transfers between devices with their start and end apart: 21 -> 24, of which waited for: 9 -> 10; matrix products, arithmetic and copies ran while one was open for 1% -> 2% of each run, Pallas kernels for 13% -> 13%
where the time goes in v6:
time: 62.5 us; the launch traced here: 62.3 us
  starting transfers between devices  25.4 us (41%)
  waiting for transfers between devices  24.6 us (39%)
  Pallas kernels  10.1 us (16%)
  local copies, waits for them, and re-layouts  1.13 us (2%)
  other arithmetic  0.88 us (1%)
    ppermute x8, waiting for transfers between devices, shift(): return lax.ppermute(value, 'seq', pairs)  17.3 us
    ppermute x8, starting transfers between devices, shift(): return lax.ppermute(value, 'seq', pairs)  11 us
    pallas_call x10, Pallas kernels, call_kernel(): pl.pallas_call(body, out_shape=out_shape, in_specs=[in_vmem] * len(operan...  10.1 us
    ppermute x9, starting transfers between devices, flip(): return lax.ppermute(value, 'seq', pairs)  8.78 us
    ppermute x9, waiting for transfers between devices, flip(): return lax.ppermute(value, 'seq', pairs)  5.19 us
    ppermute x3, starting transfers between devices, swap(): lax.ppermute(same, 'head', [(0, 1), (1, 0)])  4.68 us
    ppermute x3, waiting for transfers between devices, swap(): lax.ppermute(other, ('seq', 'head'), crossed)  1.51 us
  transfers between devices with their start and end apart: 24, of which 10 were waited for; matrix products, arithmetic and copies ran while one was open for 2% of the time, Pallas kernels for 13%

profile of v6, /device:TPU:0, one launch (start us, length us, event | category | flops | bytes accessed | tf_op | source)
XLA Modules:
  0.0 62.3 jit_solution(6345457403348756500)
XLA Ops:
  0.0 2.9 %collective-permute-start = (bf16[224,896]{1,0:T(8,128)(2,1)}, bf16[224,896]{1,0:T(8,128)(2,1)S(1)}, u32[]{:S(2)}, u32[]{:S(2)}) collective-permute-start(bf16[224,896]{1,0:T(8,128)(2,1)} %bitcast.3), channel_id=1, source_target_pairs={{0,4},{2,6},{8,0},{10,2},{16,8},{18,10},{24,16},{26,18},{28,24},{3... | collective-permute-start | bytes 1204232 | tf_op jit(solution)/shard_map/ppermute | solution.py:131
  3.0 0.9 %pad_maximum_fusion.refs_1_ = bf16[2,256,128]{2,1,0:T(8,128)(2,1)S(1)} fusion(bf16[1,256,128]{2,1,0:T(8,128)(2,1)} %bitcast.11, bf16[1,256,128]{2,1,0:T(8,128)(2,1)} %bitcast.12), kind=kLoop, calls=%fused_computation | loop fusion | flops 65536 | bytes 262144 | tf_op jit(solution)/shard_map/stack | solution.py:440
  3.9 0.7 %collective-permute-start.6 = (bf16[2,256,128]{2,1,0:T(8,128)(2,1)S(1)}, bf16[2,256,128]{2,1,0:T(8,128)(2,1)S(1)}, u32[]{:S(2)}, u32[]{:S(2)}) collective-permute-start(bf16[2,256,128]{2,1,0:T(8,128)(2,1)S(1)} %pad_maximum_fusion.refs_1_), channel_id=1, source_target_pairs={{2,4},{6,8},{10,12},{14,16},{18,20},{22,24},{26,28},{4,2},{8,6},{1... | collective-permute-start | bytes 393224 | tf_op jit(solution)/shard_map/ppermute | solution.py:97
  4.6 3.6 %collective-permute-start.5 = (bf16[2,256,128]{2,1,0:T(8,128)(2,1)S(1)}, bf16[2,256,128]{2,1,0:T(8,128)(2,1)S(1)}, u32[]{:S(2)}, u32[]{:S(2)}) collective-permute-start(bf16[2,256,128]{2,1,0:T(8,128)(2,1)S(1)} %pad_maximum_fusion.refs_1_), channel_id=1, source_target_pairs={{0,8},{2,10},{4,12},{6,14},{8,0},{10,2},{12,4},{14,6},{16,24},{18,... | collective-permute-start | bytes 393224 | tf_op jit(solution)/shard_map/ppermute | solution.py:35
  8.2 2.6 %collective-permute-start.4 = (bf16[2,256,128]{2,1,0:T(8,128)(2,1)S(1)}, bf16[2,256,128]{2,1,0:T(8,128)(2,1)S(1)}, u32[]{:S(2)}, u32[]{:S(2)}) collective-permute-start(bf16[2,256,128]{2,1,0:T(8,128)(2,1)S(1)} %pad_maximum_fusion.refs_1_), channel_id=1, source_target_pairs={{0,16},{2,18},{4,20},{6,22},{8,24},{10,26},{12,28},{14,30},{16,0},... | collective-permute-start | bytes 393224 | tf_op jit(solution)/shard_map/ppermute | solution.py:35
  10.8 1.0 %copy-done.1 = bf16[256,896]{1,0:T(8,128)(2,1)S(1)} copy-done((bf16[256,896]{1,0:T(8,128)(2,1)S(1)}, bf16[256,896]{1,0:T(8,128)(2,1)}, u32[]{:S(2)}) %copy-start.1) | copy-done | bytes 458776
  11.8 2.1 %collective-permute-done.refs_2_.refs_3_.refs_5_.refs_4_ = bf16[224,896]{1,0:T(8,128)(2,1)S(1)} collective-permute-done((bf16[224,896]{1,0:T(8,128)(2,1)}, bf16[224,896]{1,0:T(8,128)(2,1)S(1)}, u32[]{:S(2)}, u32[]{:S(2)}) %collective-permute-start) | collective-permute-done | bytes 401440 | tf_op jit(solution)/shard_map/ppermute | solution.py:131
  13.9 1.4 %collective-permute-start.3 = (bf16[2,256,128]{2,1,0:T(8,128)(2,1)S(1)}, bf16[2,256,128]{2,1,0:T(8,128)(2,1)S(1)}, u32[]{:S(2)}, u32[]{:S(2)}) collective-permute-start(bf16[2,256,128]{2,1,0:T(8,128)(2,1)S(1)} %pad_maximum_fusion.refs_1_), channel_id=1, source_target_pairs={{0,4},{2,6},{4,0},{6,2},{8,12},{10,14},{12,8},{14,10},{16,20},{18,... | collective-permute-start | bytes 393224 | tf_op jit(solution)/shard_map/ppermute | solution.py:35
  15.3 4.2 %collective-permute-done.5.refs_5_ = bf16[2,256,128]{2,1,0:T(8,128)(2,1)S(1)} collective-permute-done((bf16[2,256,128]{2,1,0:T(8,128)(2,1)S(1)}, bf16[2,256,128]{2,1,0:T(8,128)(2,1)S(1)}, u32[]{:S(2)}, u32[]{:S(2)}) %collective-permute-start.5) | collective-permute-done | bytes 131104 | tf_op jit(solution)/shard_map/ppermute | solution.py:35
  19.6 1.6 %collective-permute-start.8 = (bf16[224,896]{1,0:T(8,128)(2,1)S(1)}, bf16[224,896]{1,0:T(8,128)(2,1)S(1)}, u32[]{:S(2)}, u32[]{:S(2)}) collective-permute-start(bf16[224,896]{1,0:T(8,128)(2,1)S(1)} %collective-permute-done.refs_2_.refs_3_.refs_5_.refs_4_), channel_id=1, source_target_pairs={{0,4},{2,6},{8,0},{10,2},{16,8},{18,10},{24,16},{26,18},{28,24},{3... | collective-permute-start | bytes 1204232 | tf_op jit(solution)/shard_map/ppermute | solution.py:131
  21.2 1.3 %collective-permute-start.9 = (bf16[224,896]{1,0:T(8,128)(2,1)S(1)}, bf16[224,896]{1,0:T(8,128)(2,1)S(1)}, u32[]{:S(2)}, u32[]{:S(2)}) collective-permute-start(bf16[224,896]{1,0:T(8,128)(2,1)S(1)} %collective-permute-done.1.refs_3_.refs_4_.refs_6_.refs_5_), channel_id=1, source_target_pairs={{0,8},{2,10},{8,16},{10,18},{16,24},{18,26},{24,28},{26,30},{28,20... | collective-permute-start | bytes 1204232 | tf_op jit(solution)/shard_map/ppermute | solution.py:131
  22.4 4.1 %shard_map.47.refs_0_ = bf16[256,896]{1,0:T(8,128)(2,1)S(1)} custom-call(bf16[256,896]{1,0:T(8,128)(2,1)S(1)} %shard_map.46.refs_0_, bf16[2,256,128]{2,1,0:T(8,128)(2,1)S(1)} %pad_maximum_fusion.refs_1_, bf16[2,256,128]{2,1,0:T(8,128)(2,1)S(1)} %collective-permute-done.2.refs_2_, bf16[2,256,128]{2,1,0:T(8,128)(2,1)S(1)} %collective-permute-done.3.refs_3_, ...), custom_call_target="tpu_custom_call" | custom-call | flops 1 | bytes 1 | tf_op jit(solution)/shard_map/pallas_call | solution.py:22
  26.6 2.6 %collective-permute-done.8.refs_4_.refs_5_.refs_7_.refs_6_ = bf16[224,896]{1,0:T(8,128)(2,1)S(1)} collective-permute-done((bf16[224,896]{1,0:T(8,128)(2,1)S(1)}, bf16[224,896]{1,0:T(8,128)(2,1)S(1)}, u32[]{:S(2)}, u32[]{:S(2)}) %collective-permute-start.8) | collective-permute-done | bytes 401440 | tf_op jit(solution)/shard_map/ppermute | solution.py:131
  29.2 2.5 %collective-permute-start.10 = (bf16[224,896]{1,0:T(8,128)(2,1)S(1)}, bf16[224,896]{1,0:T(8,128)(2,1)S(1)}, u32[]{:S(2)}, u32[]{:S(2)}) collective-permute-start(bf16[224,896]{1,0:T(8,128)(2,1)S(1)} %collective-permute-done.8.refs_4_.refs_5_.refs_7_.refs_6_), channel_id=1, source_target_pairs={{0,4},{2,6},{8,0},{10,2},{16,8},{18,10},{24,16},{26,18},{28,24},{3... | collective-permute-start | bytes 1204232 | tf_op jit(solution)/shard_map/ppermute | solution.py:131
  31.7 0.6 shard_map.49
  32.3 1.6 %collective-permute-start.12 = (bf16[224,256]{1,0:T(8,128)(2,1)S(1)}, bf16[224,256]{1,0:T(8,128)(2,1)S(1)}, u32[]{:S(2)}, u32[]{:S(2)}) collective-permute-start(bf16[224,256]{1,0:T(8,128)(2,1)S(1)} %get-tuple-element.43), channel_id=1, source_target_pairs={{0,1},{1,0},{2,3},{3,2},{4,5},{5,4},{6,7},{7,6},{8,9},{9,8},{10,11... | collective-permute-start | bytes 344072 | tf_op jit(solution)/shard_map/ppermute | solution.py:394
  33.9 4.9 %collective-permute-done.10.refs_6_.refs_7_.refs_9_.refs_8_ = bf16[224,896]{1,0:T(8,128)(2,1)S(1)} collective-permute-done((bf16[224,896]{1,0:T(8,128)(2,1)S(1)}, bf16[224,896]{1,0:T(8,128)(2,1)S(1)}, u32[]{:S(2)}, u32[]{:S(2)}) %collective-permute-start.10) | collective-permute-done | bytes 401440 | tf_op jit(solution)/shard_map/ppermute | solution.py:131
  38.9 0.5 shard_map.50
  39.4 2.0 %collective-permute-done.11.refs_7_.refs_10_.refs_9_ = bf16[224,896]{1,0:T(8,128)(2,1)S(1)} collective-permute-done((bf16[224,896]{1,0:T(8,128)(2,1)S(1)}, bf16[224,896]{1,0:T(8,128)(2,1)S(1)}, u32[]{:S(2)}, u32[]{:S(2)}) %collective-permute-start.11) | collective-permute-done | bytes 401440 | tf_op jit(solution)/shard_map/ppermute | solution.py:131
  41.4 0.5 shard_map.51
  41.9 1.6 %collective-permute-start.16 = (bf16[448,256]{1,0:T(8,128)(2,1)S(1)}, bf16[448,256]{1,0:T(8,128)(2,1)S(1)}, u32[]{:S(2)}, u32[]{:S(2)}) collective-permute-start(bf16[448,256]{1,0:T(8,128)(2,1)S(1)} %get-tuple-element.47), channel_id=1, source_target_pairs={{0,1},{1,0},{2,3},{3,2},{4,5},{5,4},{6,7},{7,6},{8,9},{9,8},{10,11... | collective-permute-start | bytes 688136 | tf_op jit(solution)/shard_map/ppermute | solution.py:394
  43.5 2.1 %collective-permute-start.15 = (bf16[112,896]{1,0:T(8,128)(2,1)S(1)}, bf16[112,896]{1,0:T(8,128)(2,1)S(1)}, u32[]{:S(2)}, u32[]{:S(2)}) collective-permute-start(bf16[112,896]{1,0:T(8,128)(2,1)S(1)} %slice.19), channel_id=1, source_target_pairs={{0,8},{2,10},{8,16},{10,18},{16,24},{18,26},{24,28},{26,30},{28,20... | collective-permute-start | bytes 602120 | tf_op jit(solution)/shard_map/ppermute | solution.py:131
  46.1 1.0 %shard_map.48.refs_2_ = bf16[896,256]{1,0:T(8,128)(2,1)S(1)} custom-call(bf16[256,896]{1,0:T(8,128)(2,1)S(1)} %collective-permute-done.7.refs_0_.refs_1_, bf16[224,896]{1,0:T(8,128)(2,1)S(1)} %bitcast.8, bf16[224,896]{1,0:T(8,128)(2,1)S(1)} %collective-permute-done.refs_2_.refs_3_.refs_5_.refs_4_, ...), custom_call_target="tpu_custom_call" | custom-call | flops 1 | bytes 1 | tf_op jit(solution)/shard_map/pallas_call | solution.py:22
  47.1 4.7 %collective-permute-done.15.refs_11_.refs_9_ = bf16[112,896]{1,0:T(8,128)(2,1)S(1)} collective-permute-done((bf16[112,896]{1,0:T(8,128)(2,1)S(1)}, bf16[112,896]{1,0:T(8,128)(2,1)S(1)}, u32[]{:S(2)}, u32[]{:S(2)}) %collective-permute-start.15) | collective-permute-done | bytes 200736 | tf_op jit(solution)/shard_map/ppermute | solution.py:131
  51.8 1.0 %collective-permute-done.14.refs_10_.refs_8_ = bf16[112,896]{1,0:T(8,128)(2,1)S(1)} collective-permute-done((bf16[112,896]{1,0:T(8,128)(2,1)S(1)}, bf16[112,896]{1,0:T(8,128)(2,1)S(1)}, u32[]{:S(2)}, u32[]{:S(2)}) %collective-permute-start.14) | collective-permute-done | bytes 200736 | tf_op jit(solution)/shard_map/ppermute | solution.py:131
  53.6 1.5 %collective-permute-start.22 = (bf16[224,256]{1,0:T(8,128)(2,1)S(1)}, bf16[224,256]{1,0:T(8,128)(2,1)S(1)}, u32[]{:S(2)}, u32[]{:S(2)}) collective-permute-start(bf16[224,256]{1,0:T(8,128)(2,1)S(1)} %get-tuple-element.59), channel_id=1, source_target_pairs={{0,1},{1,0},{2,3},{3,2},{4,5},{5,4},{6,7},{7,6},{8,9},{9,8},{10,11... | collective-permute-start | bytes 344072 | tf_op jit(solution)/shard_map/ppermute | solution.py:394
  55.9 0.9 %shard_map.53.keep_ref = f32[896,256]{1,0:T(8,128)S(1)} custom-call(bf16[256,896]{1,0:T(8,128)(2,1)S(1)} %shard_map.47.refs_0_, bf16[224,896]{1,0:T(8,128)(2,1)S(1)} %bitcast.10, bf16[224,896]{1,0:T(8,128)(2,1)S(1)} %collective-permute-done.refs_2_.refs_3_.refs_5_.refs_4_, bf16[224,896]{1,0:T(8,128)(2,1)S(1)} %collective-permute-done.1.refs_3_.refs_4_.refs_6_.refs_5_, ...), custom_call_target="tpu_custom_call" | custom-call | flops 1 | bytes 1 | tf_op jit(solution)/shard_map/pallas_call | solution.py:22
  57.3 1.0 %collective-permute-done.19 = bf16[224,256]{1,0:T(8,128)(2,1)S(1)} collective-permute-done((bf16[224,256]{1,0:T(8,128)(2,1)S(1)}, bf16[224,256]{1,0:T(8,128)(2,1)S(1)}, u32[]{:S(2)}, u32[]{:S(2)}) %collective-permute-start.19) | collective-permute-done | bytes 114720 | tf_op jit(solution)/shard_map/ppermute | solution.py:35
  58.3 0.7 %shard_map.54.done_ref = bf16[256,1792]{1,0:T(8,128)(2,1)S(1)} custom-call(f32[896,256]{1,0:T(8,128)S(1)} %shard_map.53.keep_ref, bf16[896,256]{1,0:T(8,128)(2,1)S(1)} %constant_dynamic-update-slice_fusion.from_core_ref, bf16[224,256]{1,0:T(8,128)(2,1)S(1)} %collective-permute-done.12.refs_0_, bf16[224,256]{1,0:T(8,128)(2,1)S(1)} %collective-permute-done.13.refs_1_, ...), custom_call_target="tpu_custom_call" | custom-call | flops 1 | bytes 1 | tf_op jit(solution)/shard_map/pallas_call | solution.py:22
  59.0 0.6 collective-permute-done.22.same_ref
  59.6 1.5 %collective-permute-done.23.other_ref = bf16[224,256]{1,0:T(8,128)(2,1)S(1)} collective-permute-done((bf16[224,256]{1,0:T(8,128)(2,1)S(1)}, bf16[224,256]{1,0:T(8,128)(2,1)S(1)}, u32[]{:S(2)}, u32[]{:S(2)}) %collective-permute-start.23) | collective-permute-done | bytes 114720 | tf_op jit(solution)/shard_map/ppermute | solution.py:395
  61.1 1.2 %shard_map.55 = bf16[256,1792]{1,0:T(8,128)(2,1)} custom-call(f32[896,256]{1,0:T(8,128)S(1)} %shard_map.53.keep_ref, bf16[896,256]{1,0:T(8,128)(2,1)S(1)} %constant_dynamic-update-slice_fusion.from_core_ref, bf16[256,1792]{1,0:T(8,128)(2,1)S(1)} %shard_map.54.done_ref, bf16[224,256]{1,0:T(8,128)(2,1)S(1)} %collective-permute-done.22.same_ref, ...), custom_call_target="tpu_custom_call" | custom-call | flops 1 | bytes 1 | tf_op jit(solution)/shard_map/pallas_call | solution.py:22
  (38 shorter events, 2.7 us)
Async XLA Ops:
  0.0 13.9 %collective-permute-start = (bf16[224,896]{1,0:T(8,128)(2,1)}, bf16[224,896]{1,0:T(8,128)(2,1)S(1)}, u32[]{:S(2)}, u32[]{:S(2)}) collective-permute-start(bf16[224,896]{1,0:T(8,128)(2,1)} %bitcast.3), channel_id=1, source_target_pairs={{0,4},{2,6},{8,0},{10,2},{16,8},{18,10},{24,16},{26,18},{28,24},{3... | collective-permute-start | bytes 1204232 | tf_op jit(solution)/shard_map/ppermute | solution.py:131
  2.9 16.6 %collective-permute-start.1 = (bf16[224,896]{1,0:T(8,128)(2,1)}, bf16[224,896]{1,0:T(8,128)(2,1)S(1)}, u32[]{:S(2)}, u32[]{:S(2)}) collective-permute-start(bf16[224,896]{1,0:T(8,128)(2,1)} %bitcast.4), channel_id=1, source_target_pairs={{0,8},{2,10},{8,16},{10,18},{16,24},{18,26},{24,28},{26,30},{28,20... | collective-permute-start | bytes 1204232 | tf_op jit(solution)/shard_map/ppermute | solution.py:131
  3.9 11.4 %collective-permute-start.6 = (bf16[2,256,128]{2,1,0:T(8,128)(2,1)S(1)}, bf16[2,256,128]{2,1,0:T(8,128)(2,1)S(1)}, u32[]{:S(2)}, u32[]{:S(2)}) collective-permute-start(bf16[2,256,128]{2,1,0:T(8,128)(2,1)S(1)} %pad_maximum_fusion.refs_1_), channel_id=1, source_target_pairs={{2,4},{6,8},{10,12},{14,16},{18,20},{22,24},{26,28},{4,2},{8,6},{1... | collective-permute-start | bytes 393224 | tf_op jit(solution)/shard_map/ppermute | solution.py:97
  4.6 15.0 %collective-permute-start.5 = (bf16[2,256,128]{2,1,0:T(8,128)(2,1)S(1)}, bf16[2,256,128]{2,1,0:T(8,128)(2,1)S(1)}, u32[]{:S(2)}, u32[]{:S(2)}) collective-permute-start(bf16[2,256,128]{2,1,0:T(8,128)(2,1)S(1)} %pad_maximum_fusion.refs_1_), channel_id=1, source_target_pairs={{0,8},{2,10},{4,12},{6,14},{8,0},{10,2},{12,4},{14,6},{16,24},{18,... | collective-permute-start | bytes 393224 | tf_op jit(solution)/shard_map/ppermute | solution.py:35
  8.2 11.4 %collective-permute-start.4 = (bf16[2,256,128]{2,1,0:T(8,128)(2,1)S(1)}, bf16[2,256,128]{2,1,0:T(8,128)(2,1)S(1)}, u32[]{:S(2)}, u32[]{:S(2)}) collective-permute-start(bf16[2,256,128]{2,1,0:T(8,128)(2,1)S(1)} %pad_maximum_fusion.refs_1_), channel_id=1, source_target_pairs={{0,16},{2,18},{4,20},{6,22},{8,24},{10,26},{12,28},{14,30},{16,0},... | collective-permute-start | bytes 393224 | tf_op jit(solution)/shard_map/ppermute | solution.py:35
  10.8 1.0 %copy-start.1 = (bf16[256,896]{1,0:T(8,128)(2,1)S(1)}, bf16[256,896]{1,0:T(8,128)(2,1)}, u32[]{:S(2)}) copy-start(bf16[256,896]{1,0:T(8,128)(2,1)} %from_ref.1) | copy-start | bytes 1376260
  11.8 19.9 %copy-start = (bf16[896,224]{0,1:T(8,128)(2,1)S(1)}, bf16[896,224]{0,1:T(8,128)(2,1)}, u32[]{:S(2)}) copy-start(bf16[896,224]{0,1:T(8,128)(2,1)} %param.7) | copy-start | bytes 1204228
  13.9 5.7 %collective-permute-start.3 = (bf16[2,256,128]{2,1,0:T(8,128)(2,1)S(1)}, bf16[2,256,128]{2,1,0:T(8,128)(2,1)S(1)}, u32[]{:S(2)}, u32[]{:S(2)}) collective-permute-start(bf16[2,256,128]{2,1,0:T(8,128)(2,1)S(1)} %pad_maximum_fusion.refs_1_), channel_id=1, source_target_pairs={{0,4},{2,6},{4,0},{6,2},{8,12},{10,14},{12,8},{14,10},{16,20},{18,... | collective-permute-start | bytes 393224 | tf_op jit(solution)/shard_map/ppermute | solution.py:35
  15.3 4.2 %collective-permute-start.2 = (bf16[2,256,128]{2,1,0:T(8,128)(2,1)S(1)}, bf16[2,256,128]{2,1,0:T(8,128)(2,1)S(1)}, u32[]{:S(2)}, u32[]{:S(2)}) collective-permute-start(bf16[2,256,128]{2,1,0:T(8,128)(2,1)S(1)} %pad_maximum_fusion.refs_1_), channel_id=1, source_target_pairs={{0,2},{2,0},{4,6},{6,4},{8,10},{10,8},{12,14},{14,12},{16,18},{18,... | collective-permute-start | bytes 393224 | tf_op jit(solution)/shard_map/ppermute | solution.py:35
  19.6 9.7 %collective-permute-start.8 = (bf16[224,896]{1,0:T(8,128)(2,1)S(1)}, bf16[224,896]{1,0:T(8,128)(2,1)S(1)}, u32[]{:S(2)}, u32[]{:S(2)}) collective-permute-start(bf16[224,896]{1,0:T(8,128)(2,1)S(1)} %collective-permute-done.refs_2_.refs_3_.refs_5_.refs_4_), channel_id=1, source_target_pairs={{0,4},{2,6},{8,0},{10,2},{16,8},{18,10},{24,16},{26,18},{28,24},{3... | collective-permute-start | bytes 1204232 | tf_op jit(solution)/shard_map/ppermute | solution.py:131
  21.2 10.6 %collective-permute-start.9 = (bf16[224,896]{1,0:T(8,128)(2,1)S(1)}, bf16[224,896]{1,0:T(8,128)(2,1)S(1)}, u32[]{:S(2)}, u32[]{:S(2)}) collective-permute-start(bf16[224,896]{1,0:T(8,128)(2,1)S(1)} %collective-permute-done.1.refs_3_.refs_4_.refs_6_.refs_5_), channel_id=1, source_target_pairs={{0,8},{2,10},{8,16},{10,18},{16,24},{18,26},{24,28},{26,30},{28,20... | collective-permute-start | bytes 1204232 | tf_op jit(solution)/shard_map/ppermute | solution.py:131
  26.6 5.2 %collective-permute-start.7 = (bf16[256,896]{1,0:T(8,128)(2,1)S(1)}, bf16[256,896]{1,0:T(8,128)(2,1)S(1)}, u32[]{:S(2)}, u32[]{:S(2)}) collective-permute-start(bf16[256,896]{1,0:T(8,128)(2,1)S(1)} %shard_map.47.refs_0_), channel_id=1, source_target_pairs={{0,2},{2,0},{4,6},{6,4},{8,10},{10,8},{12,14},{14,12},{16,18},{18,... | collective-permute-start | bytes 1376264 | tf_op jit(solution)/shard_map/ppermute | solution.py:35
  29.2 9.6 %collective-permute-start.10 = (bf16[224,896]{1,0:T(8,128)(2,1)S(1)}, bf16[224,896]{1,0:T(8,128)(2,1)S(1)}, u32[]{:S(2)}, u32[]{:S(2)}) collective-permute-start(bf16[224,896]{1,0:T(8,128)(2,1)S(1)} %collective-permute-done.8.refs_4_.refs_5_.refs_7_.refs_6_), channel_id=1, source_target_pairs={{0,4},{2,6},{8,0},{10,2},{16,8},{18,10},{24,16},{26,18},{28,24},{3... | collective-permute-start | bytes 1204232 | tf_op jit(solution)/shard_map/ppermute | solution.py:131
  31.7 9.6 %collective-permute-start.11 = (bf16[224,896]{1,0:T(8,128)(2,1)S(1)}, bf16[224,896]{1,0:T(8,128)(2,1)S(1)}, u32[]{:S(2)}, u32[]{:S(2)}) collective-permute-start(bf16[224,896]{1,0:T(8,128)(2,1)S(1)} %collective-permute-done.9.refs_5_.refs_6_.refs_8_.refs_7_), channel_id=1, source_target_pairs={{0,8},{2,10},{8,16},{10,18},{16,24},{18,26},{24,28},{26,30},{28,20... | collective-permute-start | bytes 1204232 | tf_op jit(solution)/shard_map/ppermute | solution.py:131
  32.3 11.1 %collective-permute-start.12 = (bf16[224,256]{1,0:T(8,128)(2,1)S(1)}, bf16[224,256]{1,0:T(8,128)(2,1)S(1)}, u32[]{:S(2)}, u32[]{:S(2)}) collective-permute-start(bf16[224,256]{1,0:T(8,128)(2,1)S(1)} %get-tuple-element.43), channel_id=1, source_target_pairs={{0,1},{1,0},{2,3},{3,2},{4,5},{5,4},{6,7},{7,6},{8,9},{9,8},{10,11... | collective-permute-start | bytes 344072 | tf_op jit(solution)/shard_map/ppermute | solution.py:394
  33.9 9.6 %collective-permute-start.13 = (bf16[224,256]{1,0:T(8,128)(2,1)S(1)}, bf16[224,256]{1,0:T(8,128)(2,1)S(1)}, u32[]{:S(2)}, u32[]{:S(2)}) collective-permute-start(bf16[224,256]{1,0:T(8,128)(2,1)S(1)} %get-tuple-element.44), channel_id=1, source_target_pairs={{0,3},{1,2},{2,1},{3,0},{4,7},{5,6},{6,5},{7,4},{8,11},{9,10},{10,... | collective-permute-start | bytes 344072 | tf_op jit(solution)/shard_map/ppermute | solution.py:395
  41.9 11.0 %collective-permute-start.16 = (bf16[448,256]{1,0:T(8,128)(2,1)S(1)}, bf16[448,256]{1,0:T(8,128)(2,1)S(1)}, u32[]{:S(2)}, u32[]{:S(2)}) collective-permute-start(bf16[448,256]{1,0:T(8,128)(2,1)S(1)} %get-tuple-element.47), channel_id=1, source_target_pairs={{0,1},{1,0},{2,3},{3,2},{4,5},{5,4},{6,7},{7,6},{8,9},{9,8},{10,11... | collective-permute-start | bytes 688136 | tf_op jit(solution)/shard_map/ppermute | solution.py:394
  43.5 9.4 %collective-permute-start.17 = (bf16[448,256]{1,0:T(8,128)(2,1)S(1)}, bf16[448,256]{1,0:T(8,128)(2,1)S(1)}, u32[]{:S(2)}, u32[]{:S(2)}) collective-permute-start(bf16[448,256]{1,0:T(8,128)(2,1)S(1)} %get-tuple-element.48), channel_id=1, source_target_pairs={{0,3},{1,2},{2,1},{3,0},{4,7},{5,6},{6,5},{7,4},{8,11},{9,10},{10,... | collective-permute-start | bytes 688136 | tf_op jit(solution)/shard_map/ppermute | solution.py:395
  43.5 8.3 %collective-permute-start.15 = (bf16[112,896]{1,0:T(8,128)(2,1)S(1)}, bf16[112,896]{1,0:T(8,128)(2,1)S(1)}, u32[]{:S(2)}, u32[]{:S(2)}) collective-permute-start(bf16[112,896]{1,0:T(8,128)(2,1)S(1)} %slice.19), channel_id=1, source_target_pairs={{0,8},{2,10},{8,16},{10,18},{16,24},{18,26},{24,28},{26,30},{28,20... | collective-permute-start | bytes 602120 | tf_op jit(solution)/shard_map/ppermute | solution.py:131
  45.7 7.2 %collective-permute-start.14 = (bf16[112,896]{1,0:T(8,128)(2,1)S(1)}, bf16[112,896]{1,0:T(8,128)(2,1)S(1)}, u32[]{:S(2)}, u32[]{:S(2)}) collective-permute-start(bf16[112,896]{1,0:T(8,128)(2,1)S(1)} %slice.18), channel_id=1, source_target_pairs={{0,4},{2,6},{8,0},{10,2},{16,8},{18,10},{24,16},{26,18},{28,24},{3... | collective-permute-start | bytes 602120 | tf_op jit(solution)/shard_map/ppermute | solution.py:131
  53.4 3.4 %collective-permute-start.18 = (bf16[224,256]{1,0:T(8,128)(2,1)S(1)}, bf16[224,256]{1,0:T(8,128)(2,1)S(1)}, u32[]{:S(2)}, u32[]{:S(2)}) collective-permute-start(bf16[224,256]{1,0:T(8,128)(2,1)S(1)} %get-tuple-element.64), channel_id=1, source_target_pairs={{0,2},{2,0},{4,6},{6,4},{8,10},{10,8},{12,14},{14,12},{16,18},{18,... | collective-permute-start | bytes 344072 | tf_op jit(solution)/shard_map/ppermute | solution.py:35
  53.6 6.0 %collective-permute-start.22 = (bf16[224,256]{1,0:T(8,128)(2,1)S(1)}, bf16[224,256]{1,0:T(8,128)(2,1)S(1)}, u32[]{:S(2)}, u32[]{:S(2)}) collective-permute-start(bf16[224,256]{1,0:T(8,128)(2,1)S(1)} %get-tuple-element.59), channel_id=1, source_target_pairs={{0,1},{1,0},{2,3},{3,2},{4,5},{5,4},{6,7},{7,6},{8,9},{9,8},{10,11... | collective-permute-start | bytes 344072 | tf_op jit(solution)/shard_map/ppermute | solution.py:394
  55.1 6.0 %collective-permute-start.23 = (bf16[224,256]{1,0:T(8,128)(2,1)S(1)}, bf16[224,256]{1,0:T(8,128)(2,1)S(1)}, u32[]{:S(2)}, u32[]{:S(2)}) collective-permute-start(bf16[224,256]{1,0:T(8,128)(2,1)S(1)} %get-tuple-element.60), channel_id=1, source_target_pairs={{0,3},{1,2},{2,1},{3,0},{4,7},{5,6},{6,5},{7,4},{8,11},{9,10},{10,... | collective-permute-start | bytes 344072 | tf_op jit(solution)/shard_map/ppermute | solution.py:395
  55.4 2.9 %collective-permute-start.21 = (bf16[224,256]{1,0:T(8,128)(2,1)S(1)}, bf16[224,256]{1,0:T(8,128)(2,1)S(1)}, u32[]{:S(2)}, u32[]{:S(2)}) collective-permute-start(bf16[224,256]{1,0:T(8,128)(2,1)S(1)} %get-tuple-element.61), channel_id=1, source_target_pairs={{0,2},{2,0},{4,6},{6,4},{8,10},{10,8},{12,14},{14,12},{16,18},{18,... | collective-permute-start | bytes 344072 | tf_op jit(solution)/shard_map/ppermute | solution.py:35
  55.8 2.5 %collective-permute-start.20 = (bf16[224,256]{1,0:T(8,128)(2,1)S(1)}, bf16[224,256]{1,0:T(8,128)(2,1)S(1)}, u32[]{:S(2)}, u32[]{:S(2)}) collective-permute-start(bf16[224,256]{1,0:T(8,128)(2,1)S(1)} %get-tuple-element.62), channel_id=1, source_target_pairs={{0,2},{2,0},{4,6},{6,4},{8,10},{10,8},{12,14},{14,12},{16,18},{18,... | collective-permute-start | bytes 344072 | tf_op jit(solution)/shard_map/ppermute | solution.py:35
  56.8 1.4 %collective-permute-start.19 = (bf16[224,256]{1,0:T(8,128)(2,1)S(1)}, bf16[224,256]{1,0:T(8,128)(2,1)S(1)}, u32[]{:S(2)}, u32[]{:S(2)}) collective-permute-start(bf16[224,256]{1,0:T(8,128)(2,1)S(1)} %get-tuple-element.63), channel_id=1, source_target_pairs={{0,2},{2,0},{4,6},{6,4},{8,10},{10,8},{12,14},{14,12},{16,18},{18,... | collective-permute-start | bytes 344072 | tf_op jit(solution)/shard_map/ppermute | solution.py:35
